TPU v7x, 32 devices: a whole 2x2x4 slice. The times are simulated.
32 devices in a mesh: grp: 4 (over x, core), ep: 8 (over z, y).
Axes of the slice: x: 2, y: 2, z: 4, core: 2. Of those that a mesh axis runs over, the one named last changes fastest.
Arguments:
- tokens: bfloat16 [2, 4, 512, 2048], P(None, 'grp', 'ep'), may hold values from -6 to 6
- routes: int32 [2, 4, 512, 8], P(None, 'grp', 'ep'), may hold values from 0 to 15, all different within a row; in each aligned block of 64 rows (0 to 63, 64 to 127, ..., all dimensions but the last counted through in order) at most 36 rows name the same one
- attn_gain: bfloat16 [2048], P(('grp', 'ep')), may hold values from 0.5 to 1.5
- w_query: bfloat16 [2048, 2048], P(('grp', 'ep')), may hold values from -0.125 to 0.125
- w_key: bfloat16 [2048, 2048], P(('grp', 'ep')), may hold values from -0.125 to 0.125
- w_value: bfloat16 [2048, 2048], P(('grp', 'ep')), may hold values from -0.125 to 0.125
- query_gain: bfloat16 [2048], P(('grp', 'ep')), may hold values from 0.5 to 1.5
- key_gain: bfloat16 [2048], P(('grp', 'ep')), may hold values from 0.5 to 1.5
- w_out: bfloat16 [2048, 2048], P(('grp', 'ep')), may hold values from -0.75 to 0.75
- moe_gain: bfloat16 [2048], P(('grp', 'ep')), may hold values from 0.5 to 1.5
- w_router: bfloat16 [2048, 16], P(('grp', 'ep')), may hold values from -0.0625 to 0.0625
- w_gate: bfloat16 [16, 2048, 1024], P('ep'), may hold values from -0.125 to 0.125
- w_up: bfloat16 [16, 2048, 1024], P('ep'), may hold values from -0.125 to 0.125
- w_down: bfloat16 [16, 1024, 2048], P('ep'), may hold values from -1.5 to 1.5
- cotangent: bfloat16 [2, 4, 512, 2048], P(None, 'grp', 'ep'), may hold values from -6 to 6
Outputs:
- block_out: bfloat16 [2, 4, 512, 2048], P(None, 'grp', 'ep')
- d_tokens: float32 [2, 4, 512, 2048], P(None, 'grp', 'ep')
- d_attn_gain: float32 [2048], P(('grp', 'ep'))
- d_query: float32 [2048, 2048], P(('grp', 'ep'))
- d_key: float32 [2048, 2048], P(('grp', 'ep'))
- d_value: float32 [2048, 2048], P(('grp', 'ep'))
- d_query_gain: float32 [2048], P(('grp', 'ep'))
- d_key_gain: float32 [2048], P(('grp', 'ep'))
- d_out: float32 [2048, 2048], P(('grp', 'ep'))
- d_moe_gain: float32 [2048], P(('grp', 'ep'))
- d_router: float32 [2048, 16], P(('grp', 'ep'))
- d_gate: float32 [16, 2048, 1024], P('ep')
- d_up: float32 [16, 2048, 1024], P('ep')
- d_down: float32 [16, 1024, 2048], P('ep')
Inputs may be any that keep to these rules, and one draw needn't show every extreme that they name: `routes`: each token names 8 different experts. In each micro-batch the 64 tokens of one device name no expert more than 36 times.
All inputs are finite; a program needn't handle non-finite values.
Results may differ from a plain program's by a relative error of at most 0.02.
Values may be sent and summed in bfloat16 or wider, within the bound.
No kernel may reach another device: no remote copies, remote signals or barrier semaphores. Data moves between devices by JAX's collectives and lax.ppermute only.
A program may use at most 384 MiB of HBM per device.

v0:
```python
import math

import jax
import jax.numpy as jnp
from jax import lax
from jax.sharding import PartitionSpec as P

HEADS = 16
CAP = 36


NORM_EPSILON = 1e-05
ROPE_BASE = 10000.0


def rms_scale(values, gain_vec):
    return (
        values
        * lax.rsqrt(jnp.mean(values * values, axis=-1, keepdims=True) + NORM_EPSILON)
        * gain_vec
    )


def rotary(values, positions):
    half_dim = values.shape[-1] // 2
    frequency = jnp.exp(
        -math.log(ROPE_BASE) * jnp.arange(half_dim, dtype=jnp.float32) * 2.0 / values.shape[-1]
    )
    angles = positions.astype(jnp.float32)[:, None] * frequency[None, :]
    cosine = jnp.cos(angles)[:, None, :]
    sine_part = jnp.sin(angles)[:, None, :]
    first_half = values[..., :half_dim]
    second = values[..., half_dim:]
    return jnp.concatenate(
        [first_half * cosine - second * sine_part, second * cosine + first_half * sine_part],
        axis=-1,
    )


def prepare(raw_rows, gain_vec, positions):
    normed = rms_scale(raw_rows, gain_vec)
    shaped = normed.reshape(raw_rows.shape[0], HEADS, raw_rows.shape[1] // HEADS)
    return rotary(shaped, positions).reshape(raw_rows.shape)


def contract_rows(left, right):
    return lax.dot_general(
        left, right, (((0,), (0,)), ((), ())), preferred_element_type=jnp.float32
    )


def contract_cols(left, right):
    return lax.dot_general(
        left, right, (((1,), (1,)), ((), ())), preferred_element_type=jnp.float32
    )


def add_pairs(first_set, second_set):
    return tuple((left + right for left, right in zip(first_set, second_set)))


def per_device(
    tokens,
    routes,
    attn_gain,
    w_query,
    w_key,
    w_value,
    query_gain,
    key_gain,
    w_out,
    moe_gain,
    w_router,
    w_gate,
    w_up,
    w_down,
    cotangent,
):
    micro_count, seq_parts, row_count, model_width = tokens.shape
    top_count = routes.shape[3]
    tokens = tokens.reshape(micro_count, seq_parts * row_count, model_width)
    routes = routes.reshape(micro_count, seq_parts * row_count, top_count)
    cotangent = cotangent.reshape(micro_count, seq_parts * row_count, model_width)
    row_count = seq_parts * row_count
    expert_count = w_router.shape[1]
    group_size = lax.axis_size("ep")
    seq_len = row_count * group_size
    head_dim = model_width // HEADS
    score_scale = 1.0 / math.sqrt(head_dim)
    pair_count = row_count * top_count
    positions = lax.axis_index("ep") * row_count + jnp.arange(row_count, dtype=jnp.int32)
    allowed = positions[:, None] >= jnp.arange(seq_len, dtype=jnp.int32)[None, :]
    slot_ids = jnp.arange(expert_count * CAP, dtype=jnp.int32)
    expert_ids = jnp.arange(expert_count, dtype=jnp.int32)

    def attention_probs(query_heads, key_heads):
        scores = (
            jnp.einsum("qhd,khd->hqk", query_heads, key_heads, preferred_element_type=jnp.float32)
            * score_scale
        )
        return jnp.where(allowed[None, :, :], scores, -1e30)

    kept_state = []
    outputs = []
    for micro_index in range(micro_count):
        weights = (
            lax.all_gather(attn_gain, ("grp", "ep"), axis=0, tiled=True),
            lax.all_gather(query_gain, ("grp", "ep"), axis=0, tiled=True),
            lax.all_gather(key_gain, ("grp", "ep"), axis=0, tiled=True),
            lax.all_gather(moe_gain, ("grp", "ep"), axis=0, tiled=True),
            lax.all_gather(w_query, ("grp", "ep"), axis=0, tiled=True),
            lax.all_gather(w_key, ("grp", "ep"), axis=0, tiled=True),
            lax.all_gather(w_value, ("grp", "ep"), axis=0, tiled=True),
            lax.all_gather(w_out, ("grp", "ep"), axis=0, tiled=True),
            lax.all_gather(w_router, ("grp", "ep"), axis=0, tiled=True),
        )
        (
            gain_attn,
            gain_query,
            gain_key,
            gain_moe,
            full_query,
            full_key,
            full_value,
            full_out,
            full_router,
        ) = weights
        resid_in = tokens[micro_index].astype(jnp.float32)
        normed = rms_scale(resid_in, gain_attn.astype(jnp.float32)).astype(jnp.bfloat16)
        query_raw = jnp.dot(normed, full_query, preferred_element_type=jnp.float32)
        key_raw = jnp.dot(normed, full_key, preferred_element_type=jnp.float32)
        value_low = jnp.dot(normed, full_value, preferred_element_type=jnp.float32).astype(
            jnp.bfloat16
        )
        query_low = prepare(query_raw, gain_query.astype(jnp.float32), positions).astype(
            jnp.bfloat16
        )
        key_low = prepare(key_raw, gain_key.astype(jnp.float32), positions).astype(jnp.bfloat16)
        all_keys, all_values = (
            lax.all_gather(key_low, "ep", axis=0, tiled=True),
            lax.all_gather(value_low, "ep", axis=0, tiled=True),
        )
        query_heads = query_low.reshape(row_count, HEADS, head_dim)
        key_heads = all_keys.reshape(seq_len, HEADS, head_dim)
        value_heads = all_values.reshape(seq_len, HEADS, head_dim)
        scores = attention_probs(query_heads, key_heads)
        top_score = jnp.max(scores, axis=-1, keepdims=True)
        exp_scores = jnp.exp(scores - top_score)
        totals = jnp.sum(exp_scores, axis=-1, keepdims=True)
        log_total = top_score + jnp.log(totals)
        attn_probs = exp_scores / totals
        attended = jnp.einsum(
            "hqk,khd->qhd",
            attn_probs.astype(jnp.bfloat16),
            value_heads,
            preferred_element_type=jnp.float32,
        )
        attended = attended.reshape(row_count, model_width).astype(jnp.bfloat16)
        resid_mid = resid_in + jnp.dot(attended, full_out, preferred_element_type=jnp.float32)
        moe_in = rms_scale(resid_mid, gain_moe.astype(jnp.float32)).astype(jnp.bfloat16)
        router_probs = jax.nn.softmax(
            jnp.dot(moe_in, full_router, preferred_element_type=jnp.float32), axis=-1
        )
        route_ids = routes[micro_index]
        gate_weights = jnp.take_along_axis(router_probs, route_ids, axis=1)
        flat_route = route_ids.reshape(-1)
        member = (flat_route[:, None] == expert_ids[None, :]).astype(jnp.int32)
        slot_rank = jnp.sum((jnp.cumsum(member, axis=0) - member) * member, axis=1)
        pair_slot = (flat_route * CAP + slot_rank).reshape(row_count, top_count)
        dispatch_table = jnp.any(slot_ids[:, None, None] == pair_slot[None, :, :], axis=-1).astype(
            jnp.bfloat16
        )
        outgoing = jnp.dot(dispatch_table, moe_in, preferred_element_type=jnp.float32).astype(
            jnp.bfloat16
        )
        outgoing = outgoing.reshape(expert_count, CAP, model_width)
        incoming = lax.all_to_all(outgoing, "ep", split_axis=0, concat_axis=1, tiled=True)
        gate_pre = jnp.einsum("erd,edf->erf", incoming, w_gate, preferred_element_type=jnp.float32)
        up_pre = jnp.einsum("erd,edf->erf", incoming, w_up, preferred_element_type=jnp.float32)
        activation = (jax.nn.silu(gate_pre) * up_pre).astype(jnp.bfloat16)
        expert_rows = jnp.einsum(
            "erf,efd->erd", activation, w_down, preferred_element_type=jnp.float32
        ).astype(jnp.bfloat16)
        returned = lax.all_to_all(expert_rows, "ep", split_axis=1, concat_axis=0, tiled=True)
        picked = returned.reshape(expert_count * CAP, model_width)[pair_slot]
        mixture = jnp.sum(gate_weights[:, :, None] * picked.astype(jnp.float32), axis=1)
        outputs.append((resid_mid + mixture).astype(jnp.bfloat16))
        kept_state.append(
            (
                resid_in,
                normed,
                query_raw,
                key_raw,
                query_low,
                all_keys,
                all_values,
                log_total,
                attended,
                resid_mid,
                moe_in,
                router_probs,
                gate_weights,
                route_ids,
                pair_slot,
                incoming,
                gate_pre,
                up_pre,
                activation,
                picked,
            )
        )
    square_zero = jnp.zeros((model_width, model_width), jnp.float32)
    vector_zero = jnp.zeros((model_width,), jnp.float32)
    dense_acc = (
        vector_zero,
        square_zero,
        square_zero,
        square_zero,
        vector_zero,
        vector_zero,
        square_zero,
        vector_zero,
        jnp.zeros((model_width, expert_count), jnp.float32),
    )
    expert_acc = (
        jnp.zeros(w_gate.shape, jnp.float32),
        jnp.zeros(w_up.shape, jnp.float32),
        jnp.zeros(w_down.shape, jnp.float32),
    )
    grad_inputs = []
    for micro_index in reversed(range(micro_count)):
        weights_back = (
            lax.all_gather(attn_gain, ("grp", "ep"), axis=0, tiled=True),
            lax.all_gather(query_gain, ("grp", "ep"), axis=0, tiled=True),
            lax.all_gather(key_gain, ("grp", "ep"), axis=0, tiled=True),
            lax.all_gather(moe_gain, ("grp", "ep"), axis=0, tiled=True),
            lax.all_gather(w_query, ("grp", "ep"), axis=0, tiled=True),
            lax.all_gather(w_key, ("grp", "ep"), axis=0, tiled=True),
            lax.all_gather(w_value, ("grp", "ep"), axis=0, tiled=True),
            lax.all_gather(w_out, ("grp", "ep"), axis=0, tiled=True),
            lax.all_gather(w_router, ("grp", "ep"), axis=0, tiled=True),
        )
        (
            gain_attn,
            gain_query,
            gain_key,
            gain_moe,
            full_query,
            full_key,
            full_value,
            full_out,
            full_router,
        ) = weights_back
        (
            resid_in,
            normed,
            query_raw,
            key_raw,
            query_low,
            all_keys,
            all_values,
            log_total,
            attended,
            resid_mid,
            moe_in,
            router_probs,
            gate_weights,
            route_ids,
            pair_slot,
            incoming,
            gate_pre,
            up_pre,
            activation,
            picked,
        ) = kept_state[micro_index]
        grad_out = cotangent[micro_index].astype(jnp.float32)
        grad_gates = jnp.sum(grad_out[:, None, :] * picked.astype(jnp.float32), axis=-1)
        pair_grad = (gate_weights[:, :, None] * grad_out[:, None, :]).astype(jnp.bfloat16)
        padded_grad = jnp.concatenate(
            [pair_grad.reshape(pair_count, model_width), jnp.zeros((1, model_width), jnp.bfloat16)],
            axis=0,
        )
        slot_owner = (
            jnp.full((expert_count * CAP,), pair_count, jnp.int32)
            .at[pair_slot.reshape(-1)]
            .set(jnp.arange(pair_count, dtype=jnp.int32))
        )
        slot_grads = padded_grad[slot_owner].reshape(expert_count, CAP, model_width)
        grad_rows = lax.all_to_all(slot_grads, "ep", split_axis=0, concat_axis=1, tiled=True)
        down_term = jnp.einsum(
            "erf,erd->efd", activation, grad_rows, preferred_element_type=jnp.float32
        )
        grad_act = jnp.einsum("erd,efd->erf", grad_rows, w_down, preferred_element_type=jnp.float32)
        sigmoid_gate = jax.nn.sigmoid(gate_pre)
        grad_gate_pre = (
            grad_act * up_pre * sigmoid_gate * (1.0 + gate_pre * (1.0 - sigmoid_gate))
        ).astype(jnp.bfloat16)
        grad_up_pre = (grad_act * gate_pre * sigmoid_gate).astype(jnp.bfloat16)
        gate_term = jnp.einsum(
            "erd,erf->edf", incoming, grad_gate_pre, preferred_element_type=jnp.float32
        )
        up_term = jnp.einsum(
            "erd,erf->edf", incoming, grad_up_pre, preferred_element_type=jnp.float32
        )
        row_grad = jnp.einsum(
            "erf,edf->erd", grad_gate_pre, w_gate, preferred_element_type=jnp.float32
        )
        row_grad = (
            row_grad
            + jnp.einsum("erf,edf->erd", grad_up_pre, w_up, preferred_element_type=jnp.float32)
        ).astype(jnp.bfloat16)
        grad_back = lax.all_to_all(row_grad, "ep", split_axis=1, concat_axis=0, tiled=True)
        grad_pairs = grad_back.reshape(expert_count * CAP, model_width)[pair_slot]
        chosen = (route_ids[:, :, None] == expert_ids[None, None, :]).astype(jnp.float32)
        grad_probs = jnp.sum(grad_gates[:, :, None] * chosen, axis=1)
        grad_logits = router_probs * (
            grad_probs - jnp.sum(router_probs * grad_probs, axis=-1, keepdims=True)
        )
        grad_logits = grad_logits.astype(jnp.bfloat16)
        router_term = contract_rows(moe_in, grad_logits)
        grad_moe_in = jnp.sum(grad_pairs.astype(jnp.float32), axis=1) + contract_cols(
            grad_logits, full_router
        )
        unused_moe, pull_moe = jax.vjp(rms_scale, resid_mid, gain_moe.astype(jnp.float32))
        grad_mid_part, grad_gain_moe = pull_moe(grad_moe_in)
        grad_mid = grad_out + grad_mid_part
        grad_attn = grad_mid.astype(jnp.bfloat16)
        out_term = contract_rows(attended, grad_attn)
        grad_attended = (
            contract_cols(grad_attn, full_out)
            .astype(jnp.bfloat16)
            .reshape(row_count, HEADS, head_dim)
        )
        query_heads = query_low.reshape(row_count, HEADS, head_dim)
        key_heads = all_keys.reshape(seq_len, HEADS, head_dim)
        value_heads = all_values.reshape(seq_len, HEADS, head_dim)
        attn_probs = jnp.exp(attention_probs(query_heads, key_heads) - log_total)
        grad_value_part = jnp.einsum(
            "hqk,qhd->khd",
            attn_probs.astype(jnp.bfloat16),
            grad_attended,
            preferred_element_type=jnp.float32,
        )
        grad_pa = jnp.einsum(
            "qhd,khd->hqk", grad_attended, value_heads, preferred_element_type=jnp.float32
        )
        row_delta = jnp.sum(attn_probs * grad_pa, axis=-1, keepdims=True)
        grad_scores = (attn_probs * (grad_pa - row_delta)).astype(jnp.bfloat16)
        grad_query = (
            jnp.einsum(
                "hqk,khd->qhd", grad_scores, key_heads, preferred_element_type=jnp.float32
            ).reshape(row_count, model_width)
            * score_scale
        )
        grad_key_part = (
            jnp.einsum(
                "hqk,qhd->khd", grad_scores, query_heads, preferred_element_type=jnp.float32
            ).reshape(seq_len, model_width)
            * score_scale
        )
        grad_key, grad_value = (
            lax.psum_scatter(
                grad_key_part.astype(jnp.bfloat16), "ep", scatter_dimension=0, tiled=True
            ).astype(jnp.float32),
            lax.psum_scatter(
                grad_value_part.reshape(seq_len, model_width).astype(jnp.bfloat16),
                "ep",
                scatter_dimension=0,
                tiled=True,
            ).astype(jnp.float32),
        )
        unused_query, pull_query = jax.vjp(
            lambda raw_part, gain_part: prepare(raw_part, gain_part, positions),
            query_raw,
            gain_query.astype(jnp.float32),
        )
        grad_query_raw, grad_gain_query = pull_query(grad_query)
        unused_key, pull_key = jax.vjp(
            lambda raw_part, gain_part: prepare(raw_part, gain_part, positions),
            key_raw,
            gain_key.astype(jnp.float32),
        )
        grad_key_raw, grad_gain_key = pull_key(grad_key)
        low_query = grad_query_raw.astype(jnp.bfloat16)
        low_key = grad_key_raw.astype(jnp.bfloat16)
        low_value = grad_value.astype(jnp.bfloat16)
        query_term = contract_rows(normed, low_query)
        key_term = contract_rows(normed, low_key)
        value_term = contract_rows(normed, low_value)
        grad_normed = (
            contract_cols(low_query, full_query)
            + contract_cols(low_key, full_key)
            + contract_cols(low_value, full_value)
        )
        unused_attn, pull_attn = jax.vjp(rms_scale, resid_in, gain_attn.astype(jnp.float32))
        grad_in_part, grad_gain_attn = pull_attn(grad_normed)
        grad_inputs.append(grad_mid + grad_in_part)
        dense_acc = add_pairs(
            dense_acc,
            (
                grad_gain_attn,
                query_term,
                key_term,
                value_term,
                grad_gain_query,
                grad_gain_key,
                out_term,
                grad_gain_moe,
                router_term,
            ),
        )
        expert_acc = add_pairs(expert_acc, (gate_term, up_term, down_term))
    reduced = (
        lax.psum_scatter(dense_acc[0], ("grp", "ep"), scatter_dimension=0, tiled=True),
        lax.psum_scatter(dense_acc[1], ("grp", "ep"), scatter_dimension=0, tiled=True),
        lax.psum_scatter(dense_acc[2], ("grp", "ep"), scatter_dimension=0, tiled=True),
        lax.psum_scatter(dense_acc[3], ("grp", "ep"), scatter_dimension=0, tiled=True),
        lax.psum_scatter(dense_acc[4], ("grp", "ep"), scatter_dimension=0, tiled=True),
        lax.psum_scatter(dense_acc[5], ("grp", "ep"), scatter_dimension=0, tiled=True),
        lax.psum_scatter(dense_acc[6], ("grp", "ep"), scatter_dimension=0, tiled=True),
        lax.psum_scatter(dense_acc[7], ("grp", "ep"), scatter_dimension=0, tiled=True),
        lax.psum_scatter(dense_acc[8], ("grp", "ep"), scatter_dimension=0, tiled=True),
    )
    summed_gate, summed_up, summed_down = (
        lax.psum(expert_acc[0].astype(jnp.bfloat16), "grp").astype(jnp.float32),
        lax.psum(expert_acc[1].astype(jnp.bfloat16), "grp").astype(jnp.float32),
        lax.psum(expert_acc[2].astype(jnp.bfloat16), "grp").astype(jnp.float32),
    )
    block_out = jnp.stack(outputs).reshape(
        micro_count, seq_parts, row_count // seq_parts, model_width
    )
    d_tokens = jnp.stack(grad_inputs[::-1]).reshape(
        micro_count, seq_parts, row_count // seq_parts, model_width
    )
    return (
        block_out,
        d_tokens,
        reduced[0],
        reduced[1],
        reduced[2],
        reduced[3],
        reduced[4],
        reduced[5],
        reduced[6],
        reduced[7],
        reduced[8],
        summed_gate,
        summed_up,
        summed_down,
    )


def solution(mesh):
    return jax.shard_map(
        per_device,
        mesh=mesh,
        in_specs=(
            P(None, "grp", "ep", None),
            P(None, "grp", "ep", None),
            P(("grp", "ep")),
            P(("grp", "ep"), None),
            P(("grp", "ep"), None),
            P(("grp", "ep"), None),
            P(("grp", "ep")),
            P(("grp", "ep")),
            P(("grp", "ep"), None),
            P(("grp", "ep")),
            P(("grp", "ep"), None),
            P("ep", None, None),
            P("ep", None, None),
            P("ep", None, None),
            P(None, "grp", "ep", None),
        ),
        out_specs=(
            P(None, "grp", "ep", None),
            P(None, "grp", "ep", None),
            P(("grp", "ep")),
            P(("grp", "ep"), None),
            P(("grp", "ep"), None),
            P(("grp", "ep"), None),
            P(("grp", "ep")),
            P(("grp", "ep")),
            P(("grp", "ep"), None),
            P(("grp", "ep")),
            P(("grp", "ep"), None),
            P("ep", None, None),
            P("ep", None, None),
            P("ep", None, None),
        ),
        check_vma=False,
    )
```

profile of v0, /device:TPU:0, one launch (start us, length us, event | category | flops | bytes accessed | tf_op | source)
XLA Modules:
  0.0 3374.1 jit_solution(15801567178942500562)
XLA Ops:
  12.9 42.7 %all-reduce.19 = (bf16[2048]{0:T(1024)(128)(2,1)S(1)}, bf16[2048]{0:T(1024)(128)(2,1)S(1)}, bf16[2048]{0:T(1024)(128)(2,1)S(1)}, bf16[2048]{0:T(1024)(128)(2,1)S(1)}) all-reduce(bf16[2048]{0:T(1024)(128)(2,1)S(1)} %dynamic-update-slice, bf16[2048]{0:T(1024)(128)(2,1)S(1)} %dynamic-update-slice.2, ...), channel_id=1, replica_groups=mesh['grp'=4,'ep'=8] {'grp','ep'}, use_global_device_ids=true, to_apply=%add.10 | all-reduce | flops 8192 | bytes 32768
  57.6 34.0 %all-gather.14.cloned.1.call-done = bf16[2048,2048]{1,0:T(8,128)(2,1)} async-done(((bf16[64,2048]{1,0:T(8,128)(2,1)}), bf16[2048,2048]{1,0:T(8,128)(2,1)}) %all-gather.14.cloned.1.call-update) | async-done | bytes 8388624 | tf_op jit(solution)/shard_map/all_gather | solution.py:111
  100.2 70.4 %all-gather.16.cloned.1.call-done = bf16[2048,2048]{1,0:T(8,128)(2,1)} async-done(((bf16[64,2048]{1,0:T(8,128)(2,1)}), bf16[2048,2048]{1,0:T(8,128)(2,1)}) %all-gather.16.cloned.1.call-update) | async-done | bytes 8388624 | tf_op jit(solution)/shard_map/all_gather | solution.py:112
  183.0 66.7 %all-gather.10.cloned.1.call-done = bf16[2048,2048]{1,0:T(8,128)(2,1)} async-done(((bf16[64,2048]{1,0:T(8,128)(2,1)}), bf16[2048,2048]{1,0:T(8,128)(2,1)}) %all-gather.10.cloned.1.call-update) | async-done | bytes 8388624 | tf_op jit(solution)/shard_map/all_gather | solution.py:113
  259.3 67.5 %all-gather = bf16[32,64,16]{1,2,0:T(8,128)(2,1)S(1)} all-gather(bf16[1,64,16]{1,2,0:T(8,128)(2,1)S(1)} %bitcast.502), channel_id=1, replica_groups=mesh['grp'=4,'ep'=8] {'grp','ep'}, dimensions={0}, use_global_device_ids=true | all-gather | bytes 67584 | tf_op jit(solution)/shard_map/all_gather | solution.py:115
  338.3 13.1 all-gather.12.cloned.1.call-done
  353.8 76.4 %all-gather.20.cloned.1.call-done = bf16[2048,2048]{1,0:T(8,128)(2,1)} async-done(((bf16[64,2048]{1,0:T(8,128)(2,1)}), bf16[2048,2048]{1,0:T(8,128)(2,1)}) %all-gather.20.cloned.1.call-update) | async-done | bytes 8388624 | tf_op jit(solution)/shard_map/all_gather | solution.py:114
  461.7 53.3 %all-to-all-done.4 = bf16[16,36,2048]{2,1,0:T(8,128)(2,1)} async-done(((bf16[16,36,2048]{2,1,0:T(8,128)(2,1)}), bf16[16,36,2048]{2,1,0:T(8,128)(2,1)}, u32[]{:S(2)}, u32[]{:S(2)}) %all-to-all-start.4) | async-done | bytes 2359328 | tf_op jit(solution)/shard_map/all_to_all | solution.py:289
  526.0 78.0 %all-to-all-done = bf16[16,36,2048]{2,1,0:T(8,128)(2,1)} async-done(((bf16[16,36,2048]{2,1,0:T(8,128)(2,1)}), bf16[16,36,2048]{2,1,0:T(8,128)(2,1)}, u32[]{:S(2)}, u32[]{:S(2)}) %all-to-all-start) | async-done | bytes 2359328 | tf_op jit(solution)/shard_map/all_to_all | solution.py:177
  668.5 52.2 %all-to-all-done.1 = bf16[2,288,2048]{2,0,1:T(2,128)(2,1)} async-done(((bf16[2,288,2048]{2,0,1:T(2,128)(2,1)}), bf16[2,288,2048]{2,0,1:T(2,128)(2,1)}, u32[]{:S(2)}, u32[]{:S(2)}) %all-to-all-start.1) | async-done | bytes 2359328 | tf_op jit(solution)/shard_map/all_to_all | solution.py:184
  759.9 17.5 all-to-all-done.5
  817.2 41.8 %all-to-all-done.2 = bf16[16,36,2048]{2,1,0:T(8,128)(2,1)} async-done(((bf16[16,36,2048]{2,1,0:T(8,128)(2,1)}), bf16[16,36,2048]{2,1,0:T(8,128)(2,1)}, u32[]{:S(2)}, u32[]{:S(2)}) %all-to-all-start.2) | async-done | bytes 2359328 | tf_op jit(solution)/shard_map/all_to_all | solution.py:177
  883.5 38.7 %all-to-all-done.6 = bf16[16,36,2048]{2,1,0:T(8,128)(2,1)S(1)} async-done(((bf16[16,36,2048]{2,1,0:T(8,128)(2,1)}), bf16[16,36,2048]{2,1,0:T(8,128)(2,1)S(1)}, u32[]{:S(2)}, u32[]{:S(2)}) %all-to-all-start.6) | async-done | bytes 2359328 | tf_op jit(solution)/shard_map/all_to_all | solution.py:289
  967.4 35.2 %all-to-all-done.3 = bf16[2,288,2048]{2,0,1:T(2,128)(2,1)S(1)} async-done(((bf16[2,288,2048]{2,0,1:T(2,128)(2,1)}), bf16[2,288,2048]{2,0,1:T(2,128)(2,1)S(1)}, u32[]{:S(2)}, u32[]{:S(2)}) %all-to-all-start.3) | async-done | bytes 2359328 | tf_op jit(solution)/shard_map/all_to_all | solution.py:184
  1023.5 36.9 %all-to-all-done.7 = bf16[2,288,2048]{2,0,1:T(2,128)(2,1)} async-done(((bf16[2,288,2048]{2,0,1:T(2,128)(2,1)}), bf16[2,288,2048]{2,0,1:T(2,128)(2,1)}, u32[]{:S(2)}, u32[]{:S(2)}) %all-to-all-start.7) | async-done | bytes 2359328 | tf_op jit(solution)/shard_map/all_to_all | solution.py:312
  1147.4 12.1 add_convert_fusion
  1159.6 12.0 add_convert_fusion.1
  1175.1 11.7 add_convert_fusion.2
  1209.2 14.1 reduce-scatter.28.cloned.1.call-done
  1223.3 14.1 convolution_add_fusion.1
  1243.0 50.6 %reduce-scatter.16.cloned.1.call-done = bf16[64,2048]{1,0:T(8,128)(2,1)} async-done(((bf16[512,2048]{1,0:T(8,128)(2,1)}), bf16[64,2048]{1,0:T(8,128)(2,1)}) %reduce-scatter.16.cloned.1.call-update) | async-done | bytes 262160 | tf_op jit(solution)/shard_map/reduce_scatter | solution.py:362
  1294.7 69.0 %reduce-scatter.18.cloned.1.call-done = bf16[64,2048]{1,0:T(8,128)(2,1)} async-done(((bf16[512,2048]{1,0:T(8,128)(2,1)}), bf16[64,2048]{1,0:T(8,128)(2,1)}) %reduce-scatter.18.cloned.1.call-update) | async-done | bytes 262160 | tf_op jit(solution)/shard_map/reduce_scatter | solution.py:362
  1396.3 103.8 %reduce-scatter.32.cloned.1.call-done = f32[64,16]{1,0:T(8,128)} async-done(((f32[2048,16]{1,0:T(8,128)}), f32[64,16]{1,0:T(8,128)}) %reduce-scatter.32.cloned.1.call-update) | async-done | bytes 4112
  1525.1 38.9 %all-reduce.18 = (f32[2048]{0:T(1024)S(1)}, f32[2048]{0:T(1024)S(1)}, f32[2048]{0:T(1024)S(1)}, f32[2048]{0:T(1024)S(1)}) all-reduce(f32[2048]{0:T(1024)S(1)} %add.434, f32[2048]{0:T(1024)S(1)} %add.438, f32[2048]{0:T(1024)S(1)} %add.439, f32[2048]{0:T(1024)S(1)} %add.441), channel_id=6, replica_groups=mesh['grp'=4,'ep'=8] {'grp','ep'}, use_global_device_ids=true, to_apply=%region_52.54.clone | all-reduce | flops 8192 | bytes 65536
  1567.7 358.0 %all-reduce.23.cloned.1.call-done = (bf16[2,2048,1024]{2,1,0:T(8,128)(2,1)}, bf16[2,2048,1024]{2,1,0:T(8,128)(2,1)}, bf16[2,1024,2048]{2,1,0:T(8,128)(2,1)}) async-done(((bf16[2,2048,1024]{2,1,0:T(8,128)(2,1)}, bf16[2,2048,1024]{2,1,0:T(8,128)(2,1)}, bf16[2,1024,2048]{2,1,0:T(8,128)(2,1)}), (bf16[2,2048,1024]{2,1,0:T(8,128)(2,1)}, bf16[2,2048,1024]{2,1,0:T(8,128)(2,1)}, ...) | async-done | bytes 25165840 | tf_op jit(solution)/shard_map/psum | solution.py:425
  1925.7 11.7 convert_element_type.388
  1937.4 11.7 convert_element_type.390
  1949.1 11.7 convert_element_type.392
  1960.9 325.9 %reduce-scatter.26.cloned.1.call-done = f32[64,2048]{1,0:T(8,128)} async-done(((f32[2048,2048]{1,0:T(8,128)}), f32[64,2048]{1,0:T(8,128)}) %reduce-scatter.26.cloned.1.call-update) | async-done | bytes 524304 | tf_op jit(solution)/shard_map/reduce_scatter | solution.py:420
  2286.8 360.1 %reduce-scatter.24.cloned.1.call-done = f32[64,2048]{1,0:T(8,128)} async-done(((f32[2048,2048]{1,0:T(8,128)}), f32[64,2048]{1,0:T(8,128)}) %reduce-scatter.24.cloned.1.call-update) | async-done | bytes 524304 | tf_op jit(solution)/shard_map/reduce_scatter | solution.py:417
  2646.9 360.1 %reduce-scatter.22.cloned.1.call-done = f32[64,2048]{1,0:T(8,128)} async-done(((f32[2048,2048]{1,0:T(8,128)}), f32[64,2048]{1,0:T(8,128)}) %reduce-scatter.22.cloned.1.call-update) | async-done | bytes 524304 | tf_op jit(solution)/shard_map/reduce_scatter | solution.py:416
  3006.9 360.1 %reduce-scatter.20.cloned.1.call-done = f32[64,2048]{1,0:T(8,128)} async-done(((f32[2048,2048]{1,0:T(8,128)}), f32[64,2048]{1,0:T(8,128)}) %reduce-scatter.20.cloned.1.call-update) | async-done | bytes 524304 | tf_op jit(solution)/shard_map/reduce_scatter | solution.py:415
  (650 shorter events, 507.1 us)
Async XLA Ops:
  7.2 84.4 %all-gather.14.cloned.1.call-start = ((), (), s32[]{:S(2)}) async-start(), calls=%async_computation.19 | async-start | bytes 8650752 | tf_op jit(solution)/shard_map/all_gather | solution.py:111
  7.9 162.7 %all-gather.16.cloned.1.call-start = ((), (), s32[]{:S(2)}) async-start(), calls=%async_computation.20 | async-start | bytes 8650752 | tf_op jit(solution)/shard_map/all_gather | solution.py:112
  8.7 241.0 %all-gather.10.cloned.1.call-start = ((), (), s32[]{:S(2)}) async-start(), calls=%async_computation.17 | async-start | bytes 8650752 | tf_op jit(solution)/shard_map/all_gather | solution.py:113
  9.4 321.9 %all-gather.18.cloned.1.call-start = ((), (), s32[]{:S(2)}) async-start(), calls=%async_computation.21 | async-start | bytes 2359296 | tf_op jit(solution)/shard_map/all_gather | solution.py:140
  55.6 588.7 %copy-start.15 = (f32[2048]{0:T(1024)}, f32[2048]{0:T(1024)S(1)}, u32[]{:S(2)}) copy-start(f32[2048]{0:T(1024)S(1)} %convert_element_type.310) | copy-start | bytes 24580
  57.4 192.3 %copy-start.107 = (f32[64]{0:T(128)}, f32[64]{0:T(128)S(1)}, u32[]{:S(2)}) copy-start(f32[64]{0:T(128)S(1)} %fusion.136) | copy-start | bytes 772
  182.0 153.2 %copy-start.58 = (bf16[64,16,64]{2,0,1:T(8,128)(2,1)}, bf16[64,16,64]{2,0,1:T(8,128)(2,1)S(1)}, u32[]{:S(2)}) copy-start(bf16[64,16,64]{2,0,1:T(8,128)(2,1)S(1)} %get-tuple-element.130) | copy-start | bytes 393220
  182.0 153.2 %copy-start.60 = (bf16[64,16,64]{2,0,1:T(8,128)(2,1)}, bf16[64,16,64]{2,0,1:T(8,128)(2,1)S(1)}, u32[]{:S(2)}) copy-start(bf16[64,16,64]{2,0,1:T(8,128)(2,1)S(1)} %get-tuple-element.131) | copy-start | bytes 393220
  182.9 168.5 %all-gather.12.cloned.1.call-start = ((), (), s32[]{:S(2)}) async-start(), calls=%async_computation.18 | async-start | bytes 2359296 | tf_op jit(solution)/shard_map/all_gather | solution.py:141
  255.4 174.8 %all-gather.20.cloned.1.call-start = ((), (), s32[]{:S(2)}) async-start(), calls=%async_computation.22 | async-start | bytes 8650752 | tf_op jit(solution)/shard_map/all_gather | solution.py:114
  327.0 476.7 %copy-start.72 = (bf16[2048,16]{0,1:T(8,128)(2,1)}, bf16[2048,16]{0,1:T(8,128)(2,1)S(1)}, u32[]{:S(2)}) copy-start(bf16[2048,16]{0,1:T(8,128)(2,1)S(1)} %reshape.793) | copy-start | bytes 196612
  435.3 355.6 %copy-start.25 = (f32[64,2048]{1,0:T(8,128)}, f32[64,2048]{1,0:T(8,128)S(1)}, u32[]{:S(2)}) copy-start(f32[64,2048]{1,0:T(8,128)S(1)} %get-tuple-element.208) | copy-start | bytes 1572868
  450.2 64.7 %all-to-all-start.4 = ((bf16[16,36,2048]{2,1,0:T(8,128)(2,1)}), bf16[16,36,2048]{2,1,0:T(8,128)(2,1)}, u32[]{:S(2)}, u32[]{:S(2)}) async-start(bf16[16,36,2048]{2,1,0:T(8,128)(2,1)} %reshape.664), calls=%async_computation.4 | async-start | bytes 5242880 | tf_op jit(solution)/shard_map/all_to_all | solution.py:289
  515.0 89.1 %all-to-all-start = ((bf16[16,36,2048]{2,1,0:T(8,128)(2,1)}), bf16[16,36,2048]{2,1,0:T(8,128)(2,1)}, u32[]{:S(2)}, u32[]{:S(2)}) async-start(bf16[16,36,2048]{2,1,0:T(8,128)(2,1)} %reshape.654), calls=%async_computation | async-start | bytes 5242880 | tf_op jit(solution)/shard_map/all_to_all | solution.py:177
  519.4 209.8 %all-gather.24.cloned.1.call-start = ((), (), s32[]{:S(2)}) async-start(), calls=%async_computation.24 | async-start | bytes 2359296 | tf_op jit(solution)/shard_map/all_gather | solution.py:140
  639.7 81.1 %all-to-all-start.1 = ((bf16[2,288,2048]{2,0,1:T(2,128)(2,1)}), bf16[2,288,2048]{2,0,1:T(2,128)(2,1)}, u32[]{:S(2)}, u32[]{:S(2)}) async-start(bf16[2,288,2048]{2,0,1:T(2,128)(2,1)} %copy.287), calls=%async_computation.1 | async-start | bytes 4718592 | tf_op jit(solution)/shard_map/all_to_all | solution.py:184
  644.2 92.7 %all-gather.22.cloned.1.call-start = ((), (), s32[]{:S(2)}) async-start(), calls=%async_computation.23 | async-start | bytes 2359296 | tf_op jit(solution)/shard_map/all_gather | solution.py:141
  720.7 56.7 %all-to-all-start.5 = ((bf16[2,288,2048]{2,0,1:T(2,128)(2,1)}), bf16[2,288,2048]{2,0,1:T(2,128)(2,1)}, u32[]{:S(2)}, u32[]{:S(2)}) async-start(bf16[2,288,2048]{2,0,1:T(2,128)(2,1)} %copy.308), calls=%async_computation.5 | async-start | bytes 4718592 | tf_op jit(solution)/shard_map/all_to_all | solution.py:312
  795.7 63.3 %all-to-all-start.2 = ((bf16[16,36,2048]{2,1,0:T(8,128)(2,1)}), bf16[16,36,2048]{2,1,0:T(8,128)(2,1)}, u32[]{:S(2)}, u32[]{:S(2)}) async-start(bf16[16,36,2048]{2,1,0:T(8,128)(2,1)} %reshape.661), calls=%async_computation.2 | async-start | bytes 5242880 | tf_op jit(solution)/shard_map/all_to_all | solution.py:177
  858.9 63.3 %all-to-all-start.6 = ((bf16[16,36,2048]{2,1,0:T(8,128)(2,1)}), bf16[16,36,2048]{2,1,0:T(8,128)(2,1)S(1)}, u32[]{:S(2)}, u32[]{:S(2)}) async-start(bf16[16,36,2048]{2,1,0:T(8,128)(2,1)} %reshape.671), calls=%async_computation.7 | async-start | bytes 5242880 | tf_op jit(solution)/shard_map/all_to_all | solution.py:289
  944.9 57.7 %all-to-all-start.3 = ((bf16[2,288,2048]{2,0,1:T(2,128)(2,1)}), bf16[2,288,2048]{2,0,1:T(2,128)(2,1)S(1)}, u32[]{:S(2)}, u32[]{:S(2)}) async-start(bf16[2,288,2048]{2,0,1:T(2,128)(2,1)} %copy.303), calls=%async_computation.3 | async-start | bytes 4718592 | tf_op jit(solution)/shard_map/all_to_all | solution.py:184
  1002.6 57.8 %all-to-all-start.7 = ((bf16[2,288,2048]{2,0,1:T(2,128)(2,1)}), bf16[2,288,2048]{2,0,1:T(2,128)(2,1)}, u32[]{:S(2)}, u32[]{:S(2)}) async-start(bf16[2,288,2048]{2,0,1:T(2,128)(2,1)} %copy.324), calls=%async_computation.8 | async-start | bytes 4718592 | tf_op jit(solution)/shard_map/all_to_all | solution.py:312
  1007.0 191.7 %reduce-scatter.30.cloned.1.call-start = ((), (), s32[]{:S(2)}) async-start(), calls=%async_computation.32 | async-start | bytes 2359296
  1086.6 136.7 %reduce-scatter.28.cloned.1.call-start = ((), (), s32[]{:S(2)}) async-start(), calls=%async_computation.31 | async-start | bytes 2359296
  1100.1 193.5 %reduce-scatter.16.cloned.1.call-start = ((), (), s32[]{:S(2)}) async-start(), calls=%async_computation.25 | async-start | bytes 2359296 | tf_op jit(solution)/shard_map/reduce_scatter | solution.py:362
  1107.6 256.1 %reduce-scatter.18.cloned.1.call-start = ((), (), s32[]{:S(2)}) async-start(), calls=%async_computation.26 | async-start | bytes 2359296 | tf_op jit(solution)/shard_map/reduce_scatter | solution.py:362
  1127.0 373.1 %reduce-scatter.32.cloned.1.call-start = ((), (), s32[]{:S(2)}) async-start(), calls=%async_computation.33 | async-start | bytes 1081344
  1174.9 750.8 %all-reduce.23.cloned.1.call-start = ((), (), s32[]{:S(2)}) async-start(), calls=%async_computation.34 | async-start | bytes 50331648 | tf_op jit(solution)/shard_map/psum | solution.py:425
  1186.9 1099.9 %reduce-scatter.26.cloned.1.call-start = ((), (), s32[]{:S(2)}) async-start(), calls=%async_computation.30 | async-start | bytes 17301504 | tf_op jit(solution)/shard_map/reduce_scatter | solution.py:420
  1198.6 1448.3 %reduce-scatter.24.cloned.1.call-start = ((), (), s32[]{:S(2)}) async-start(), calls=%async_computation.29 | async-start | bytes 17301504 | tf_op jit(solution)/shard_map/reduce_scatter | solution.py:417
  1237.4 1769.5 %reduce-scatter.22.cloned.1.call-start = ((), (), s32[]{:S(2)}) async-start(), calls=%async_computation.28 | async-start | bytes 17301504 | tf_op jit(solution)/shard_map/reduce_scatter | solution.py:416
  1380.2 1986.8 %reduce-scatter.20.cloned.1.call-start = ((), (), s32[]{:S(2)}) async-start(), calls=%async_computation.27 | async-start | bytes 17301504 | tf_op jit(solution)/shard_map/reduce_scatter | solution.py:415
  (169 other events, 2484.0 us)
Sparse Core Ops, SparseCore 0:
  11.0 80.5 all-gather.13
  94.6 75.9 all-gather.15
  173.6 75.9 all-gather.9
  252.2 48.6 all-gather.17
  303.5 47.9 all-gather.11
  354.3 75.8 all-gather.19
  522.9 81.7 all-gather.23
  650.2 73.0 all-gather.21
  1086.7 66.3 reduce-scatter.29
  1156.6 66.6 reduce-scatter.27
  1226.8 66.6 reduce-scatter.15
  1297.0 66.6 reduce-scatter.17
  1366.0 134.1 reduce-scatter.31
  1503.7 422.0 all-reduce.22
  1928.4 358.2 reduce-scatter.25
  2289.5 357.3 reduce-scatter.23
  2649.6 357.3 reduce-scatter.21
  3009.7 357.3 reduce-scatter.19
where the time goes:
time: 3390 us; the launch traced here: 3370 us
  waiting for transfers between devices  2620 us (77%)
  matrix products  317 us (9%)
  local copies, waits for them, and re-layouts  155 us (5%)
  blocking collectives  149 us (4%)
  other arithmetic  80.3 us (2%)
  starting transfers between devices  37.2 us (1%)
    reduce_scatter x1, waiting for transfers between devices, per_device(): lax.psum_scatter(dense_acc[3], ('grp', 'ep'), scatter_dimension=0, tiled=...  360 us
    reduce_scatter x1, waiting for transfers between devices, per_device(): lax.psum_scatter(dense_acc[1], ('grp', 'ep'), scatter_dimension=0, tiled=...  360 us
    reduce_scatter x1, waiting for transfers between devices, per_device(): lax.psum_scatter(dense_acc[2], ('grp', 'ep'), scatter_dimension=0, tiled=...  360 us
    psum x1, waiting for transfers between devices, per_device(): lax.psum(expert_acc[0].astype(jnp.bfloat16), 'grp').astype(jnp.float32)  358 us
    reduce_scatter x1, waiting for transfers between devices, per_device(): lax.psum_scatter(dense_acc[6], ('grp', 'ep'), scatter_dimension=0, tiled=...  326 us
    unnamed x21, waiting for transfers between devices  120 us
    all_to_all x2, waiting for transfers between devices, per_device(): lax.all_to_all(outgoing, 'ep', split_axis=0, concat_axis=1, tiled=True)  120 us
    reduce_scatter x2, waiting for transfers between devices, per_device(): lax.psum_scatter(grad_key_part.astype(jnp.bfloat16), 'ep', scatter_dimens...  120 us
  transfers between devices with their start and end apart: 26, of which 22 were waited for; matrix products, arithmetic and copies ran while one was open for 14% of the time, Pallas kernels for 0%

commit v1 on v0

v1 whole, which is shorter than its diff:
```python
import math

import jax
import jax.numpy as jnp
from jax import lax
from jax.sharding import Mesh, PartitionSpec as P

HEADS = 16
CAP = 36
NORM_EPSILON = 1e-05
ROPE_BASE = 10000.0
ALL = ("x", "core", "z", "y")
SWAP = ((0, 1), (1, 0))
F32 = jnp.float32
BF16 = jnp.bfloat16


def turn(count, step):
    return tuple((i, (i + step) % count) for i in range(count))


def mm(left, right):
    return jnp.dot(left, right, preferred_element_type=F32)


def mm_rows(left, right):
    return lax.dot_general(left, right, (((0,), (0,)), ((), ())), preferred_element_type=F32)


def mm_cols(left, right):
    return lax.dot_general(left, right, (((1,), (1,)), ((), ())), preferred_element_type=F32)


def unturn(items, index):
    count = len(items)
    if count == 1:
        return items
    placed = []
    for place in range(count):
        chosen = items[(0 - place) % count]
        for at in range(1, count):
            chosen = jnp.where(index == at, items[(at - place) % count], chosen)
        placed.append(chosen)
    return placed


def gather_ep(block, z_count, y_count):
    rows = []
    for k in range(z_count):
        along = block if k == 0 else lax.ppermute(block, "z", turn(z_count, k))
        for j in range(y_count):
            rows.append(along if j == 0 else lax.ppermute(along, "y", turn(y_count, j)))
    return jnp.concatenate(rows, axis=0)


def scatter_ep(part, z_count, y_count):
    rows = part.shape[0] // (z_count * y_count)
    low = part.astype(BF16)

    def piece(source, k, j):
        at = (k * y_count + j) * rows
        return source[at : at + rows]

    total = None
    for k in list(range(1, z_count)) + [0]:
        along = piece(part, k, 0).astype(F32)
        for j in range(1, y_count):
            along = along + lax.ppermute(piece(low, k, j), "y", turn(y_count, -j)).astype(F32)
        if k:
            along = lax.ppermute(along.astype(BF16), "z", turn(z_count, -k)).astype(F32)
        total = along if total is None else total + along
    return total


def sum_ep(values, z_count, y_count):
    shape = values.shape
    values = values.reshape(shape[0], z_count, y_count, -1)
    along = values
    for j in range(1, y_count):
        along = along + jnp.roll(lax.ppermute(values, "y", turn(y_count, j)), j, axis=2)
    total = along
    for k in range(1, z_count):
        total = total + jnp.roll(lax.ppermute(along, "z", turn(z_count, k)), k, axis=1)
    return total.reshape(shape)


def gather_grp(block, x_count):
    x_at, core = lax.axis_index("x"), lax.axis_index("core")
    mine = [block] + [lax.ppermute(block, "x", turn(x_count, i)) for i in range(1, x_count)]
    theirs = [lax.ppermute(item, "core", SWAP) for item in mine]
    mine, theirs = unturn(mine, x_at), unturn(theirs, x_at)
    stacked = []
    for own, other in zip(mine, theirs):
        stacked += [jnp.where(core == 0, own, other), jnp.where(core == 0, other, own)]
    return jnp.stack(stacked)


def scatter_grp(parts, x_count):
    x_at, core = lax.axis_index("x"), lax.axis_index("core")
    parts = parts.reshape((x_count, 2) + parts.shape[1:])
    away = lax.dynamic_index_in_dim(parts, 1 - core, 1, keepdims=False).astype(BF16)
    kept = lax.dynamic_index_in_dim(parts, core, 1, keepdims=False)
    kept = kept + lax.ppermute(away, "core", SWAP).astype(F32)
    total = lax.dynamic_index_in_dim(kept, x_at, 0, keepdims=False)
    for i in range(1, x_count):
        away = lax.dynamic_index_in_dim(kept, (x_at - i) % x_count, 0, keepdims=False)
        total = total + lax.ppermute(away.astype(BF16), "x", turn(x_count, -i)).astype(F32)
    return total


def norm_scale(values):
    return lax.rsqrt(jnp.mean(values * values, axis=-1, keepdims=True) + NORM_EPSILON)


def make_per_device(x_count, z_count, y_count):
    group_size = z_count * y_count
    grp_size = 2 * x_count

    def per_device(
        tokens,
        routes,
        attn_gain,
        w_query,
        w_key,
        w_value,
        query_gain,
        key_gain,
        w_out,
        moe_gain,
        w_router,
        w_gate,
        w_up,
        w_down,
        cotangent,
    ):
        micro_count, seq_parts, row_count, width = tokens.shape
        top_count = routes.shape[3]
        tokens = tokens.reshape(micro_count, row_count, width)
        routes = routes.reshape(micro_count, row_count, top_count)
        cotangent = cotangent.reshape(micro_count, row_count, width)
        expert_count = w_router.shape[1]
        seq_len = row_count * group_size
        head_dim = width // HEADS
        half = head_dim // 2
        score_scale = 1.0 / math.sqrt(head_dim)
        weight_rows = w_query.shape[0]
        pieces = head_dim // weight_rows
        heads_here = grp_size // pieces
        head_sets = group_size // pieces
        local_width = heads_here * head_dim
        x_at, core = lax.axis_index("x"), lax.axis_index("core")
        z_at, y_at = lax.axis_index("z"), lax.axis_index("y")
        ep_at = z_at * y_count + y_at
        set_at, piece_at = ep_at // pieces, ep_at % pieces
        slots = CAP * group_size
        local_experts = w_gate.shape[0]
        ff_width = w_gate.shape[2]

        def gather(block):
            return gather_ep(block, z_count, y_count)

        def scatter(part):
            return scatter_ep(part, z_count, y_count)

        small = jnp.concatenate(
            [w_router]
            + [g[:, None] for g in (attn_gain, query_gain, key_gain, moe_gain)],
            axis=1,
        )
        small = lax.all_gather(small, ALL, axis=0, tiled=True)
        full_router = small[:, :expert_count]
        gains = small[:, expert_count:].astype(F32).T
        gain_attn, gain_query, gain_key, gain_moe = gains[0:1], gains[1], gains[2], gains[3:4]

        def head_part(vector):
            shaped = vector.reshape(pieces, heads_here, head_sets, head_dim)
            shaped = lax.dynamic_index_in_dim(shaped, piece_at, 0, keepdims=False)
            return lax.dynamic_index_in_dim(shaped, set_at, 1, keepdims=False).reshape(1, -1)

        def head_part_back(vector):
            piece_hot = jnp.arange(pieces) == piece_at
            set_hot = jnp.arange(head_sets) == set_at
            hot = piece_hot[:, None, None, None] & set_hot[None, None, :, None]
            return jnp.where(hot, vector.reshape(1, heads_here, 1, head_dim), 0.0).reshape(-1)

        gain_query, gain_key = head_part(gain_query), head_part(gain_key)

        def by_owner(weight):
            shaped = weight.reshape(weight_rows, pieces, heads_here, head_sets, head_dim)
            return shaped.transpose(3, 1, 0, 2, 4).reshape(group_size, weight_rows, local_width)

        qkv = jnp.concatenate([by_owner(w) for w in (w_query, w_key, w_value)], axis=2)
        qkv = lax.all_to_all(qkv, ("z", "y"), split_axis=0, concat_axis=0, tiled=True)
        qkv = gather_grp(qkv.reshape(group_size * weight_rows, 3 * local_width), x_count)
        qkv = qkv.reshape(width, 3 * local_width)
        out_pairs = []
        for s in range(head_sets):
            for t in range(pieces):
                for h in range(heads_here):
                    for p in range(pieces):
                        home = (t * heads_here + h) * group_size + s * pieces + p
                        user = (h * pieces + p) * group_size + s * pieces + t
                        out_pairs.append((home, user))
        out_here = lax.ppermute(w_out, ALL, out_pairs)
        out_here = gather_grp(out_here, x_count).reshape(local_width, width)

        z_from = (z_at - jnp.arange(z_count, dtype=jnp.int32)) % z_count
        y_from = (y_at - jnp.arange(y_count, dtype=jnp.int32)) % y_count
        block_from = z_from[:, None] * y_count + y_from[None, :]
        positions = (
            block_from.reshape(-1)[:, None] * row_count
            + jnp.arange(row_count, dtype=jnp.int32)[None, :]
        ).reshape(-1)
        frequency = jnp.exp(
            -math.log(ROPE_BASE) * jnp.arange(half, dtype=F32) * 2.0 / head_dim
        )
        angles = positions.astype(F32)[:, None] * frequency[None, :]
        cosine, sine = jnp.cos(angles), jnp.sin(angles)
        cos_both = jnp.concatenate([cosine, cosine], axis=1)
        sin_both = jnp.concatenate([-sine, sine], axis=1)
        allowed = positions[:, None] >= positions[None, :]

        def halves_swapped(values):
            parts = []
            for h in range(heads_here):
                at = h * head_dim
                parts += [values[:, at + half : at + head_dim], values[:, at : at + half]]
            return jnp.concatenate(parts, axis=1)

        wide_cos = jnp.concatenate([cos_both] * heads_here, axis=1)
        wide_sin = jnp.concatenate([sin_both] * heads_here, axis=1)

        def rope(values):
            return values * wide_cos + halves_swapped(values) * wide_sin

        def rope_back(values):
            return values * wide_cos - halves_swapped(values) * wide_sin

        if local_experts == 2:
            expert_at = ep_at * 2 + core
            gate_w = lax.dynamic_index_in_dim(w_gate, core, 0, keepdims=False)
            up_w = lax.dynamic_index_in_dim(w_up, core, 0, keepdims=False)
            down_w = lax.dynamic_index_in_dim(w_down, core, 0, keepdims=False)
        else:
            assert local_experts == 1
            expert_at = ep_at
            part = ff_width // 2
            gate_w = lax.dynamic_slice_in_dim(w_gate[0], core * part, part, 1)
            up_w = lax.dynamic_slice_in_dim(w_up[0], core * part, part, 1)
            down_w = lax.dynamic_slice_in_dim(w_down[0], core * part, part, 0)
        expert_hot = jnp.arange(expert_count, dtype=jnp.int32) == expert_at

        named = lax.all_gather(routes, ("core", "z", "y"), axis=0, tiled=False)
        named = named.reshape((2, z_count, y_count) + routes.shape)
        named = jnp.any(named == expert_at, axis=-1)
        named = jnp.where(core == 0, named, named[::-1])
        named = jnp.take(jnp.take(named, z_from, axis=1), y_from, axis=2)
        named = named.transpose(0, 3, 1, 2, 4).reshape(2 * micro_count, seq_len)
        earlier = jnp.arange(seq_len)[:, None] < jnp.arange(seq_len)[None, :]
        rank = mm(named.astype(BF16), earlier.astype(BF16)).astype(jnp.int32)
        rank = jnp.where(named, rank, -1)
        select = rank[:, None, :] == jnp.arange(slots, dtype=jnp.int32)[None, :, None]
        select = select.reshape(2, micro_count, slots, seq_len)
        select_low = select.astype(BF16)

        state = []
        for m in range(micro_count):
            own = tokens[m]
            rows = gather(own).astype(F32)
            row_scale = norm_scale(rows)
            normed = (rows * row_scale * gain_attn).astype(BF16)
            raw = mm(normed, qkv)
            query_raw, key_raw = raw[:, :local_width], raw[:, local_width : 2 * local_width]
            value = raw[:, 2 * local_width :].astype(BF16)
            squares = jnp.stack(
                [jnp.sum(query_raw * query_raw, axis=1), jnp.sum(key_raw * key_raw, axis=1)]
            )
            squares = sum_ep(squares, z_count, y_count)
            scales = lax.rsqrt(squares / width + NORM_EPSILON)
            query_scale, key_scale = scales[0][:, None], scales[1][:, None]
            query = rope(query_raw * query_scale * gain_query).astype(BF16)
            key = rope(key_raw * key_scale * gain_key).astype(BF16)
            probs, attended = [], []
            for h in range(heads_here):
                at = slice(h * head_dim, (h + 1) * head_dim)
                scores = mm_cols(query[:, at], key[:, at]) * score_scale
                scores = jnp.where(allowed, scores, -1e30)
                scores = jnp.exp(scores - jnp.max(scores, axis=-1, keepdims=True))
                prob = scores / jnp.sum(scores, axis=-1, keepdims=True)
                probs.append(prob)
                attended.append(mm(prob.astype(BF16), value[:, at]).astype(BF16))
            attended = jnp.concatenate(attended, axis=1)
            resid_mid = own.astype(F32) + scatter(mm(attended, out_here))
            state.append(
                dict(
                    own=own,
                    rows=rows,
                    row_scale=row_scale,
                    normed=normed,
                    query_raw=query_raw,
                    key_raw=key_raw,
                    query_scale=query_scale,
                    key_scale=key_scale,
                    query=query,
                    key=key,
                    value=value,
                    probs=probs,
                    attended=attended,
                    resid_mid=resid_mid,
                )
            )

        router_grad = jnp.zeros((width, expert_count), F32)
        outputs = []
        moe_rows, act_rows, pair_rows, gate_rows, up_rows = [], [], [], [], []
        for m in range(micro_count):
            st = state[m]
            moe_scale = norm_scale(st["resid_mid"])
            st["moe_scale"] = moe_scale
            moe_own = (st["resid_mid"] * moe_scale * gain_moe).astype(BF16)
            moe_all = [gather(moe_own)]
            moe_all.append(lax.ppermute(moe_all[0], "core", SWAP))
            cot_all = [gather(cotangent[m])]
            cot_all.append(lax.ppermute(cot_all[0], "core", SWAP))
            incoming = jnp.concatenate(
                [mm(select_low[i, m], moe_all[i]).astype(BF16) for i in range(2)], axis=0
            )
            grads_in = jnp.concatenate(
                [mm(select_low[i, m], cot_all[i]).astype(BF16) for i in range(2)], axis=0
            )
            router_probs = [
                jax.nn.softmax(mm(moe_all[i], full_router), axis=-1) for i in range(2)
            ]
            mine = [jnp.sum(jnp.where(expert_hot, p, 0.0), axis=-1) for p in router_probs]
            weights = jnp.concatenate(
                [
                    jnp.sum(jnp.where(select[i, m], mine[i][None, :], 0.0), axis=-1)
                    for i in range(2)
                ]
            )[:, None]
            gate_pre = mm(incoming, gate_w)
            up_pre = mm(incoming, up_w)
            sigmoid = jax.nn.sigmoid(gate_pre)
            activation = (gate_pre * sigmoid * up_pre).astype(BF16)
            expert_rows = mm(activation, down_w)
            wide_grads = grads_in.astype(F32)
            gate_grads = jnp.sum(wide_grads * expert_rows, axis=-1)
            pair_grad = (weights * wide_grads).astype(BF16)
            grad_act = mm_cols(pair_grad, down_w)
            grad_up = (grad_act * gate_pre * sigmoid).astype(BF16)
            grad_gate = (
                grad_act * up_pre * sigmoid * (1.0 + gate_pre * (1.0 - sigmoid))
            ).astype(BF16)
            row_grad = (mm_cols(grad_gate, gate_w) + mm_cols(grad_up, up_w)).astype(BF16)
            weighted = (weights * expert_rows).astype(BF16)
            moe_rows.append(incoming)
            act_rows.append(activation)
            pair_rows.append(pair_grad)
            gate_rows.append(grad_gate)
            up_rows.append(grad_up)
            grad_parts, out_parts = [], []
            for i in range(2):
                at = slice(i * slots, (i + 1) * slots)
                token_grads = jnp.sum(
                    jnp.where(select[i, m], gate_grads[at][:, None], 0.0), axis=0
                )
                through = (token_grads * mine[i])[:, None]
                logits_grad = jnp.where(expert_hot, through, 0.0) - router_probs[i] * through
                logits_grad = logits_grad.astype(BF16)
                router_grad = router_grad + mm_rows(moe_all[i], logits_grad)
                grad_parts.append(
                    mm_rows(select_low[i, m], row_grad[at]) + mm_cols(logits_grad, full_router)
                )
                out_parts.append(mm_rows(select_low[i, m], weighted[at]))
            grad_part = grad_parts[0] + lax.ppermute(
                grad_parts[1].astype(BF16), "core", SWAP
            ).astype(F32)
            st["grad_moe_in"] = scatter(grad_part)
            out_part = out_parts[0] + lax.ppermute(
                out_parts[1].astype(BF16), "core", SWAP
            ).astype(F32)
            outputs.append(out_part)

        moe_cat = jnp.concatenate(moe_rows, axis=0)

        def over_x(part):
            low = part.astype(BF16)
            parts = [low] + [lax.ppermute(low, "x", turn(x_count, i)) for i in range(1, x_count)]
            if x_count > 2:
                parts = unturn(parts, x_at)
            total = parts[0].astype(F32)
            for item in parts[1:]:
                total = total + item.astype(F32)
            return total.astype(BF16)

        def both_cores(own, axis):
            other = lax.ppermute(own, "core", SWAP)
            first, second = jnp.where(core == 0, own, other), jnp.where(core == 0, other, own)
            if local_experts == 2:
                return jnp.stack([first, second]).astype(F32)
            return jnp.concatenate([first, second], axis=axis)[None].astype(F32)

        d_down = both_cores(
            over_x(mm_rows(jnp.concatenate(act_rows, axis=0), jnp.concatenate(pair_rows, axis=0))),
            0,
        )
        d_gate = both_cores(over_x(mm_rows(moe_cat, jnp.concatenate(gate_rows, axis=0))), 1)
        d_up = both_cores(over_x(mm_rows(moe_cat, jnp.concatenate(up_rows, axis=0))), 1)

        d_tokens, block_out = [], []
        moe_gain_grad = jnp.zeros((width,), F32)
        attn_gain_grad = jnp.zeros((width,), F32)
        query_gain_grad = jnp.zeros((local_width,), F32)
        key_gain_grad = jnp.zeros((local_width,), F32)
        out_grads, attended_all, raw_grads, normed_all = [], [], [], []
        for m in range(micro_count):
            st = state[m]
            resid_mid, scale = st["resid_mid"], st["moe_scale"]
            grad = st["grad_moe_in"]
            moe_gain_grad = moe_gain_grad + jnp.sum(grad * resid_mid * scale, axis=0)
            inner = grad * gain_moe
            grad_mid = (
                cotangent[m].astype(F32)
                + scale * inner
                - resid_mid * (scale**3 * jnp.mean(resid_mid * inner, axis=-1, keepdims=True))
            )
            grad_attn = gather(grad_mid.astype(BF16))
            out_grads.append(grad_attn)
            attended_all.append(st["attended"])
            grad_attended = mm_cols(grad_attn, out_here).astype(BF16)
            query, key, value = st["query"], st["key"], st["value"]
            grad_query, grad_key, grad_value = [], [], []
            for h in range(heads_here):
                at = slice(h * head_dim, (h + 1) * head_dim)
                prob = st["probs"][h]
                grad_value.append(mm_rows(prob.astype(BF16), grad_attended[:, at]).astype(BF16))
                grad_pa = mm_cols(grad_attended[:, at], value[:, at])
                delta = jnp.sum(prob * grad_pa, axis=-1, keepdims=True)
                grad_scores = (prob * (grad_pa - delta)).astype(BF16)
                grad_query.append(mm(grad_scores, key[:, at]) * score_scale)
                grad_key.append(mm_rows(grad_scores, query[:, at]) * score_scale)
            grad_query = rope_back(jnp.concatenate(grad_query, axis=1))
            grad_key = rope_back(jnp.concatenate(grad_key, axis=1))
            inner_query, inner_key = grad_query * gain_query, grad_key * gain_key
            query_raw, key_raw = st["query_raw"], st["key_raw"]
            query_scale, key_scale = st["query_scale"], st["key_scale"]
            query_gain_grad = query_gain_grad + jnp.sum(grad_query * query_raw * query_scale, axis=0)
            key_gain_grad = key_gain_grad + jnp.sum(grad_key * key_raw * key_scale, axis=0)
            means = jnp.stack(
                [jnp.sum(inner_query * query_raw, axis=1), jnp.sum(inner_key * key_raw, axis=1)]
            )
            means = sum_ep(means, z_count, y_count) / width
            query_back = (
                query_scale * inner_query - query_raw * (query_scale**3 * means[0][:, None])
            ).astype(BF16)
            key_back = (
                key_scale * inner_key - key_raw * (key_scale**3 * means[1][:, None])
            ).astype(BF16)
            raw_grad = jnp.concatenate([query_back, key_back] + grad_value, axis=1)
            raw_grads.append(raw_grad)
            normed_all.append(st["normed"])
            normed_part = mm_cols(raw_grad, qkv)
            attn_gain_grad = attn_gain_grad + jnp.sum(
                normed_part * st["rows"] * st["row_scale"], axis=0
            )
            grad_normed = scatter(normed_part)
            resid_in = st["own"].astype(F32)
            in_scale = norm_scale(resid_in)
            inner = grad_normed * gain_attn
            d_tokens.append(
                grad_mid
                + in_scale * inner
                - resid_in * (in_scale**3 * jnp.mean(resid_in * inner, axis=-1, keepdims=True))
            )
            block_out.append((resid_mid + scatter(outputs[m])).astype(BF16))

        qkv_grad = mm_rows(jnp.concatenate(normed_all, axis=0), jnp.concatenate(raw_grads, axis=0))
        qkv_grad = scatter_grp(qkv_grad.reshape(grp_size, -1, 3 * local_width), x_count)
        qkv_grad = qkv_grad.astype(BF16).reshape(group_size, weight_rows, 3 * local_width)
        qkv_grad = lax.all_to_all(
            qkv_grad, ("z", "y"), split_axis=0, concat_axis=0, tiled=True
        ).astype(F32)

        def by_row(grads):
            shaped = grads.reshape(head_sets, pieces, weight_rows, heads_here, head_dim)
            return shaped.transpose(2, 1, 3, 0, 4).reshape(weight_rows, width)

        d_query = by_row(qkv_grad[:, :, :local_width])
        d_key = by_row(qkv_grad[:, :, local_width : 2 * local_width])
        d_value = by_row(qkv_grad[:, :, 2 * local_width :])
        out_grad = mm_rows(
            jnp.concatenate(attended_all, axis=0), jnp.concatenate(out_grads, axis=0)
        )
        out_grad = scatter_grp(out_grad.reshape(grp_size, weight_rows, width), x_count)
        d_out = lax.ppermute(
            out_grad.astype(BF16), ALL, [(user, home) for home, user in out_pairs]
        ).astype(F32)

        device_count = grp_size * group_size
        vectors = jnp.stack(
            [
                attn_gain_grad,
                head_part_back(query_gain_grad),
                head_part_back(key_gain_grad),
                moe_gain_grad,
            ]
        )
        vectors = vectors.reshape(4, device_count, weight_rows).transpose(1, 0, 2)
        small_grads = jnp.concatenate(
            [
                vectors.reshape(device_count, 4 * weight_rows),
                router_grad.reshape(device_count, weight_rows * expert_count),
            ],
            axis=1,
        )
        small_grads = lax.all_to_all(small_grads, ALL, split_axis=0, concat_axis=0, tiled=True)
        small_grads = jnp.sum(small_grads, axis=0)
        gain_grads = small_grads[: 4 * weight_rows].reshape(4, weight_rows)
        d_router = small_grads[4 * weight_rows :].reshape(weight_rows, expert_count)

        shape = (micro_count, seq_parts, row_count, width)
        return (
            jnp.stack(block_out).reshape(shape),
            jnp.stack(d_tokens).reshape(shape),
            gain_grads[0],
            d_query,
            d_key,
            d_value,
            gain_grads[1],
            gain_grads[2],
            d_out,
            gain_grads[3],
            d_router,
            d_gate,
            d_up,
            d_down,
        )

    return per_device


def solution(mesh):
    devices = mesh.devices
    x_count, y_count, z_count = (
        len({device.coords[axis] for device in devices.flat}) for axis in range(3)
    )
    fine = Mesh(devices.reshape(x_count, 2, z_count, y_count), ALL)
    grp, ep = ("x", "core"), ("z", "y")
    by_token = P(None, grp, ep, None)
    vector, matrix, expert = P(ALL), P(ALL, None), P(ep, None, None)
    return jax.shard_map(
        make_per_device(x_count, z_count, y_count),
        mesh=fine,
        in_specs=(
            by_token,
            by_token,
            vector,
            matrix,
            matrix,
            matrix,
            vector,
            vector,
            matrix,
            vector,
            matrix,
            expert,
            expert,
            expert,
            by_token,
        ),
        out_specs=(
            by_token,
            by_token,
            vector,
            matrix,
            matrix,
            matrix,
            vector,
            vector,
            matrix,
            vector,
            matrix,
            expert,
            expert,
            expert,
        ),
        check_vma=False,
    )
```

time: 3390 us -> 1190 us (0.35)
  waiting for transfers between devices: 2620 us -> 396 us
  starting transfers between devices: 37.2 us -> 276 us
  matrix products: 317 us -> 178 us
  local copies, waits for them, and re-layouts: 155 us -> 80.3 us
  other arithmetic: 80.3 us -> 125 us
    reduce_scatter x6 -> x0, waiting for transfers between devices: 1530 us -> none  [the longest x1 360 us: per_device(): lax.psum_scatter(dense_acc[3], ('grp', 'ep'), scatter_dimension=0, tiled=...]
    psum x1 -> x0, waiting for transfers between devices: 358 us -> none  [per_device(): lax.psum(expert_acc[0].astype(jnp.bfloat16), 'grp').astype(jnp.float32)]
    ppermute x0 -> x154, waiting for transfers between devices: none -> 338 us  [the longest x32 86.9 us: scatter_ep(): lax.ppermute(piece(low, k, j), 'y', turn(y_count, -j)).astype(F32)]
    all_to_all x8 -> x3, waiting for transfers between devices: 354 us -> 58.1 us  [the longest x1 44.3 us: per_device(): lax.all_to_all(small_grads, ALL, split_axis=0, concat_axis=0, tiled=True)]
    all_gather x8 -> x0, waiting for transfers between devices: 261 us -> none  [the longest x1 76.4 us: per_device(): lax.all_gather(w_out, ('grp', 'ep'), axis=0, tiled=True)]
    ppermute x0 -> x154, starting transfers between devices: none -> 256 us  [the longest x24 99.8 us: scatter_ep(): along = lax.ppermute(along.astype(BF16), 'z', turn(z_count, -k)).astype(F32)]
    dot_general x62 -> x78, matrix products: 317 us -> 178 us  [the longest x22 65.4 us: mm_cols(): lax.dot_general(left, right, (((1,), (1,)), ((), ())), preferred_element_...]
    unnamed x21 -> x0, waiting for transfers between devices: 120 us -> none
  transfers between devices with their start and end apart: 26 -> 157, of which waited for: 22 -> 74; matrix products, arithmetic and copies ran while one was open for 14% -> 22% of each run, Pallas kernels for 0% -> 0%
where the time goes in v1:
time: 1190 us; the launch traced here: 1180 us
  waiting for transfers between devices  396 us (33%)
  starting transfers between devices  276 us (23%)
  matrix products  178 us (15%)
  other arithmetic  125 us (11%)
  blocking collectives  121 us (10%)
  local copies, waits for them, and re-layouts  80.3 us (7%)
    ppermute x24, starting transfers between devices, scatter_ep(): along = lax.ppermute(along.astype(BF16), 'z', turn(z_count, -k)).astype(F32)  99.8 us
    ppermute x32, waiting for transfers between devices, scatter_ep(): lax.ppermute(piece(low, k, j), 'y', turn(y_count, -j)).astype(F32)  86.9 us
    ppermute x32, waiting for transfers between devices, gather_ep(): rows.append(along if j == 0 else lax.ppermute(along, 'y', turn(y_count, j)))  82.5 us
    ppermute x24, waiting for transfers between devices, scatter_ep(): along = lax.ppermute(along.astype(BF16), 'z', turn(z_count, -k)).astype(F32)  73.4 us
    all_gather x1, blocking collectives, per_device(): small = lax.all_gather(small, ALL, axis=0, tiled=True)  66.4 us
    dot_general x22, matrix products, mm_cols(): lax.dot_general(left, right, (((1,), (1,)), ((), ())), preferred_element_...  65.4 us
    dot_general x31, matrix products, mm(): return jnp.dot(left, right, preferred_element_type=F32)  57 us
    dot_general x25, matrix products, mm_rows(): lax.dot_general(left, right, (((0,), (0,)), ((), ())), preferred_element_...  56.1 us
  transfers between devices with their start and end apart: 157, of which 74 were waited for; matrix products, arithmetic and copies ran while one was open for 22% of the time, Pallas kernels for 0%

profile of v1, /device:TPU:0, one launch (start us, length us, event | category | flops | bytes accessed | tf_op | source)
XLA Modules:
  0.0 1181.9 jit_solution(14917750271615068458)
XLA Ops:
  26.2 54.7 %all-gather = s32[32,1,64,8]{2,3,1,0:T(8,128)S(1)} all-gather(s32[2,1,64,8]{2,3,1,0:T(8,128)S(1)} %copy-done.111), channel_id=2, replica_groups=mesh['x'=2,'core'=2,'z'=4,'y'=2] {'core','z','y'}, dimensions={0}, use_global_device_ids=true | all-gather | bytes 69632 | tf_op jit(solution)/shard_map/all_gather | solution.py:253
  82.8 66.4 %all-gather.1 = bf16[32,64,20]{1,2,0:T(8,128)(2,1)S(1)} all-gather(bf16[1,64,20]{1,2,0:T(8,128)(2,1)S(1)} %bitcast.371), channel_id=1, replica_groups=mesh['x'=2,'core'=2,'z'=4,'y'=2] {'x','core','z','y'}, dimensions={0}, use_global_device_ids=true | all-gather | bytes 84480 | tf_op jit(solution)/shard_map/all_gather | solution.py:170
  245.2 9.4 collective-permute-done.81
  275.0 12.7 %collective-permute-done.7 = bf16[512,768]{1,0:T(8,128)(2,1)S(1)} collective-permute-done((bf16[512,768]{1,0:T(8,128)(2,1)}, bf16[512,768]{1,0:T(8,128)(2,1)S(1)}, u32[]{:S(2)}, u32[]{:S(2)}) %collective-permute-start.7) | collective-permute-done | bytes 786464 | tf_op jit(solution)/shard_map/ppermute | solution.py:89
  392.5 9.4 collective-permute-done.55
  401.9 8.7 collective-permute-done.21
  423.6 15.7 %collective-permute-done.60 = bf16[64,2048]{1,0:T(8,128)(2,1)S(1)} collective-permute-done((bf16[64,2048]{1,0:T(8,128)(2,1)S(1)}, bf16[64,2048]{1,0:T(8,128)(2,1)S(1)}, u32[]{:S(2)}, u32[]{:S(2)}) %collective-permute-start.60) | collective-permute-done | bytes 262176 | tf_op jit(solution)/shard_map/ppermute | solution.py:50
  509.8 8.1 multiply_convert_fusion.5
  527.7 8.1 multiply_convert_fusion.3
  535.9 7.4 convolution_convert_fusion
  559.1 8.8 convolution_convert_fusion.1
  588.9 7.6 fusion.46
  627.1 9.5 collective-permute-done.38
  644.5 8.9 collective-permute-done.84
  664.7 17.4 %collective-permute-start.35 = (bf16[64,2048]{1,0:T(8,128)(2,1)S(1)}, bf16[64,2048]{1,0:T(8,128)(2,1)S(1)}, u32[]{:S(2)}, u32[]{:S(2)}) collective-permute-start(bf16[64,2048]{1,0:T(8,128)(2,1)S(1)} %get-tuple-element.166), channel_id=1, source_target_pairs={{0,6},{2,0},{4,2},{6,4},{1,7},{3,1},{5,3},{7,5},{8,14},{10,8},{12,... | collective-permute-start | bytes 786440 | tf_op jit(solution)/shard_map/ppermute | solution.py:70
  705.7 16.0 %collective-permute-start.69 = (bf16[64,2048]{1,0:T(8,128)(2,1)S(1)}, bf16[64,2048]{1,0:T(8,128)(2,1)S(1)}, u32[]{:S(2)}, u32[]{:S(2)}) collective-permute-start(bf16[64,2048]{1,0:T(8,128)(2,1)S(1)} %get-tuple-element.169), channel_id=1, source_target_pairs={{0,6},{2,0},{4,2},{6,4},{1,7},{3,1},{5,3},{7,5},{8,14},{10,8},{12,... | collective-permute-start | bytes 786440 | tf_op jit(solution)/shard_map/ppermute | solution.py:70
  724.2 7.3 collective-permute-done.87
  732.1 12.5 %collective-permute-start.119 = (bf16[64,2048]{1,0:T(8,128)(2,1)S(1)}, bf16[64,2048]{1,0:T(8,128)(2,1)S(1)}, u32[]{:S(2)}, u32[]{:S(2)}) collective-permute-start(bf16[64,2048]{1,0:T(8,128)(2,1)S(1)} %get-tuple-element.157), channel_id=1, source_target_pairs={{0,6},{2,0},{4,2},{6,4},{1,7},{3,1},{5,3},{7,5},{8,14},{10,8},{12,... | collective-permute-start | bytes 786440 | tf_op jit(solution)/shard_map/ppermute | solution.py:70
  750.0 9.6 collective-permute-done.71
  764.8 12.9 %collective-permute-start.92 = (bf16[64,2048]{1,0:T(8,128)(2,1)S(1)}, bf16[64,2048]{1,0:T(8,128)(2,1)S(1)}, u32[]{:S(2)}, u32[]{:S(2)}) collective-permute-start(bf16[64,2048]{1,0:T(8,128)(2,1)S(1)} %get-tuple-element.123), channel_id=1, source_target_pairs={{0,2},{2,4},{4,6},{6,0},{1,3},{3,5},{5,7},{7,1},{8,10},{10,12},{12... | collective-permute-start | bytes 786440 | tf_op jit(solution)/shard_map/ppermute | solution.py:50
  796.6 14.6 %collective-permute-done.93 = bf16[64,2048]{1,0:T(8,128)(2,1)S(1)} collective-permute-done((bf16[64,2048]{1,0:T(8,128)(2,1)S(1)}, bf16[64,2048]{1,0:T(8,128)(2,1)S(1)}, u32[]{:S(2)}, u32[]{:S(2)}) %collective-permute-start.93) | collective-permute-done | bytes 262176 | tf_op jit(solution)/shard_map/ppermute | solution.py:52
  933.4 8.5 fusion.18
  969.1 44.3 %all-to-all-done.1 = f32[32,1,1280]{2,1,0:T(1,128)S(1)} async-done(((f32[32,1,1280]{2,1,0:T(1,128)}), f32[32,1,1280]{2,1,0:T(1,128)S(1)}, u32[]{:S(2)}, u32[]{:S(2)}) %all-to-all-start.1) | async-done | bytes 163872 | tf_op jit(solution)/shard_map/all_to_all | solution.py:516
  1016.3 7.8 add_convert_fusion.1
  1060.3 7.5 collective-permute-start.105
  1079.6 12.7 %collective-permute-done.105 = bf16[64,2048]{1,0:T(8,128)(2,1)S(1)} collective-permute-done((bf16[64,2048]{1,0:T(8,128)(2,1)S(1)}, bf16[64,2048]{1,0:T(8,128)(2,1)S(1)}, u32[]{:S(2)}, u32[]{:S(2)}) %collective-permute-start.105) | collective-permute-done | bytes 262176 | tf_op jit(solution)/shard_map/ppermute | solution.py:70
  1098.1 12.8 %all-to-all-start.2 = ((bf16[8,64,768]{2,1,0:T(8,128)(2,1)}), bf16[8,64,768]{2,1,0:T(8,128)(2,1)S(1)}, u32[]{:S(2)}, u32[]{:S(2)}) async-start(bf16[8,64,768]{2,1,0:T(8,128)(2,1)} %bitcast.330), calls=%async_computation.2 | async-start | bytes 1572864 | tf_op jit(solution)/shard_map/all_to_all | solution.py:480
  1116.9 13.8 %all-to-all-done.2 = bf16[8,64,768]{2,1,0:T(8,128)(2,1)S(1)} async-done(((bf16[8,64,768]{2,1,0:T(8,128)(2,1)}), bf16[8,64,768]{2,1,0:T(8,128)(2,1)S(1)}, u32[]{:S(2)}, u32[]{:S(2)}) %all-to-all-start.2) | async-done | bytes 786464 | tf_op jit(solution)/shard_map/all_to_all | solution.py:480
  1140.7 9.4 maximum_convert_fusion.2
  1150.2 11.0 select_bitcast_fusion.3
  1161.2 10.7 maximum_convert_fusion.1
  1171.9 9.4 maximum_convert_fusion
  (1044 shorter events, 703.5 us)
Async XLA Ops:
  2.6 181.2 %collective-permute-start.3 = (bf16[64,2048]{1,0:T(8,128)(2,1)}, bf16[64,2048]{1,0:T(8,128)(2,1)}, u32[]{:S(2)}, u32[]{:S(2)}) collective-permute-start(bf16[64,2048]{1,0:T(8,128)(2,1)} %get-tuple-element.247), channel_id=1, source_target_pairs={{0,4},{2,6},{4,0},{6,2},{1,5},{3,7},{5,1},{7,3},{8,12},{10,14},{12... | collective-permute-start | bytes 786440 | tf_op jit(solution)/shard_map/ppermute | solution.py:50
  6.6 148.4 %collective-permute-start.1 = (bf16[64,2048]{1,0:T(8,128)(2,1)}, bf16[64,2048]{1,0:T(8,128)(2,1)}, u32[]{:S(2)}, u32[]{:S(2)}) collective-permute-start(bf16[64,2048]{1,0:T(8,128)(2,1)} %get-tuple-element.247), channel_id=1, source_target_pairs={{0,2},{2,4},{4,6},{6,0},{1,3},{3,5},{5,7},{7,1},{8,10},{10,12},{12... | collective-permute-start | bytes 786440 | tf_op jit(solution)/shard_map/ppermute | solution.py:50
  8.2 144.8 %collective-permute-start = (bf16[64,2048]{1,0:T(8,128)(2,1)}, bf16[64,2048]{1,0:T(8,128)(2,1)}, u32[]{:S(2)}, u32[]{:S(2)}) collective-permute-start(bf16[64,2048]{1,0:T(8,128)(2,1)} %get-tuple-element.247), channel_id=1, source_target_pairs={{0,1},{1,0},{2,3},{3,2},{4,5},{5,4},{6,7},{7,6},{8,9},{9,8},{10,11... | collective-permute-start | bytes 786440 | tf_op jit(solution)/shard_map/ppermute | solution.py:52
  9.7 189.4 %collective-permute-start.5 = (bf16[64,2048]{1,0:T(8,128)(2,1)}, bf16[64,2048]{1,0:T(8,128)(2,1)}, u32[]{:S(2)}, u32[]{:S(2)}) collective-permute-start(bf16[64,2048]{1,0:T(8,128)(2,1)} %get-tuple-element.247), channel_id=1, source_target_pairs={{0,6},{2,0},{4,2},{6,4},{1,7},{3,1},{5,3},{7,5},{8,14},{10,8},{12,... | collective-permute-start | bytes 786440 | tf_op jit(solution)/shard_map/ppermute | solution.py:50
  15.6 253.2 %all-to-all-start = ((bf16[8,64,768]{2,1,0:T(8,128)(2,1)}), bf16[8,64,768]{2,1,0:T(8,128)(2,1)}, u32[]{:S(2)}, u32[]{:S(2)}) async-start(bf16[8,64,768]{2,1,0:T(8,128)(2,1)} %pad_maximum_fusion.13), calls=%async_computation | async-start | bytes 1572864 | tf_op jit(solution)/shard_map/all_to_all | solution.py:193
  20.0 184.3 %collective-permute-start.44 = (bf16[64,2048]{1,0:T(8,128)(2,1)}, bf16[64,2048]{1,0:T(8,128)(2,1)}, u32[]{:S(2)}, u32[]{:S(2)}) collective-permute-start(bf16[64,2048]{1,0:T(8,128)(2,1)} %get-tuple-element.248), channel_id=1, source_target_pairs={{0,4},{2,6},{4,0},{6,2},{1,5},{3,7},{5,1},{7,3},{8,12},{10,14},{12... | collective-permute-start | bytes 786440 | tf_op jit(solution)/shard_map/ppermute | solution.py:50
  183.0 60.0 %collective-permute-start.46 = (bf16[64,2048]{1,0:T(8,128)(2,1)}, bf16[64,2048]{1,0:T(8,128)(2,1)S(1)}, u32[]{:S(2)}, u32[]{:S(2)}) collective-permute-start(bf16[64,2048]{1,0:T(8,128)(2,1)} %get-tuple-element.248), channel_id=1, source_target_pairs={{0,6},{2,0},{4,2},{6,4},{1,7},{3,1},{5,3},{7,5},{8,14},{10,8},{12,... | collective-permute-start | bytes 786440 | tf_op jit(solution)/shard_map/ppermute | solution.py:50
  183.8 47.8 %collective-permute-start.112 = (bf16[64,2048]{1,0:T(8,128)(2,1)S(1)}, bf16[64,2048]{1,0:T(8,128)(2,1)S(1)}, u32[]{:S(2)}, u32[]{:S(2)}) collective-permute-start(bf16[64,2048]{1,0:T(8,128)(2,1)S(1)} %copy-done.79), channel_id=1, source_target_pairs={{0,4},{2,6},{4,0},{6,2},{1,5},{3,7},{5,1},{7,3},{8,12},{10,14},{12... | collective-permute-start | bytes 786440 | tf_op jit(solution)/shard_map/ppermute | solution.py:50
  199.1 44.0 %collective-permute-start.114 = (bf16[64,2048]{1,0:T(8,128)(2,1)S(1)}, bf16[64,2048]{1,0:T(8,128)(2,1)S(1)}, u32[]{:S(2)}, u32[]{:S(2)}) collective-permute-start(bf16[64,2048]{1,0:T(8,128)(2,1)S(1)} %copy-done.79), channel_id=1, source_target_pairs={{0,6},{2,0},{4,2},{6,4},{1,7},{3,1},{5,3},{7,5},{8,14},{10,8},{12,... | collective-permute-start | bytes 786440 | tf_op jit(solution)/shard_map/ppermute | solution.py:50
  231.5 59.7 %collective-permute-start.17 = (bf16[64,2048]{1,0:T(8,128)(2,1)}, bf16[64,2048]{1,0:T(8,128)(2,1)}, u32[]{:S(2)}, u32[]{:S(2)}) collective-permute-start(bf16[64,2048]{1,0:T(8,128)(2,1)} %collective-permute-done.14), channel_id=1, source_target_pairs={{0,8},{8,0},{1,9},{9,1},{2,10},{10,2},{3,11},{11,3},{4,12},{12,4},... | collective-permute-start | bytes 786440 | tf_op jit(solution)/shard_map/ppermute | solution.py:90
  257.4 98.5 %collective-permute-start.82 = (bf16[512,2048]{1,0:T(8,128)(2,1)}, bf16[512,2048]{1,0:T(8,128)(2,1)}, u32[]{:S(2)}, u32[]{:S(2)}) collective-permute-start(bf16[512,2048]{1,0:T(8,128)(2,1)} %constant_dynamic-update-slice_fusion.36), channel_id=1, source_target_pairs={{0,8},{8,0},{1,9},{9,1},{2,10},{10,2},{3,11},{11,3},{4,12},{12,4},... | collective-permute-start | bytes 6291464 | tf_op jit(solution)/shard_map/ppermute | solution.py:324
  257.4 34.4 %collective-permute-start.16 = (bf16[64,2048]{1,0:T(8,128)(2,1)}, bf16[64,2048]{1,0:T(8,128)(2,1)}, u32[]{:S(2)}, u32[]{:S(2)}) collective-permute-start(bf16[64,2048]{1,0:T(8,128)(2,1)} %collective-permute-done.15), channel_id=1, source_target_pairs={{0,8},{8,0},{1,9},{9,1},{2,10},{10,2},{3,11},{11,3},{4,12},{12,4},... | collective-permute-start | bytes 786440 | tf_op jit(solution)/shard_map/ppermute | solution.py:90
  291.3 121.7 %collective-permute-start.116 = (bf16[512,2048]{1,0:T(8,128)(2,1)}, bf16[512,2048]{1,0:T(8,128)(2,1)}, u32[]{:S(2)}, u32[]{:S(2)}) collective-permute-start(bf16[512,2048]{1,0:T(8,128)(2,1)} %constant_dynamic-update-slice_fusion.54), channel_id=1, source_target_pairs={{0,8},{8,0},{1,9},{9,1},{2,10},{10,2},{3,11},{11,3},{4,12},{12,4},... | collective-permute-start | bytes 6291464 | tf_op jit(solution)/shard_map/ppermute | solution.py:324
  558.5 39.3 %collective-permute-start.67 = (bf16[512,2048]{1,0:T(8,128)(2,1)}, bf16[512,2048]{1,0:T(8,128)(2,1)S(1)}, u32[]{:S(2)}, u32[]{:S(2)}) collective-permute-start(bf16[512,2048]{1,0:T(8,128)(2,1)} %convolution_convert_fusion.2), channel_id=1, source_target_pairs={{0,8},{8,0},{1,9},{9,1},{2,10},{10,2},{3,11},{11,3},{4,12},{12,4},... | collective-permute-start | bytes 6291464 | tf_op jit(solution)/shard_map/ppermute | solution.py:379
  559.0 42.4 %collective-permute-start.33 = (bf16[512,2048]{1,0:T(8,128)(2,1)}, bf16[512,2048]{1,0:T(8,128)(2,1)S(1)}, u32[]{:S(2)}, u32[]{:S(2)}) collective-permute-start(bf16[512,2048]{1,0:T(8,128)(2,1)} %convolution_convert_fusion.3), channel_id=1, source_target_pairs={{0,8},{8,0},{1,9},{9,1},{2,10},{10,2},{3,11},{11,3},{4,12},{12,4},... | collective-permute-start | bytes 6291464 | tf_op jit(solution)/shard_map/ppermute | solution.py:379
  605.8 38.3 %collective-permute-start.40 = (bf16[64,2048]{1,0:T(8,128)(2,1)S(1)}, bf16[64,2048]{1,0:T(8,128)(2,1)S(1)}, u32[]{:S(2)}, u32[]{:S(2)}) collective-permute-start(bf16[64,2048]{1,0:T(8,128)(2,1)S(1)} %get-tuple-element.199), channel_id=1, source_target_pairs={{0,1},{1,0},{2,3},{3,2},{4,5},{5,4},{6,7},{7,6},{8,9},{9,8},{10,11... | collective-permute-start | bytes 786440 | tf_op jit(solution)/shard_map/ppermute | solution.py:68
  619.7 62.6 %collective-permute-start.118 = (bf16[64,2048]{1,0:T(8,128)(2,1)S(1)}, bf16[64,2048]{1,0:T(8,128)(2,1)S(1)}, u32[]{:S(2)}, u32[]{:S(2)}) collective-permute-start(bf16[64,2048]{1,0:T(8,128)(2,1)S(1)} %get-tuple-element.186), channel_id=1, source_target_pairs={{0,1},{1,0},{2,3},{3,2},{4,5},{5,4},{6,7},{7,6},{8,9},{9,8},{10,11... | collective-permute-start | bytes 786440 | tf_op jit(solution)/shard_map/ppermute | solution.py:68
  644.2 38.2 %collective-permute-start.122 = (bf16[64,2048]{1,0:T(8,128)(2,1)S(1)}, bf16[64,2048]{1,0:T(8,128)(2,1)S(1)}, u32[]{:S(2)}, u32[]{:S(2)}) collective-permute-start(bf16[64,2048]{1,0:T(8,128)(2,1)S(1)} %get-tuple-element.188), channel_id=1, source_target_pairs={{0,1},{1,0},{2,3},{3,2},{4,5},{5,4},{6,7},{7,6},{8,9},{9,8},{10,11... | collective-permute-start | bytes 786440 | tf_op jit(solution)/shard_map/ppermute | solution.py:68
  694.9 36.6 %collective-permute-start.87 = (bf16[64,2048]{1,0:T(8,128)(2,1)S(1)}, bf16[64,2048]{1,0:T(8,128)(2,1)S(1)}, u32[]{:S(2)}, u32[]{:S(2)}) collective-permute-start(bf16[64,2048]{1,0:T(8,128)(2,1)S(1)} %get-tuple-element.165), channel_id=1, source_target_pairs={{0,4},{2,6},{4,0},{6,2},{1,5},{3,7},{5,1},{7,3},{8,12},{10,14},{12... | collective-permute-start | bytes 786440 | tf_op jit(solution)/shard_map/ppermute | solution.py:70
  705.1 39.5 %collective-permute-start.124 = (bf16[64,2048]{1,0:T(8,128)(2,1)S(1)}, bf16[64,2048]{1,0:T(8,128)(2,1)S(1)}, u32[]{:S(2)}, u32[]{:S(2)}) collective-permute-start(bf16[64,2048]{1,0:T(8,128)(2,1)S(1)} %get-tuple-element.187), channel_id=1, source_target_pairs={{0,1},{1,0},{2,3},{3,2},{4,5},{5,4},{6,7},{7,6},{8,9},{9,8},{10,11... | collective-permute-start | bytes 786440 | tf_op jit(solution)/shard_map/ppermute | solution.py:68
  705.7 39.5 %collective-permute-start.69 = (bf16[64,2048]{1,0:T(8,128)(2,1)S(1)}, bf16[64,2048]{1,0:T(8,128)(2,1)S(1)}, u32[]{:S(2)}, u32[]{:S(2)}) collective-permute-start(bf16[64,2048]{1,0:T(8,128)(2,1)S(1)} %get-tuple-element.169), channel_id=1, source_target_pairs={{0,6},{2,0},{4,2},{6,4},{1,7},{3,1},{5,3},{7,5},{8,14},{10,8},{12,... | collective-permute-start | bytes 786440 | tf_op jit(solution)/shard_map/ppermute | solution.py:70
  745.2 36.9 %collective-permute-start.121 = (bf16[64,2048]{1,0:T(8,128)(2,1)S(1)}, bf16[64,2048]{1,0:T(8,128)(2,1)S(1)}, u32[]{:S(2)}, u32[]{:S(2)}) collective-permute-start(bf16[64,2048]{1,0:T(8,128)(2,1)S(1)} %get-tuple-element.159), channel_id=1, source_target_pairs={{0,4},{2,6},{4,0},{6,2},{1,5},{3,7},{5,1},{7,3},{8,12},{10,14},{12... | collective-permute-start | bytes 786440 | tf_op jit(solution)/shard_map/ppermute | solution.py:70
  748.3 266.6 %collective-permute-start.150 = (bf16[2048,1024]{1,0:T(8,128)(2,1)}, bf16[2048,1024]{1,0:T(8,128)(2,1)}, u32[]{:S(2)}, u32[]{:S(2)}) collective-permute-start(bf16[2048,1024]{1,0:T(8,128)(2,1)} %convolution_convert_fusion), channel_id=1, source_target_pairs={{0,16},{16,0},{1,17},{17,1},{2,18},{18,2},{3,19},{19,3},{4,20},{20... | collective-permute-start | bytes 12582920 | tf_op jit(solution)/shard_map/ppermute | solution.py:388
  784.8 246.2 %collective-permute-start.148 = (bf16[2048,1024]{1,0:T(8,128)(2,1)}, bf16[2048,1024]{1,0:T(8,128)(2,1)}, u32[]{:S(2)}, u32[]{:S(2)}) collective-permute-start(bf16[2048,1024]{1,0:T(8,128)(2,1)} %convolution_convert_fusion.1), channel_id=1, source_target_pairs={{0,16},{16,0},{1,17},{17,1},{2,18},{18,2},{3,19},{19,3},{4,20},{20... | collective-permute-start | bytes 12582920 | tf_op jit(solution)/shard_map/ppermute | solution.py:388
  832.6 36.1 %collective-permute-start.130 = (bf16[64,2048]{1,0:T(8,128)(2,1)}, bf16[64,2048]{1,0:T(8,128)(2,1)}, u32[]{:S(2)}, u32[]{:S(2)}) collective-permute-start(bf16[64,2048]{1,0:T(8,128)(2,1)} %get-tuple-element.121), channel_id=1, source_target_pairs={{0,6},{2,0},{4,2},{6,4},{1,7},{3,1},{5,3},{7,5},{8,14},{10,8},{12,... | collective-permute-start | bytes 786440 | tf_op jit(solution)/shard_map/ppermute | solution.py:50
  868.7 155.3 %collective-permute-start.152 = (bf16[1024,2048]{1,0:T(8,128)(2,1)}, bf16[1024,2048]{1,0:T(8,128)(2,1)}, u32[]{:S(2)}, u32[]{:S(2)}) collective-permute-start(bf16[1024,2048]{1,0:T(8,128)(2,1)} %fusion.46), channel_id=1, source_target_pairs={{0,16},{16,0},{1,17},{17,1},{2,18},{18,2},{3,19},{19,3},{4,20},{20... | collective-permute-start | bytes 12582920 | tf_op jit(solution)/shard_map/ppermute | solution.py:388
  946.7 66.7 %all-to-all-start.1 = ((f32[32,1,1280]{2,1,0:T(1,128)}), f32[32,1,1280]{2,1,0:T(1,128)S(1)}, u32[]{:S(2)}, u32[]{:S(2)}) async-start(f32[32,1,1280]{2,1,0:T(1,128)} %copy.138), calls=%async_computation.1 | async-start | bytes 327680 | tf_op jit(solution)/shard_map/all_to_all | solution.py:516
  961.6 75.9 %collective-permute-start.145 = (bf16[2,64,2048]{2,1,0:T(8,128)(2,1)}, bf16[2,64,2048]{2,1,0:T(8,128)(2,1)}, u32[]{:S(2)}, u32[]{:S(2)}) collective-permute-start(bf16[2,64,2048]{2,1,0:T(8,128)(2,1)} %fusion.145), channel_id=1, source_target_pairs={{0,8},{8,0},{1,9},{9,1},{2,10},{10,2},{3,11},{11,3},{4,12},{12,4},... | collective-permute-start | bytes 1572872 | tf_op jit(solution)/shard_map/ppermute | solution.py:103
  966.7 87.4 %collective-permute-start.143 = (bf16[2,512,768]{2,1,0:T(8,128)(2,1)S(1)}, bf16[2,512,768]{2,1,0:T(8,128)(2,1)}, u32[]{:S(2)}, u32[]{:S(2)}) collective-permute-start(bf16[2,512,768]{2,1,0:T(8,128)(2,1)S(1)} %fusion.76), channel_id=1, source_target_pairs={{0,8},{8,0},{1,9},{9,1},{2,10},{10,2},{3,11},{11,3},{4,12},{12,4},... | collective-permute-start | bytes 4718600 | tf_op jit(solution)/shard_map/ppermute | solution.py:103
  1030.9 104.8 %collective-permute-start.153 = (bf16[1024,2048]{1,0:T(8,128)(2,1)}, bf16[1024,2048]{1,0:T(8,128)(2,1)}, u32[]{:S(2)}, u32[]{:S(2)}) collective-permute-start(bf16[1024,2048]{1,0:T(8,128)(2,1)} %add_convert_fusion), channel_id=1, source_target_pairs={{0,8},{8,0},{1,9},{9,1},{2,10},{10,2},{3,11},{11,3},{4,12},{12,4},... | collective-permute-start | bytes 12582920 | tf_op jit(solution)/shard_map/ppermute | solution.py:397
  1069.9 80.2 %collective-permute-start.151 = (bf16[2048,1024]{1,0:T(8,128)(2,1)}, bf16[2048,1024]{1,0:T(8,128)(2,1)}, u32[]{:S(2)}, u32[]{:S(2)}) collective-permute-start(bf16[2048,1024]{1,0:T(8,128)(2,1)} %add_convert_fusion.1), channel_id=1, source_target_pairs={{0,8},{8,0},{1,9},{9,1},{2,10},{10,2},{3,11},{11,3},{4,12},{12,4},... | collective-permute-start | bytes 12582920 | tf_op jit(solution)/shard_map/ppermute | solution.py:397
  1069.9 80.2 %collective-permute-start.149 = (bf16[2048,1024]{1,0:T(8,128)(2,1)}, bf16[2048,1024]{1,0:T(8,128)(2,1)}, u32[]{:S(2)}, u32[]{:S(2)}) collective-permute-start(bf16[2048,1024]{1,0:T(8,128)(2,1)} %add_convert_fusion.2), channel_id=1, source_target_pairs={{0,8},{8,0},{1,9},{9,1},{2,10},{10,2},{3,11},{11,3},{4,12},{12,4},... | collective-permute-start | bytes 12582920 | tf_op jit(solution)/shard_map/ppermute | solution.py:397
  (301 other events, 5641.3 us)

commit v2 on v1

v2 whole, which is shorter than its diff:
```python
import functools
import math

import jax
import jax.numpy as jnp
from jax import lax
from jax.experimental import pallas as pl
from jax.experimental.pallas import tpu as pltpu
from jax.sharding import Mesh, PartitionSpec as P

HEADS = 16
CAP = 36
NORM_EPSILON = 1e-05
ROPE_BASE = 10000.0
ALL = ("x", "core", "z", "y")
SWAP = ((0, 1), (1, 0))
F32 = jnp.float32
BF16 = jnp.bfloat16


def turn(count, step):
    return tuple((i, (i + step) % count) for i in range(count))


def flip(count, bits):
    return tuple((i, i ^ bits) for i in range(count))


def after(values, *others):
    return lax.optimization_barrier((values,) + others)[0]


def mm(left, right):
    return jnp.dot(left, right, preferred_element_type=F32)


def mm_rows(left, right):
    return lax.dot_general(left, right, (((0,), (0,)), ((), ())), preferred_element_type=F32)


def mm_cols(left, right):
    return lax.dot_general(left, right, (((1,), (1,)), ((), ())), preferred_element_type=F32)


def unturn(items, index):
    count = len(items)
    if count == 1:
        return items
    placed = []
    for place in range(count):
        chosen = items[(0 - place) % count]
        for at in range(1, count):
            chosen = jnp.where(index == at, items[(at - place) % count], chosen)
        placed.append(chosen)
    return placed


def gather_ep(block, y_count, micro_count):
    by_z = {0: block}
    by_z[2] = lax.ppermute(block, "z", flip(4, 2))
    by_z[1] = lax.ppermute(block, "z", flip(4, 1))
    blocks = {}

    def along_y(a):
        blocks[a, 0] = by_z[a]
        for j in range(1, y_count):
            blocks[a, j] = lax.ppermute(by_z[a], "y", flip(y_count, j))

    along_y(0)
    by_z[3] = lax.ppermute(by_z[2], "z", flip(4, 1))
    for a in (1, 2, 3):
        along_y(a)
    rows = block.shape[0] // micro_count
    return jnp.concatenate(
        [
            blocks[a, j][m * rows : (m + 1) * rows]
            for m in range(micro_count)
            for a in range(4)
            for j in range(y_count)
        ],
        axis=0,
    )


def scatter_ep(part, y_count, micro_count):
    rows = part.shape[0] // (4 * y_count * micro_count)

    def piece(a, j):
        starts = [((m * 4 + a) * y_count + j) * rows for m in range(micro_count)]
        return jnp.concatenate([part[at : at + rows] for at in starts], axis=0)

    sums = {}

    def along_y(a):
        total = piece(a, 0).astype(F32)
        for j in range(1, y_count):
            arrived = lax.ppermute(piece(a, j).astype(BF16), "y", flip(y_count, j))
            total = total + arrived.astype(F32)
        sums[a] = total

    along_y(3)
    along_y(2)
    sums[2] = sums[2] + lax.ppermute(sums[3].astype(BF16), "z", flip(4, 1)).astype(F32)
    across = lax.ppermute(sums[2].astype(BF16), "z", flip(4, 2)).astype(F32)
    along_y(1)
    near = lax.ppermute(sums[1].astype(BF16), "z", flip(4, 1)).astype(F32)
    along_y(0)
    return sums[0] + near + across


def sum_ep(values, y_count, micro_count):
    shape = values.shape
    values = values.reshape(shape[0] * micro_count, 4, y_count, -1)

    def moved(source, axis, count, at, bits):
        arrived = lax.ppermute(source, axis, flip(count, bits))
        picked = [lax.index_in_dim(arrived, b ^ bits, at, keepdims=True) for b in range(count)]
        return jnp.concatenate(picked, axis=at)

    along = values
    for j in range(1, y_count):
        along = along + moved(values, "y", y_count, 2, j)
    total = along
    for a in (1, 2, 3):
        total = total + moved(along, "z", 4, 1, a)
    return total.reshape(shape)


def gather_grp(block, x_count):
    x_at, core = lax.axis_index("x"), lax.axis_index("core")
    mine = [block] + [lax.ppermute(block, "x", turn(x_count, i)) for i in range(1, x_count)]
    theirs = [lax.ppermute(item, "core", SWAP) for item in mine]
    mine, theirs = unturn(mine, x_at), unturn(theirs, x_at)
    stacked = []
    for own, other in zip(mine, theirs):
        stacked += [jnp.where(core == 0, own, other), jnp.where(core == 0, other, own)]
    return jnp.stack(stacked)


def keep_core(parts, x_count):
    core = lax.axis_index("core")
    parts = parts.reshape((x_count, 2) + parts.shape[1:])
    away = lax.dynamic_index_in_dim(parts, 1 - core, 1, keepdims=False).astype(BF16)
    kept = lax.dynamic_index_in_dim(parts, core, 1, keepdims=False)
    return kept + lax.ppermute(away, "core", SWAP).astype(F32)


def keep_x(kept, x_count):
    x_at = lax.axis_index("x")
    total = lax.dynamic_index_in_dim(kept, x_at, 0, keepdims=False)
    for i in range(1, x_count):
        away = lax.dynamic_index_in_dim(kept, (x_at - i) % x_count, 0, keepdims=False)
        total = total + lax.ppermute(away.astype(BF16), "x", turn(x_count, -i)).astype(F32)
    return total


def experts_kernel(count, which, hot_ref, router_ref, *refs):
    select, select_t, moe, cot = (refs[i * count : (i + 1) * count] for i in range(4))
    gate_ref, up_ref, down_ref = refs[4 * count : 4 * count + 3]
    rest = refs[4 * count + 3 :]
    grad_out, row_out = rest[:count], rest[count : 2 * count]
    rows_ref, cot_ref, act_ref, dgate_ref, dup_ref, logit_ref = rest[2 * count : 2 * count + 6]
    total_ref, back_ref, prob_ref, weight_ref, share_ref = rest[2 * count + 6 :]
    step = pl.program_id(0)
    slots = select[0].shape[1]

    @pl.when(step == 0)
    def _():
        for i in range(count):
            at = pl.ds(i * slots, slots)
            rows_ref[at, :] = mm(select[i][0], moe[i][...]).astype(BF16)
            cot_ref[at, :] = mm(select[i][0], cot[i][...]).astype(BF16)
        logits = mm(rows_ref[...], router_ref[...])
        lane = lax.broadcasted_iota(jnp.int32, logits.shape, 1)
        logits = jnp.where(lane < which, logits, -1e30)
        logits = jnp.exp(logits - jnp.max(logits, axis=1, keepdims=True))
        prob = logits / jnp.sum(logits, axis=1, keepdims=True)
        prob_ref[...] = prob
        weight = jnp.sum(prob * hot_ref[...], axis=1, keepdims=True)
        weight_ref[...] = jnp.broadcast_to(weight, weight_ref.shape)
        share_ref[...] = jnp.zeros_like(share_ref)

    weight = weight_ref[:, :1]
    gate_w, up_w, down_w = gate_ref[0], up_ref[0], down_ref[0]
    gate = mm(rows_ref[...], gate_w)
    up = mm(rows_ref[...], up_w)
    sigmoid = jax.nn.sigmoid(gate)
    silu = gate * sigmoid
    active = silu * up
    act = (weight * active).astype(BF16)
    act_ref[...] = act
    grad = mm_cols(cot_ref[...], down_w)
    share_ref[...] += jnp.broadcast_to(
        jnp.sum(active * grad, axis=1, keepdims=True), share_ref.shape
    )
    grad = weight * grad
    dup = (grad * silu).astype(BF16)
    dgate = (grad * up * (sigmoid + silu * (1.0 - sigmoid))).astype(BF16)
    dup_ref[...] = dup
    dgate_ref[...] = dgate
    weighted = mm(act, down_w)
    back = mm_cols(dgate, gate_w) + mm_cols(dup, up_w)

    @pl.when(step == 0)
    def _():
        total_ref[...] = weighted
        back_ref[...] = back

    @pl.when(step > 0)
    def _():
        total_ref[...] += weighted
        back_ref[...] += back

    @pl.when(step == pl.num_programs(0) - 1)
    def _():
        logit = (share_ref[...] * weight_ref[...] * (hot_ref[...] - prob_ref[...])).astype(BF16)
        logit_ref[...] = logit
        for i in range(count):
            at = pl.ds(i * slots, slots)
            back = (back_ref[at, :] + mm_cols(logit_ref[at, :], router_ref[...])).astype(BF16)
            grad_out[i][...] = mm(select_t[i][0], back).astype(BF16)
            row_out[i][...] = mm(select_t[i][0], total_ref[at, :].astype(BF16)).astype(BF16)


def run_experts(
    sets, at, hot, router, select, select_t, micro, moe, cot, w_gate, w_up, w_down, experts, hidden
):
    count, (slots, seq_len), width = len(sets), select.shape[1:], router.shape[0]
    block = 256
    steps, rows = hidden // block, count * slots

    def whole(array):
        return pl.BlockSpec(
            array.shape, lambda f, at: (0,) * array.ndim, pipeline_mode=pl.Buffered(1)
        )

    def kept(shape):
        return pl.BlockSpec(shape, lambda f, at: (0, 0))

    wide = pl.BlockSpec((1, width, block), lambda f, at: (at[0], 0, at[1] + f))
    tall = pl.BlockSpec((1, block, width), lambda f, at: (at[0], at[1] + f, 0))
    hidden_rows = pl.BlockSpec((rows, block), lambda f, at: (0, f))
    one_micro = pl.BlockSpec(
        (seq_len, width), lambda f, at: (micro, 0), pipeline_mode=pl.Buffered(1)
    )
    tables = [array for array in (select, select_t) for _ in sets]
    table_specs = [
        pl.BlockSpec(
            (1,) + array.shape[1:],
            functools.partial(lambda one, f, at: (one, 0, 0), one),
            pipeline_mode=pl.Buffered(1),
        )
        for array in (select, select_t)
        for one in sets
    ]
    one_micro = pl.BlockSpec(
        (seq_len, width), lambda f, at: (micro, 0), pipeline_mode=pl.Buffered(1)
    )
    tables = [array for array in (select, select_t) for _ in sets]
    table_specs = [
        pl.BlockSpec(
            (1,) + array.shape[1:],
            functools.partial(lambda one, f, at: (one, 0, 0), one),
            pipeline_mode=pl.Buffered(1),
        )
        for array in (select, select_t)
        for one in sets
    ]
    tokens = jax.ShapeDtypeStruct((seq_len, width), BF16)
    gathered = jax.ShapeDtypeStruct((rows, width), BF16)
    inner = jax.ShapeDtypeStruct((rows, hidden), BF16)
    result = pl.pallas_call(
        lambda at, *refs: experts_kernel(count, experts, *refs),
        grid_spec=pltpu.PrefetchScalarGridSpec(
            num_scalar_prefetch=1,
            grid=(steps,),
            in_specs=[whole(hot), whole(router)]
            + table_specs
            + [one_micro] * (2 * count)
            + [wide, wide, tall],
            out_specs=[kept((seq_len, width))] * (2 * count)
            + [kept((rows, width))] * 2
            + [hidden_rows] * 3
            + [kept((rows, 128))],
            scratch_shapes=[pltpu.VMEM((rows, width), F32)] * 2
            + [pltpu.VMEM((rows, 128), F32)] * 3,
        ),
        out_shape=[tokens] * (2 * count)
        + [gathered] * 2
        + [inner] * 3
        + [jax.ShapeDtypeStruct((rows, 128), BF16)],
        compiler_params=pltpu.CompilerParams(
            dimension_semantics=("arbitrary",), vmem_limit_bytes=60 * 2**20
        ),
        cost_estimate=pl.CostEstimate(
            flops=12 * rows * hidden * width + 8 * rows * seq_len * width,
            bytes_accessed=6 * hidden * width + 16 * seq_len * width + 8 * rows * width,
            transcendentals=rows * hidden,
        ),
        name="experts",
    )(at, hot, router, *tables, *moe, *cot, w_gate, w_up, w_down)
    return result[:count], result[count : 2 * count], result[2 * count :]


def norm_scale(values):
    return lax.rsqrt(jnp.mean(values * values, axis=-1, keepdims=True) + NORM_EPSILON)


def make_per_device(x_count, z_count, y_count):
    group_size = z_count * y_count
    grp_size = 2 * x_count

    assert z_count == 4

    def per_device(
        tokens,
        routes,
        attn_gain,
        w_query,
        w_key,
        w_value,
        query_gain,
        key_gain,
        w_out,
        moe_gain,
        w_router,
        w_gate,
        w_up,
        w_down,
        cotangent,
    ):
        micro_count, seq_parts, row_count, width = tokens.shape
        top_count = routes.shape[3]
        tokens = tokens.reshape(micro_count, row_count, width)
        routes = routes.reshape(micro_count, row_count, top_count)
        cotangent = cotangent.reshape(micro_count, row_count, width)
        expert_count = w_router.shape[1]
        seq_len = row_count * group_size
        head_dim = width // HEADS
        half = head_dim // 2
        score_scale = 1.0 / math.sqrt(head_dim)
        weight_rows = w_query.shape[0]
        pieces = head_dim // weight_rows
        heads_here = grp_size // pieces
        head_sets = group_size // pieces
        local_width = heads_here * head_dim
        x_at, core = lax.axis_index("x"), lax.axis_index("core")
        z_at, y_at = lax.axis_index("z"), lax.axis_index("y")
        ep_at = z_at * y_count + y_at
        set_at, piece_at = ep_at // pieces, ep_at % pieces
        slots = CAP * group_size
        local_experts = w_gate.shape[0]
        ff_width = w_gate.shape[2]

        def gather(block):
            return gather_ep(block.reshape(-1, width), y_count, micro_count)

        def scatter(part):
            return scatter_ep(part, y_count, micro_count)

        def by_owner(weight):
            shaped = weight.reshape(weight_rows, pieces, heads_here, head_sets, head_dim)
            return shaped.transpose(3, 1, 0, 2, 4).reshape(group_size, weight_rows, local_width)

        qkv = jnp.concatenate([by_owner(w) for w in (w_query, w_key, w_value)], axis=2)
        qkv = lax.all_to_all(qkv, ("z", "y"), split_axis=0, concat_axis=0, tiled=True)
        small = jnp.concatenate(
            [w_router]
            + [g[:, None] for g in (attn_gain, query_gain, key_gain, moe_gain)],
            axis=1,
        ).reshape(-1)
        naming = jnp.any(
            routes.reshape(1, -1, top_count)
            == jnp.arange(expert_count, dtype=jnp.int32)[:, None, None],
            axis=-1,
        ).astype(BF16)
        if local_experts == 2:
            naming = naming.reshape(group_size, 2, -1).transpose(1, 0, 2)
        else:
            assert local_experts == 1
            naming = jnp.broadcast_to(naming[None], (2,) + naming.shape)
        device_count = grp_size * group_size
        naming = jnp.broadcast_to(naming[None], (x_count,) + naming.shape).reshape(device_count, -1)
        small = jnp.concatenate(
            [jnp.broadcast_to(small[None], (device_count, small.shape[0])), naming], axis=1
        )
        small = lax.all_to_all(after(small, qkv), ALL, split_axis=0, concat_axis=0, tiled=True)
        named = small[:, -micro_count * row_count :]
        small = small[:, : -micro_count * row_count].reshape(width, expert_count + 4)
        full_router = small[:, :expert_count]
        gains = small[:, expert_count:].astype(F32).T
        gain_attn, gain_query, gain_key, gain_moe = gains[0:1], gains[1], gains[2], gains[3:4]

        def head_part(vector):
            shaped = vector.reshape(pieces, heads_here, head_sets, head_dim)
            shaped = lax.dynamic_index_in_dim(shaped, piece_at, 0, keepdims=False)
            return lax.dynamic_index_in_dim(shaped, set_at, 1, keepdims=False).reshape(1, -1)

        def head_part_back(vector):
            piece_hot = jnp.arange(pieces) == piece_at
            set_hot = jnp.arange(head_sets) == set_at
            hot = piece_hot[:, None, None, None] & set_hot[None, None, :, None]
            return jnp.where(hot, vector.reshape(1, heads_here, 1, head_dim), 0.0).reshape(-1)

        gain_query, gain_key = head_part(gain_query), head_part(gain_key)

        sent_qkv = qkv
        qkv = gather_grp(qkv.reshape(group_size * weight_rows, 3 * local_width), x_count)
        qkv = qkv.reshape(width, 3 * local_width)
        out_pairs = []
        for s in range(head_sets):
            for t in range(pieces):
                for h in range(heads_here):
                    for p in range(pieces):
                        home = (t * heads_here + h) * group_size + s * pieces + p
                        user = (h * pieces + p) * group_size + s * pieces + t
                        out_pairs.append((home, user))
        out_here = lax.ppermute(w_out, ALL, out_pairs)
        out_here = gather_grp(out_here, x_count).reshape(local_width, width)

        z_from = z_at ^ jnp.arange(z_count, dtype=jnp.int32)
        y_from = y_at ^ jnp.arange(y_count, dtype=jnp.int32)
        block_from = z_from[:, None] * y_count + y_from[None, :]
        positions = (
            block_from.reshape(-1)[:, None] * row_count
            + jnp.arange(row_count, dtype=jnp.int32)[None, :]
        ).reshape(-1)
        frequency = jnp.exp(
            -math.log(ROPE_BASE) * jnp.arange(half, dtype=F32) * 2.0 / head_dim
        )
        angles = positions.astype(F32)[:, None] * frequency[None, :]
        cosine, sine = jnp.cos(angles), jnp.sin(angles)
        cos_both = jnp.concatenate([cosine, cosine], axis=1)
        sin_both = jnp.concatenate([-sine, sine], axis=1)
        allowed = positions[:, None] >= positions[None, :]

        def halves_swapped(values):
            parts = []
            for h in range(heads_here):
                at = h * head_dim
                parts += [values[:, at + half : at + head_dim], values[:, at : at + half]]
            return jnp.concatenate(parts, axis=1)

        wide_cos = jnp.tile(cos_both, (micro_count, heads_here))
        wide_sin = jnp.tile(sin_both, (micro_count, heads_here))

        def rope(values):
            return values * wide_cos + halves_swapped(values) * wide_sin

        def rope_back(values):
            return values * wide_cos - halves_swapped(values) * wide_sin

        if local_experts == 2:
            expert_at, hidden = ep_at * 2 + core, ff_width
            expert_place = jnp.stack([core, 0 * core]).astype(jnp.int32)
        else:
            expert_at, hidden = ep_at, ff_width // 2
            expert_place = jnp.stack([0 * core, core * (hidden // 256)]).astype(jnp.int32)
        hot = (jnp.arange(128, dtype=jnp.int32) == expert_at).astype(F32)[None]
        padded_router = jnp.pad(full_router, ((0, 0), (0, 128 - expert_count)))

        named = named.reshape((x_count, 2, z_count, y_count, micro_count, row_count))
        named = lax.dynamic_index_in_dim(named, x_at, 0, keepdims=False)
        named = jnp.where(core == 0, named, named[::-1])
        named = jnp.take(jnp.take(named, z_from, axis=1), y_from, axis=2)
        named = named.transpose(3, 0, 1, 2, 4).reshape(2 * micro_count, seq_len) > 0.5
        earlier = jnp.arange(seq_len)[:, None] < jnp.arange(seq_len)[None, :]
        rank = mm(named.astype(BF16), earlier.astype(BF16)).astype(jnp.int32)
        rank = jnp.where(named, rank, -1)
        slot_ids = jnp.arange(slots, dtype=jnp.int32)
        select = (rank[:, None, :] == slot_ids[None, :, None]).astype(BF16)
        select_t = (rank[:, :, None] == slot_ids[None, None, :]).astype(BF16)

        def micro_rows(m):
            return slice(m * seq_len, (m + 1) * seq_len)

        def head_cols(h):
            return slice(h * head_dim, (h + 1) * head_dim)

        own = tokens.reshape(-1, width).astype(F32)
        micros = range(micro_count)
        rows = gather(tokens)
        low_rows = rows
        rows = rows.astype(F32)
        row_scale = norm_scale(rows)
        normed = (rows * row_scale * gain_attn).astype(BF16)
        raw = mm(normed, qkv)
        query_raw, key_raw = raw[:, :local_width], raw[:, local_width : 2 * local_width]
        value = raw[:, 2 * local_width :].astype(BF16)
        squares = jnp.stack(
            [jnp.sum(query_raw * query_raw, axis=1), jnp.sum(key_raw * key_raw, axis=1)]
        )
        squares = sum_ep(squares, y_count, micro_count)
        cot_all = [gather(after(cotangent, low_rows))]
        scales = lax.rsqrt(squares / width + NORM_EPSILON)
        query_scale, key_scale = scales[0][:, None], scales[1][:, None]
        query = rope(query_raw * query_scale * gain_query).astype(BF16)
        key = rope(key_raw * key_scale * gain_key).astype(BF16)
        probs, attended = {}, []
        for m in range(micro_count):
            here = []
            for h in range(heads_here):
                at = micro_rows(m), head_cols(h)
                scores = mm_cols(query[at], key[at]) * score_scale
                scores = jnp.where(allowed, scores, -1e30)
                scores = jnp.exp(scores - jnp.max(scores, axis=-1, keepdims=True))
                prob = scores / jnp.sum(scores, axis=-1, keepdims=True)
                probs[m, h] = prob
                here.append(mm(prob.astype(BF16), value[at]).astype(BF16))
            attended.append(jnp.concatenate(here, axis=1))
        attended = jnp.concatenate(attended, axis=0)
        resid_mid = own + scatter(mm(attended, out_here).astype(BF16))

        def with_other_core(parts):
            arrived = [lax.ppermute(p[1], "core", SWAP) for p in parts]
            return jnp.concatenate(
                [
                    (p[0].astype(F32) + other.astype(F32)).astype(BF16)
                    for p, other in zip(parts, arrived)
                ],
                axis=0,
            )

        moe_scale = norm_scale(resid_mid)
        moe_all = [gather((resid_mid * moe_scale * gain_moe).astype(BF16))]
        moe_all.append(lax.ppermute(moe_all[0], "core", SWAP))
        cot_all.append(lax.ppermute(cot_all[0], "core", SWAP))
        saved, out_parts, grad_parts = [], [], []
        for m in micros:
            sets = [slice(0, 2)] if slots <= 288 else [slice(0, 1), slice(1, 2)]
            grads, outs = [], []
            for here in sets:
                grad, out, rest = run_experts(
                    range(2 * m, 2 * m + 2)[here],
                    expert_place,
                    hot,
                    padded_router,
                    select,
                    select_t,
                    m,
                    moe_all[here],
                    cot_all[here],
                    w_gate,
                    w_up,
                    w_down,
                    expert_count,
                    hidden,
                )
                grads, outs = grads + list(grad), outs + list(out)
                saved.append(rest)
            grad_parts.append(grads)
            out_parts.append(outs)
        grad_sum = with_other_core(grad_parts)
        grad_moe_in = scatter(grad_sum)

        def over_pairs(left, right):
            total = None
            for rest in saved:
                term = mm_rows(rest[left], rest[right])
                total = term if total is None else total + term
            return total

        def halves(part):
            middle = part.shape[0] // 2
            return [part[:middle], part[middle:]]

        def over_x(low, start=None):
            sent = low if start is None else after(low, start)
            return [low] + [
                lax.ppermute(sent, "x", turn(x_count, i)) for i in range(1, x_count)
            ]

        def summed(parts, start):
            parts = [parts[0]] + [after(p, start) for p in parts[1:]]
            if x_count > 2:
                parts = unturn(parts, x_at)
            total = parts[0].astype(F32)
            for item in parts[1:]:
                total = total + item.astype(F32)
            return total.astype(BF16)

        def both_cores(sums, axis):
            first, second = [], []
            for own_part in sums:
                other = lax.ppermute(own_part, "core", SWAP)
                first.append(jnp.where(core == 0, own_part, other))
                second.append(jnp.where(core == 0, other, own_part))
            first, second = jnp.concatenate(first), jnp.concatenate(second)
            if local_experts == 2:
                return jnp.stack([first, second]).astype(F32)
            return jnp.concatenate([first, second], axis=axis)[None].astype(F32)

        down_low = over_pairs(2, 1).astype(BF16)
        saved = [[after(r, grad_sum) for r in rest] for rest in saved]
        gate_low = over_pairs(0, 3).astype(BF16)
        up_low = over_pairs(0, 4).astype(BF16)
        router_grad = over_pairs(0, 5)[:, :expert_count]
        down_parts = [over_x(p) for p in halves(down_low)]
        gate_parts = [over_x(p) for p in halves(gate_low)]
        up_first, up_second = halves(up_low)

        grad_out = cotangent.reshape(-1, width).astype(F32)
        moe_gain_grad = jnp.sum(grad_moe_in * resid_mid * moe_scale, axis=0)
        inner = grad_moe_in * gain_moe
        grad_mid = (
            grad_out
            + moe_scale * inner
            - resid_mid * (moe_scale**3 * jnp.mean(resid_mid * inner, axis=-1, keepdims=True))
        )
        grad_attn = gather(grad_mid.astype(BF16))
        mixture = scatter(with_other_core([after(p, grad_attn) for p in out_parts]))
        block_out = (resid_mid + mixture).astype(BF16)
        grad_attended = mm_cols(grad_attn, out_here).astype(BF16)
        down_sums = [summed(down_parts[0], grad_moe_in), summed(down_parts[1], grad_attn)]
        up_parts = [over_x(up_first)]
        grad_query, grad_key, grad_value = [], [], []
        for m in range(micro_count):
            query_here, key_here, value_here = [], [], []
            for h in range(heads_here):
                at = micro_rows(m), head_cols(h)
                prob = probs[m, h]
                value_here.append(mm_rows(prob.astype(BF16), grad_attended[at]).astype(BF16))
                grad_pa = mm_cols(grad_attended[at], value[at])
                delta = jnp.sum(prob * grad_pa, axis=-1, keepdims=True)
                grad_scores = (prob * (grad_pa - delta)).astype(BF16)
                query_here.append(mm(grad_scores, key[at]) * score_scale)
                key_here.append(mm_rows(grad_scores, query[at]) * score_scale)
            grad_query.append(jnp.concatenate(query_here, axis=1))
            grad_key.append(jnp.concatenate(key_here, axis=1))
            grad_value.append(jnp.concatenate(value_here, axis=1))
        grad_query = rope_back(jnp.concatenate(grad_query, axis=0))
        grad_key = rope_back(jnp.concatenate(grad_key, axis=0))
        grad_value = jnp.concatenate(grad_value, axis=0)
        inner_query, inner_key = grad_query * gain_query, grad_key * gain_key
        query_gain_grad = jnp.sum(grad_query * query_raw * query_scale, axis=0)
        key_gain_grad = jnp.sum(grad_key * key_raw * key_scale, axis=0)
        means = jnp.stack(
            [jnp.sum(inner_query * query_raw, axis=1), jnp.sum(inner_key * key_raw, axis=1)]
        )
        means = sum_ep(means, y_count, micro_count) / width
        query_back = (
            query_scale * inner_query - query_raw * (query_scale**3 * means[0][:, None])
        ).astype(BF16)
        key_back = (
            key_scale * inner_key - key_raw * (key_scale**3 * means[1][:, None])
        ).astype(BF16)
        raw_grad = jnp.concatenate([query_back, key_back, grad_value], axis=1)
        d_down = both_cores(down_sums, 0)
        normed_part = mm_cols(after(raw_grad, d_down), qkv)
        attn_gain_grad = jnp.sum(normed_part * rows * row_scale, axis=0)
        grad_normed = scatter(normed_part.astype(BF16))
        in_scale = norm_scale(own)
        inner = grad_normed * gain_attn
        d_tokens = (
            grad_mid
            + in_scale * inner
            - own * (in_scale**3 * jnp.mean(own * inner, axis=-1, keepdims=True))
        )

        qkv_grad = mm_rows(normed, raw_grad)
        qkv_kept = keep_core(qkv_grad.reshape(grp_size, -1, 3 * local_width), x_count)
        up_parts.append(over_x(up_second, qkv_kept))
        qkv_grad = keep_x(qkv_kept, x_count)
        gate_sums = [summed(gate_parts[0], raw_grad), summed(gate_parts[1], grad_normed)]
        d_gate = both_cores(gate_sums, 1)
        qkv_grad = after(qkv_grad, d_gate, block_out)
        up_sums = [summed(up_parts[0], grad_normed), summed(up_parts[1], d_gate)]
        d_up = both_cores(up_sums, 1)
        qkv_grad = qkv_grad.astype(BF16).reshape(group_size, weight_rows, 3 * local_width)
        qkv_grad = lax.all_to_all(
            qkv_grad, ("z", "y"), split_axis=0, concat_axis=0, tiled=True
        ).astype(F32)

        def by_row(grads):
            shaped = grads.reshape(head_sets, pieces, weight_rows, heads_here, head_dim)
            return shaped.transpose(2, 1, 3, 0, 4).reshape(weight_rows, width)

        d_query = by_row(qkv_grad[:, :, :local_width])
        d_key = by_row(qkv_grad[:, :, local_width : 2 * local_width])
        d_value = by_row(qkv_grad[:, :, 2 * local_width :])
        out_grad = mm_rows(attended, grad_attn)
        out_grad = keep_x(keep_core(out_grad.reshape(grp_size, weight_rows, width), x_count), x_count)
        d_out = lax.ppermute(
            out_grad.astype(BF16), ALL, [(user, home) for home, user in out_pairs]
        ).astype(F32)

        vectors = jnp.stack(
            [
                attn_gain_grad,
                head_part_back(query_gain_grad),
                head_part_back(key_gain_grad),
                moe_gain_grad,
            ]
        )
        vectors = vectors.reshape(4, device_count, weight_rows).transpose(1, 0, 2)
        small_grads = jnp.concatenate(
            [
                vectors.reshape(device_count, 4 * weight_rows),
                router_grad.reshape(device_count, weight_rows * expert_count),
            ],
            axis=1,
        )
        small_grads = lax.all_to_all(
            after(small_grads, grad_normed, gate_sums), ALL, split_axis=0, concat_axis=0, tiled=True
        )
        small_grads = jnp.sum(small_grads, axis=0)
        gain_grads = small_grads[: 4 * weight_rows].reshape(4, weight_rows)
        d_router = small_grads[4 * weight_rows :].reshape(weight_rows, expert_count)

        shape = (micro_count, seq_parts, row_count, width)
        return (
            block_out.reshape(shape),
            d_tokens.reshape(shape),
            gain_grads[0],
            d_query,
            d_key,
            d_value,
            gain_grads[1],
            gain_grads[2],
            d_out,
            gain_grads[3],
            d_router,
            d_gate,
            d_up,
            d_down,
        )

    return per_device


def solution(mesh):
    devices = mesh.devices
    x_count, y_count, z_count = (
        len({device.coords[axis] for device in devices.flat}) for axis in range(3)
    )
    fine = Mesh(devices.reshape(x_count, 2, z_count, y_count), ALL)
    grp, ep = ("x", "core"), ("z", "y")
    by_token = P(None, grp, ep, None)
    vector, matrix, expert = P(ALL), P(ALL, None), P(ep, None, None)
    return jax.shard_map(
        make_per_device(x_count, z_count, y_count),
        mesh=fine,
        in_specs=(
            by_token,
            by_token,
            vector,
            matrix,
            matrix,
            matrix,
            vector,
            vector,
            matrix,
            vector,
            matrix,
            expert,
            expert,
            expert,
            by_token,
        ),
        out_specs=(
            by_token,
            by_token,
            vector,
            matrix,
            matrix,
            matrix,
            vector,
            vector,
            matrix,
            vector,
            matrix,
            expert,
            expert,
            expert,
        ),
        check_vma=False,
    )
```

time: 1190 us -> 849 us (0.71)
  starting transfers between devices: 276 us -> 115 us
  blocking collectives: 121 us -> 0 us
  waiting for transfers between devices: 396 us -> 297 us
  matrix products: 178 us -> 79.9 us
  Pallas kernels: 0 us -> 79.3 us
  local copies, waits for them, and re-layouts: 80.3 us -> 110 us
  other arithmetic: 125 us -> 150 us
    ppermute x142 -> x84, starting transfers between devices: 246 us -> 89.2 us  [the longest x16 17.4 us: along_y(): arrived = lax.ppermute(piece(a, j).astype(BF16), 'y', flip(y_count, j))]
    all_gather x2 -> x0, blocking collectives: 121 us -> none  [the longest x1 66.4 us: per_device(): small = lax.all_gather(small, ALL, axis=0, tiled=True)]
    pallas_call x0 -> x2, Pallas kernels: none -> 79.3 us  [run_experts(): pl.pallas_call(lambda at, *refs: experts_kernel(count, experts, *refs), g...]
    dot_general x22 -> x10, matrix products: 65.4 us -> 15.7 us  [mm_cols(): lax.dot_general(left, right, (((1,), (1,)), ((), ())), preferred_element_...]
    dot_general x31 -> x11, matrix products: 57 us -> 15.8 us  [mm(): return jnp.dot(left, right, preferred_element_type=F32)]
    all_to_all x1 -> x2, waiting for transfers between devices: 44.3 us -> 4.04 us  [the longest x1 4.04 us: per_device(): lax.all_to_all(after(small, qkv), ALL, split_axis=0, concat_axis=0, tiled...]
    ppermute x142 -> x84, waiting for transfers between devices: 325 us -> 287 us  [the longest x16 62.4 us: along_y(): arrived = lax.ppermute(piece(a, j).astype(BF16), 'y', flip(y_count, j))]
    select_n x1 -> x6, other arithmetic: 0.01 us -> 15 us  [both_cores(): first.append(jnp.where(core == 0, own_part, other))]
  transfers between devices with their start and end apart: 157 -> 98, of which waited for: 74 -> 37; matrix products, arithmetic and copies ran while one was open for 22% -> 37% of each run, Pallas kernels for 0% -> 5%
where the time goes in v2:
time: 849 us; the launch traced here: 835 us
  waiting for transfers between devices  297 us (35%)
  other arithmetic  150 us (18%)
  starting transfers between devices  115 us (14%)
  local copies, waits for them, and re-layouts  110 us (13%)
  matrix products  79.9 us (9%)
  Pallas kernels  79.3 us (9%)
    pallas_call x2, Pallas kernels, run_experts(): pl.pallas_call(lambda at, *refs: experts_kernel(count, experts, *refs), g...  79.3 us
    ppermute x16, waiting for transfers between devices, along_y(): arrived = lax.ppermute(piece(a, j).astype(BF16), 'y', flip(y_count, j))  62.4 us
    unnamed x333, local copies, waits for them, and re-layouts  59.8 us
    ppermute x4, waiting for transfers between devices, gather_ep(): by_z[2] = lax.ppermute(block, 'z', flip(4, 2))  55.5 us
    dot_general x18, matrix products, mm_rows(): lax.dot_general(left, right, (((0,), (0,)), ((), ())), preferred_element_...  48.5 us
    ppermute x16, waiting for transfers between devices, along_y(): blocks[a, j] = lax.ppermute(by_z[a], 'y', flip(y_count, j))  48.3 us
    ppermute x4, waiting for transfers between devices, scatter_ep(): near = lax.ppermute(sums[1].astype(BF16), 'z', flip(4, 1)).astype(F32)  36.6 us
    convert_element_type x3, other arithmetic, both_cores(): return jnp.stack([first, second]).astype(F32)  31 us
  transfers between devices with their start and end apart: 98, of which 37 were waited for; matrix products, arithmetic and copies ran while one was open for 37% of the time, Pallas kernels for 5%

profile of v2, /device:TPU:0, one launch (start us, length us, event | category | flops | bytes accessed | tf_op | source)
XLA Modules:
  0.0 835.1 jit_solution(7968790628026969077)
XLA Ops:
  41.6 11.0 %collective-permute-done.5 = bf16[128,2048]{1,0:T(8,128)(2,1)} collective-permute-done((bf16[128,2048]{1,0:T(8,128)(2,1)S(1)}, bf16[128,2048]{1,0:T(8,128)(2,1)}, u32[]{:S(2)}, u32[]{:S(2)}) %collective-permute-start.5) | collective-permute-done | bytes 524320 | tf_op jit(solution)/shard_map/ppermute | solution.py:70
  52.9 7.7 collective-permute-done.2
  65.6 6.6 all-to-all-start.1
  101.5 23.8 %collective-permute-done.36 = bf16[128,2048]{1,0:T(8,128)(2,1)} collective-permute-done((bf16[128,2048]{1,0:T(8,128)(2,1)S(1)}, bf16[128,2048]{1,0:T(8,128)(2,1)}, u32[]{:S(2)}, u32[]{:S(2)}) %collective-permute-start.36) | collective-permute-done | bytes 524320 | tf_op jit(solution)/shard_map/ppermute | solution.py:60
  128.9 8.4 %collective-permute-done.38 = bf16[128,2048]{1,0:T(8,128)(2,1)} collective-permute-done((bf16[128,2048]{1,0:T(8,128)(2,1)}, bf16[128,2048]{1,0:T(8,128)(2,1)}, u32[]{:S(2)}, u32[]{:S(2)}) %collective-permute-start.38) | collective-permute-done | bytes 524320 | tf_op jit(solution)/shard_map/ppermute | solution.py:70
  137.8 13.9 %collective-permute-done.35 = bf16[128,2048]{1,0:T(8,128)(2,1)S(1)} collective-permute-done((bf16[128,2048]{1,0:T(8,128)(2,1)S(1)}, bf16[128,2048]{1,0:T(8,128)(2,1)S(1)}, u32[]{:S(2)}, u32[]{:S(2)}) %collective-permute-start.35) | collective-permute-done | bytes 524320 | tf_op jit(solution)/shard_map/ppermute | solution.py:67
  155.4 8.2 fusion.129
  206.3 17.3 %collective-permute-done.19 = bf16[128,2048]{1,0:T(8,128)(2,1)S(1)} collective-permute-done((bf16[128,2048]{1,0:T(8,128)(2,1)S(1)}, bf16[128,2048]{1,0:T(8,128)(2,1)S(1)}, u32[]{:S(2)}, u32[]{:S(2)}) %collective-permute-start.19) | collective-permute-done | bytes 524320 | tf_op jit(solution)/shard_map/ppermute | solution.py:97
  229.9 17.3 %collective-permute-done.20 = bf16[128,2048]{1,0:T(8,128)(2,1)S(1)} collective-permute-done((bf16[128,2048]{1,0:T(8,128)(2,1)S(1)}, bf16[128,2048]{1,0:T(8,128)(2,1)S(1)}, u32[]{:S(2)}, u32[]{:S(2)}) %collective-permute-start.20) | collective-permute-done | bytes 524320 | tf_op jit(solution)/shard_map/ppermute | solution.py:106
  253.9 13.7 %collective-permute-done.28 = bf16[128,2048]{1,0:T(8,128)(2,1)S(1)} collective-permute-done((bf16[128,2048]{1,0:T(8,128)(2,1)S(1)}, bf16[128,2048]{1,0:T(8,128)(2,1)S(1)}, u32[]{:S(2)}, u32[]{:S(2)}) %collective-permute-start.28) | collective-permute-done | bytes 524320 | tf_op jit(solution)/shard_map/ppermute | solution.py:60
  279.9 8.2 collective-permute-done.27
  308.2 40.0 %experts.3 = (bf16[512,2048]{1,0:T(8,128)(2,1)}, bf16[512,2048]{1,0:T(8,128)(2,1)}, bf16[512,2048]{1,0:T(8,128)(2,1)}, bf16[512,2048]{1,0:T(8,128)(2,1)}, bf16[5...) custom-call(s32[2]{0:T(128)} %pad_add_fusion.at, ...), custom_call_target="tpu_custom_call" | custom-call | flops 19327352832 | bytes 38797312 | tf_op jit(solution)/shard_map/experts/pallas_call | solution.py:272
  348.7 39.3 %experts.2 = (bf16[512,2048]{1,0:T(8,128)(2,1)}, bf16[512,2048]{1,0:T(8,128)(2,1)}, bf16[512,2048]{1,0:T(8,128)(2,1)}, bf16[512,2048]{1,0:T(8,128)(2,1)}, bf16[5...) custom-call(s32[2]{0:T(128)} %pad_add_fusion.at, ...), custom_call_target="tpu_custom_call" | custom-call | flops 19327352832 | bytes 38797312 | tf_op jit(solution)/shard_map/experts/pallas_call | solution.py:272
  425.1 8.1 add_convert_fusion
  435.4 6.9 collective-permute-done.44
  444.9 9.5 %collective-permute-done.48 = bf16[128,2048]{1,0:T(8,128)(2,1)S(1)} collective-permute-done((bf16[128,2048]{1,0:T(8,128)(2,1)S(1)}, bf16[128,2048]{1,0:T(8,128)(2,1)S(1)}, u32[]{:S(2)}, u32[]{:S(2)}) %collective-permute-start.48) | collective-permute-done | bytes 524320 | tf_op jit(solution)/shard_map/ppermute | solution.py:103
  455.4 9.3 %collective-permute-done.45 = bf16[128,2048]{1,0:T(8,128)(2,1)S(1)} collective-permute-done((bf16[128,2048]{1,0:T(8,128)(2,1)S(1)}, bf16[128,2048]{1,0:T(8,128)(2,1)S(1)}, u32[]{:S(2)}, u32[]{:S(2)}) %collective-permute-start.45) | collective-permute-done | bytes 524320 | tf_op jit(solution)/shard_map/ppermute | solution.py:106
  464.7 10.6 %collective-permute-done.49 = bf16[128,2048]{1,0:T(8,128)(2,1)S(1)} collective-permute-done((bf16[128,2048]{1,0:T(8,128)(2,1)S(1)}, bf16[128,2048]{1,0:T(8,128)(2,1)S(1)}, u32[]{:S(2)}, u32[]{:S(2)}) %collective-permute-start.49) | collective-permute-done | bytes 524320 | tf_op jit(solution)/shard_map/ppermute | solution.py:104
  483.7 14.3 %collective-permute-done.53 = bf16[128,2048]{1,0:T(8,128)(2,1)S(1)} collective-permute-done((bf16[128,2048]{1,0:T(8,128)(2,1)S(1)}, bf16[128,2048]{1,0:T(8,128)(2,1)S(1)}, u32[]{:S(2)}, u32[]{:S(2)}) %collective-permute-start.53) | collective-permute-done | bytes 524320 | tf_op jit(solution)/shard_map/ppermute | solution.py:60
  510.6 10.4 %collective-permute-done.52 = bf16[128,2048]{1,0:T(8,128)(2,1)S(1)} collective-permute-done((bf16[128,2048]{1,0:T(8,128)(2,1)S(1)}, bf16[128,2048]{1,0:T(8,128)(2,1)S(1)}, u32[]{:S(2)}, u32[]{:S(2)}) %collective-permute-start.52) | collective-permute-done | bytes 524320 | tf_op jit(solution)/shard_map/ppermute | solution.py:67
  614.5 10.8 %maximum_convert_fusion = f32[2,1024,2048]{2,1,0:T(8,128)} fusion(bf16[1,1024,2048]{2,1,0:T(8,128)(2,1)} %maximum_bitcast_fusion.1, bf16[1,1024,2048]{2,1,0:T(8,128)(2,1)} %maximum_bitcast_fusion), kind=kLoop, calls=%fused_computation.10 | loop fusion | flops 8388608 | bytes 25165824 | tf_op jit(solution)/shard_map/convert_element_type | solution.py:590
  625.3 7.4 fusion.4
  652.6 18.1 %collective-permute-done.75 = bf16[128,2048]{1,0:T(8,128)(2,1)} collective-permute-done((bf16[128,2048]{1,0:T(8,128)(2,1)}, bf16[128,2048]{1,0:T(8,128)(2,1)}, u32[]{:S(2)}, u32[]{:S(2)}) %collective-permute-start.75) | collective-permute-done | bytes 524320 | tf_op jit(solution)/shard_map/ppermute | solution.py:97
  685.4 10.0 %collective-permute-done.76 = bf16[128,2048]{1,0:T(8,128)(2,1)} collective-permute-done((bf16[128,2048]{1,0:T(8,128)(2,1)}, bf16[128,2048]{1,0:T(8,128)(2,1)}, u32[]{:S(2)}, u32[]{:S(2)}) %collective-permute-start.76) | collective-permute-done | bytes 524320 | tf_op jit(solution)/shard_map/ppermute | solution.py:106
  706.0 6.5 add_convert_fusion.5
  714.6 6.4 collective-permute-done.60
  723.1 6.8 collective-permute-done.62
  751.8 10.7 %maximum_convert_fusion.1 = f32[2,2048,1024]{2,1,0:T(8,128)} fusion(bf16[1,2048,1024]{2,1,0:T(8,128)(2,1)} %maximum_bitcast_fusion.3, bf16[1,2048,1024]{2,1,0:T(8,128)(2,1)} %maximum_bitcast_fusion.2), kind=kLoop, calls=%fused_computation.11 | loop fusion | flops 8388608 | bytes 25165824 | tf_op jit(solution)/shard_map/convert_element_type | solution.py:590
  762.5 14.5 %collective-permute-done.92 = bf16[1024,1024]{1,0:T(8,128)(2,1)} collective-permute-done((bf16[1024,1024]{1,0:T(8,128)(2,1)}, bf16[1024,1024]{1,0:T(8,128)(2,1)}, u32[]{:S(2)}, u32[]{:S(2)}) %collective-permute-start.92) | collective-permute-done | bytes 2097184 | tf_op jit(solution)/shard_map/ppermute | solution.py:570
  776.9 7.7 add_convert_fusion.4
  794.0 7.2 collective-permute-done.88
  825.5 9.4 %maximum_convert_fusion.2 = f32[2,2048,1024]{2,1,0:T(8,128)} fusion(bf16[1,2048,1024]{2,1,0:T(8,128)(2,1)S(1)} %maximum_bitcast_fusion.5, bf16[1,2048,1024]{2,1,0:T(8,128)(2,1)} %maximum_bitcast_fusion.4), kind=kLoop, calls=%fused_computation.12 | loop fusion | flops 8388608 | bytes 25165824 | tf_op jit(solution)/shard_map/convert_element_type | solution.py:590
  (771 shorter events, 431.7 us)
Async XLA Ops:
  0.7 32.1 %collective-permute-start = (bf16[128,2048]{1,0:T(8,128)(2,1)}, bf16[128,2048]{1,0:T(8,128)(2,1)S(1)}, u32[]{:S(2)}, u32[]{:S(2)}) collective-permute-start(bf16[128,2048]{1,0:T(8,128)(2,1)} %bitcast.187), channel_id=1, source_target_pairs={{0,1},{1,0},{2,3},{3,2},{4,5},{5,4},{6,7},{7,6},{8,9},{9,8},{10,11... | collective-permute-start | bytes 1572872 | tf_op jit(solution)/shard_map/ppermute | solution.py:67
  3.8 34.1 %collective-permute-start.1 = (bf16[128,2048]{1,0:T(8,128)(2,1)}, bf16[128,2048]{1,0:T(8,128)(2,1)S(1)}, u32[]{:S(2)}, u32[]{:S(2)}) collective-permute-start(bf16[128,2048]{1,0:T(8,128)(2,1)} %bitcast.188), channel_id=1, source_target_pairs={{0,2},{2,0},{4,6},{6,4},{1,3},{3,1},{5,7},{7,5},{8,10},{10,8},{12,... | collective-permute-start | bytes 1572872 | tf_op jit(solution)/shard_map/ppermute | solution.py:61
  13.4 50.2 %all-to-all-start = ((bf16[8,64,768]{2,1,0:T(8,128)(2,1)}), bf16[8,64,768]{2,1,0:T(8,128)(2,1)S(1)}, u32[]{:S(2)}, u32[]{:S(2)}) async-start(bf16[8,64,768]{2,1,0:T(8,128)(2,1)} %pad_maximum_fusion.3), calls=%async_computation | async-start | bytes 1572864 | tf_op jit(solution)/shard_map/all_to_all | solution.py:366
  52.6 33.0 %collective-permute-start.6 = (bf16[128,2048]{1,0:T(8,128)(2,1)}, bf16[128,2048]{1,0:T(8,128)(2,1)}, u32[]{:S(2)}, u32[]{:S(2)}) collective-permute-start(bf16[128,2048]{1,0:T(8,128)(2,1)} %collective-permute-done.5), channel_id=1, source_target_pairs={{0,1},{1,0},{2,3},{3,2},{4,5},{5,4},{6,7},{7,6},{8,9},{9,8},{10,11... | collective-permute-start | bytes 1572872 | tf_op jit(solution)/shard_map/ppermute | solution.py:67
  73.9 55.0 %collective-permute-start.7 = (bf16[512,768]{1,0:T(8,128)(2,1)S(1)}, bf16[512,768]{1,0:T(8,128)(2,1)S(1)}, u32[]{:S(2)}, u32[]{:S(2)}) collective-permute-start(bf16[512,768]{1,0:T(8,128)(2,1)S(1)} %bitcast.206), channel_id=1, source_target_pairs={{0,16},{16,0},{1,17},{17,1},{2,18},{18,2},{3,19},{19,3},{4,20},{20... | collective-permute-start | bytes 2359304 | tf_op jit(solution)/shard_map/ppermute | solution.py:131
  75.7 78.4 %collective-permute-start.9 = (bf16[512,768]{1,0:T(8,128)(2,1)S(1)}, bf16[512,768]{1,0:T(8,128)(2,1)S(1)}, u32[]{:S(2)}, u32[]{:S(2)}) collective-permute-start(bf16[512,768]{1,0:T(8,128)(2,1)S(1)} %bitcast.207), channel_id=1, source_target_pairs={{0,8},{8,0},{1,9},{9,1},{2,10},{10,2},{3,11},{11,3},{4,12},{12,4},... | collective-permute-start | bytes 2359304 | tf_op jit(solution)/shard_map/ppermute | solution.py:132
  125.3 39.2 %collective-permute-start.37 = (bf16[128,2048]{1,0:T(8,128)(2,1)}, bf16[128,2048]{1,0:T(8,128)(2,1)}, u32[]{:S(2)}, u32[]{:S(2)}) collective-permute-start(bf16[128,2048]{1,0:T(8,128)(2,1)} %collective-permute-done.36), channel_id=1, source_target_pairs={{0,1},{1,0},{2,3},{3,2},{4,5},{5,4},{6,7},{7,6},{8,9},{9,8},{10,11... | collective-permute-start | bytes 1572872 | tf_op jit(solution)/shard_map/ppermute | solution.py:67
  137.3 55.5 %collective-permute-start.39 = (bf16[128,2048]{1,0:T(8,128)(2,1)}, bf16[128,2048]{1,0:T(8,128)(2,1)}, u32[]{:S(2)}, u32[]{:S(2)}) collective-permute-start(bf16[128,2048]{1,0:T(8,128)(2,1)} %collective-permute-done.38), channel_id=1, source_target_pairs={{0,1},{1,0},{2,3},{3,2},{4,5},{5,4},{6,7},{7,6},{8,9},{9,8},{10,11... | collective-permute-start | bytes 1572872 | tf_op jit(solution)/shard_map/ppermute | solution.py:67
  189.4 34.4 %collective-permute-start.21 = (bf16[128,2048]{1,0:T(8,128)(2,1)S(1)}, bf16[128,2048]{1,0:T(8,128)(2,1)S(1)}, u32[]{:S(2)}, u32[]{:S(2)}) collective-permute-start(bf16[128,2048]{1,0:T(8,128)(2,1)S(1)} %pad_maximum_fusion.6), channel_id=1, source_target_pairs={{0,1},{1,0},{2,3},{3,2},{4,5},{5,4},{6,7},{7,6},{8,9},{9,8},{10,11... | collective-permute-start | bytes 1572872 | tf_op jit(solution)/shard_map/ppermute | solution.py:97
  190.6 33.0 %collective-permute-start.19 = (bf16[128,2048]{1,0:T(8,128)(2,1)S(1)}, bf16[128,2048]{1,0:T(8,128)(2,1)S(1)}, u32[]{:S(2)}, u32[]{:S(2)}) collective-permute-start(bf16[128,2048]{1,0:T(8,128)(2,1)S(1)} %pad_maximum_fusion.5), channel_id=1, source_target_pairs={{0,1},{1,0},{2,3},{3,2},{4,5},{5,4},{6,7},{7,6},{8,9},{9,8},{10,11... | collective-permute-start | bytes 1572872 | tf_op jit(solution)/shard_map/ppermute | solution.py:97
  191.7 38.2 %collective-permute-start.18 = (bf16[128,2048]{1,0:T(8,128)(2,1)S(1)}, bf16[128,2048]{1,0:T(8,128)(2,1)S(1)}, u32[]{:S(2)}, u32[]{:S(2)}) collective-permute-start(bf16[128,2048]{1,0:T(8,128)(2,1)S(1)} %pad_maximum_fusion.4), channel_id=1, source_target_pairs={{0,1},{1,0},{2,3},{3,2},{4,5},{5,4},{6,7},{7,6},{8,9},{9,8},{10,11... | collective-permute-start | bytes 1572872 | tf_op jit(solution)/shard_map/ppermute | solution.py:97
  253.2 55.0 %collective-permute-start.40 = (bf16[1024,2048]{1,0:T(8,128)(2,1)}, bf16[1024,2048]{1,0:T(8,128)(2,1)}, u32[]{:S(2)}, u32[]{:S(2)}) collective-permute-start(bf16[1024,2048]{1,0:T(8,128)(2,1)} %slice_dynamic-update-slice_fusion.16.refs_8_), channel_id=1, source_target_pairs={{0,8},{8,0},{1,9},{9,1},{2,10},{10,2},{3,11},{11,3},{4,12},{12,4},... | collective-permute-start | bytes 12582920 | tf_op jit(solution)/shard_map/ppermute | solution.py:527
  348.1 54.3 %collective-permute-start.42 = (bf16[512,2048]{1,0:T(8,128)(2,1)}, bf16[512,2048]{1,0:T(8,128)(2,1)}, u32[]{:S(2)}, u32[]{:S(2)}) collective-permute-start(bf16[512,2048]{1,0:T(8,128)(2,1)} %get-tuple-element.65), channel_id=1, source_target_pairs={{0,8},{8,0},{1,9},{9,1},{2,10},{10,2},{3,11},{11,3},{4,12},{12,4},... | collective-permute-start | bytes 6291464 | tf_op jit(solution)/shard_map/ppermute | solution.py:515
  400.4 82.8 %collective-permute-start.70 = (bf16[512,2048]{1,0:T(8,128)(2,1)S(1)}, bf16[512,2048]{1,0:T(8,128)(2,1)S(1)}, u32[]{:S(2)}, u32[]{:S(2)}) collective-permute-start(bf16[512,2048]{1,0:T(8,128)(2,1)S(1)} %get-tuple-element.247), channel_id=1, source_target_pairs={{0,16},{16,0},{1,17},{17,1},{2,18},{18,2},{3,19},{19,3},{4,20},{20... | collective-permute-start | bytes 6291464 | tf_op jit(solution)/shard_map/ppermute | solution.py:570
  401.8 148.6 %collective-permute-start.72 = (bf16[512,2048]{1,0:T(8,128)(2,1)}, bf16[512,2048]{1,0:T(8,128)(2,1)}, u32[]{:S(2)}, u32[]{:S(2)}) collective-permute-start(bf16[512,2048]{1,0:T(8,128)(2,1)} %get-tuple-element.248), channel_id=1, source_target_pairs={{0,16},{16,0},{1,17},{17,1},{2,18},{18,2},{3,19},{19,3},{4,20},{20... | collective-permute-start | bytes 6291464 | tf_op jit(solution)/shard_map/ppermute | solution.py:570
  407.3 36.2 %collective-permute-start.46 = (bf16[128,2048]{1,0:T(8,128)(2,1)S(1)}, bf16[128,2048]{1,0:T(8,128)(2,1)S(1)}, u32[]{:S(2)}, u32[]{:S(2)}) collective-permute-start(bf16[128,2048]{1,0:T(8,128)(2,1)S(1)} %pad_maximum_fusion.10), channel_id=1, source_target_pairs={{0,1},{1,0},{2,3},{3,2},{4,5},{5,4},{6,7},{7,6},{8,9},{9,8},{10,11... | collective-permute-start | bytes 1572872 | tf_op jit(solution)/shard_map/ppermute | solution.py:97
  408.4 33.9 %collective-permute-start.44 = (bf16[128,2048]{1,0:T(8,128)(2,1)S(1)}, bf16[128,2048]{1,0:T(8,128)(2,1)S(1)}, u32[]{:S(2)}, u32[]{:S(2)}) collective-permute-start(bf16[128,2048]{1,0:T(8,128)(2,1)S(1)} %pad_maximum_fusion.9), channel_id=1, source_target_pairs={{0,1},{1,0},{2,3},{3,2},{4,5},{5,4},{6,7},{7,6},{8,9},{9,8},{10,11... | collective-permute-start | bytes 1572872 | tf_op jit(solution)/shard_map/ppermute | solution.py:97
  483.2 110.4 %collective-permute-start.81 = (bf16[1024,1024]{1,0:T(8,128)(2,1)}, bf16[1024,1024]{1,0:T(8,128)(2,1)}, u32[]{:S(2)}, u32[]{:S(2)}) collective-permute-start(bf16[1024,1024]{1,0:T(8,128)(2,1)} %get-tuple-element.224), channel_id=1, source_target_pairs={{0,16},{16,0},{1,17},{17,1},{2,18},{18,2},{3,19},{19,3},{4,20},{20... | collective-permute-start | bytes 6291464 | tf_op jit(solution)/shard_map/ppermute | solution.py:570
  559.3 44.1 %collective-permute-start.73 = (bf16[512,2048]{1,0:T(8,128)(2,1)}, bf16[512,2048]{1,0:T(8,128)(2,1)}, u32[]{:S(2)}, u32[]{:S(2)}) collective-permute-start(bf16[512,2048]{1,0:T(8,128)(2,1)} %get-tuple-element.246), channel_id=1, source_target_pairs={{0,8},{8,0},{1,9},{9,1},{2,10},{10,2},{3,11},{11,3},{4,12},{12,4},... | collective-permute-start | bytes 6291464 | tf_op jit(solution)/shard_map/ppermute | solution.py:585
  593.6 112.4 %collective-permute-start.82 = (bf16[1024,1024]{1,0:T(8,128)(2,1)}, bf16[1024,1024]{1,0:T(8,128)(2,1)}, u32[]{:S(2)}, u32[]{:S(2)}) collective-permute-start(bf16[1024,1024]{1,0:T(8,128)(2,1)} %get-tuple-element.223), channel_id=1, source_target_pairs={{0,16},{16,0},{1,17},{17,1},{2,18},{18,2},{3,19},{19,3},{4,20},{20... | collective-permute-start | bytes 6291464 | tf_op jit(solution)/shard_map/ppermute | solution.py:570
  594.5 142.8 %collective-permute-start.90 = (bf16[1024,1024]{1,0:T(8,128)(2,1)}, bf16[1024,1024]{1,0:T(8,128)(2,1)}, u32[]{:S(2)}, u32[]{:S(2)}) collective-permute-start(bf16[1024,1024]{1,0:T(8,128)(2,1)} %get-tuple-element.215), channel_id=1, source_target_pairs={{0,16},{16,0},{1,17},{17,1},{2,18},{18,2},{3,19},{19,3},{4,20},{20... | collective-permute-start | bytes 6291464 | tf_op jit(solution)/shard_map/ppermute | solution.py:570
  598.1 39.0 %collective-permute-start.58 = (bf16[512,2048]{1,0:T(8,128)(2,1)}, bf16[512,2048]{1,0:T(8,128)(2,1)}, u32[]{:S(2)}, u32[]{:S(2)}) collective-permute-start(bf16[512,2048]{1,0:T(8,128)(2,1)} %get-tuple-element.71), channel_id=1, source_target_pairs={{0,8},{8,0},{1,9},{9,1},{2,10},{10,2},{3,11},{11,3},{4,12},{12,4},... | collective-permute-start | bytes 6291464 | tf_op jit(solution)/shard_map/ppermute | solution.py:515
  603.5 37.9 %collective-permute-start.57 = (bf16[512,2048]{1,0:T(8,128)(2,1)}, bf16[512,2048]{1,0:T(8,128)(2,1)}, u32[]{:S(2)}, u32[]{:S(2)}) collective-permute-start(bf16[512,2048]{1,0:T(8,128)(2,1)} %get-tuple-element.67), channel_id=1, source_target_pairs={{0,8},{8,0},{1,9},{9,1},{2,10},{10,2},{3,11},{11,3},{4,12},{12,4},... | collective-permute-start | bytes 6291464 | tf_op jit(solution)/shard_map/ppermute | solution.py:515
  637.2 36.9 %collective-permute-start.77 = (bf16[128,2048]{1,0:T(8,128)(2,1)}, bf16[128,2048]{1,0:T(8,128)(2,1)}, u32[]{:S(2)}, u32[]{:S(2)}) collective-permute-start(bf16[128,2048]{1,0:T(8,128)(2,1)} %pad_maximum_fusion.18), channel_id=1, source_target_pairs={{0,1},{1,0},{2,3},{3,2},{4,5},{5,4},{6,7},{7,6},{8,9},{9,8},{10,11... | collective-permute-start | bytes 1572872 | tf_op jit(solution)/shard_map/ppermute | solution.py:97
  712.7 31.6 %collective-permute-start.85 = (bf16[1024,1024]{1,0:T(8,128)(2,1)}, bf16[1024,1024]{1,0:T(8,128)(2,1)}, u32[]{:S(2)}, u32[]{:S(2)}) collective-permute-start(bf16[1024,1024]{1,0:T(8,128)(2,1)} %get-tuple-element.222), channel_id=1, source_target_pairs={{0,8},{8,0},{1,9},{9,1},{2,10},{10,2},{3,11},{11,3},{4,12},{12,4},... | collective-permute-start | bytes 6291464 | tf_op jit(solution)/shard_map/ppermute | solution.py:585
  729.8 47.1 %collective-permute-start.92 = (bf16[1024,1024]{1,0:T(8,128)(2,1)}, bf16[1024,1024]{1,0:T(8,128)(2,1)}, u32[]{:S(2)}, u32[]{:S(2)}) collective-permute-start(bf16[1024,1024]{1,0:T(8,128)(2,1)} %get-tuple-element.100), channel_id=1, source_target_pairs={{0,16},{16,0},{1,17},{17,1},{2,18},{18,2},{3,19},{19,3},{4,20},{20... | collective-permute-start | bytes 6291464 | tf_op jit(solution)/shard_map/ppermute | solution.py:570
  730.2 54.4 %collective-permute-start.59 = (bf16[128,2048]{1,0:T(8,128)(2,1)}, bf16[128,2048]{1,0:T(8,128)(2,1)}, u32[]{:S(2)}, u32[]{:S(2)}) collective-permute-start(bf16[128,2048]{1,0:T(8,128)(2,1)} %pad_maximum_fusion.12), channel_id=1, source_target_pairs={{0,1},{1,0},{2,3},{3,2},{4,5},{5,4},{6,7},{7,6},{8,9},{9,8},{10,11... | collective-permute-start | bytes 1572872 | tf_op jit(solution)/shard_map/ppermute | solution.py:97
  733.5 54.7 %all-to-all-start.2 = ((f32[32,1,1280]{2,1,0:T(1,128)}), f32[32,1,1280]{2,1,0:T(1,128)}, u32[]{:S(2)}, u32[]{:S(2)}) async-start(f32[32,1,1280]{2,1,0:T(1,128)} %copy.109), calls=%async_computation.2 | async-start | bytes 327680 | tf_op jit(solution)/shard_map/all_to_all | solution.py:703
  737.3 47.3 %collective-permute-start.61 = (bf16[128,2048]{1,0:T(8,128)(2,1)}, bf16[128,2048]{1,0:T(8,128)(2,1)S(1)}, u32[]{:S(2)}, u32[]{:S(2)}) collective-permute-start(bf16[128,2048]{1,0:T(8,128)(2,1)} %add_convert_fusion.19), channel_id=1, source_target_pairs={{0,2},{2,0},{4,6},{6,4},{1,3},{3,1},{5,7},{7,5},{8,10},{10,8},{12,... | collective-permute-start | bytes 1572872 | tf_op jit(solution)/shard_map/ppermute | solution.py:106
  739.3 45.3 %collective-permute-start.65 = (bf16[128,2048]{1,0:T(8,128)(2,1)}, bf16[128,2048]{1,0:T(8,128)(2,1)S(1)}, u32[]{:S(2)}, u32[]{:S(2)}) collective-permute-start(bf16[128,2048]{1,0:T(8,128)(2,1)} %add_convert_fusion.17), channel_id=1, source_target_pairs={{0,4},{2,6},{4,0},{6,2},{1,5},{3,7},{5,1},{7,3},{8,12},{10,14},{12... | collective-permute-start | bytes 1572872 | tf_op jit(solution)/shard_map/ppermute | solution.py:104
  784.6 33.0 %collective-permute-start.93 = (bf16[1024,1024]{1,0:T(8,128)(2,1)}, bf16[1024,1024]{1,0:T(8,128)(2,1)}, u32[]{:S(2)}, u32[]{:S(2)}) collective-permute-start(bf16[1024,1024]{1,0:T(8,128)(2,1)} %get-tuple-element.214), channel_id=1, source_target_pairs={{0,8},{8,0},{1,9},{9,1},{2,10},{10,2},{3,11},{11,3},{4,12},{12,4},... | collective-permute-start | bytes 6291464 | tf_op jit(solution)/shard_map/ppermute | solution.py:585
  787.7 32.3 %collective-permute-start.91 = (bf16[1024,1024]{1,0:T(8,128)(2,1)}, bf16[1024,1024]{1,0:T(8,128)(2,1)}, u32[]{:S(2)}, u32[]{:S(2)}) collective-permute-start(bf16[1024,1024]{1,0:T(8,128)(2,1)} %get-tuple-element.213), channel_id=1, source_target_pairs={{0,8},{8,0},{1,9},{9,1},{2,10},{10,2},{3,11},{11,3},{4,12},{12,4},... | collective-permute-start | bytes 6291464 | tf_op jit(solution)/shard_map/ppermute | solution.py:585
  (199 other events, 5077.5 us)

commit v3 on v2

--- a/solution.py
+++ b/solution.py
@@ -27,6 +27,8 @@
 
 
 def after(values, *others):
+    if not others:
+        return values
     return lax.optimization_barrier((values,) + others)[0]
 
 
@@ -145,12 +147,13 @@
     return kept + lax.ppermute(away, "core", SWAP).astype(F32)
 
 
-def keep_x(kept, x_count):
+def keep_x(kept, x_count, start=()):
     x_at = lax.axis_index("x")
     total = lax.dynamic_index_in_dim(kept, x_at, 0, keepdims=False)
     for i in range(1, x_count):
         away = lax.dynamic_index_in_dim(kept, (x_at - i) % x_count, 0, keepdims=False)
-        total = total + lax.ppermute(away.astype(BF16), "x", turn(x_count, -i)).astype(F32)
+        arrived = lax.ppermute(away.astype(BF16), "x", turn(x_count, -i))
+        total = total + after(arrived, *start).astype(F32)
     return total
 
 
@@ -226,7 +229,7 @@
     sets, at, hot, router, select, select_t, micro, moe, cot, w_gate, w_up, w_down, experts, hidden
 ):
     count, (slots, seq_len), width = len(sets), select.shape[1:], router.shape[0]
-    block = 256
+    block = min(hidden, 512)
     steps, rows = hidden // block, count * slots
 
     def whole(array):
@@ -235,7 +238,7 @@
         )
 
     def kept(shape):
-        return pl.BlockSpec(shape, lambda f, at: (0, 0))
+        return pl.BlockSpec(shape, lambda f, at: (0, 0), pipeline_mode=pl.Buffered(1))
 
     wide = pl.BlockSpec((1, width, block), lambda f, at: (at[0], 0, at[1] + f))
     tall = pl.BlockSpec((1, block, width), lambda f, at: (at[0], at[1] + f, 0))
@@ -290,7 +293,7 @@
         + [inner] * 3
         + [jax.ShapeDtypeStruct((rows, 128), BF16)],
         compiler_params=pltpu.CompilerParams(
-            dimension_semantics=("arbitrary",), vmem_limit_bytes=60 * 2**20
+            dimension_semantics=("arbitrary",), vmem_limit_bytes=62 * 2**20
         ),
         cost_estimate=pl.CostEstimate(
             flops=12 * rows * hidden * width + 8 * rows * seq_len * width,
@@ -300,6 +303,41 @@
         name="experts",
     )(at, hot, router, *tables, *moe, *cot, w_gate, w_up, w_down)
     return result[:count], result[count : 2 * count], result[2 * count :]
+
+
+def place_kernel(core_ref, own_ref, other_ref, out_ref):
+    @pl.when(core_ref[0] == 0)
+    def _():
+        out_ref[0] = own_ref[...].astype(F32)
+        out_ref[1] = other_ref[...].astype(F32)
+
+    @pl.when(core_ref[0] != 0)
+    def _():
+        out_ref[0] = other_ref[...].astype(F32)
+        out_ref[1] = own_ref[...].astype(F32)
+
+
+def place_experts(core, own, other):
+    rows, columns = own.shape
+    block = min(rows, 2**18 // columns)
+    half = pl.BlockSpec((block, columns), lambda i, core: (i, 0))
+    return pl.pallas_call(
+        place_kernel,
+        grid_spec=pltpu.PrefetchScalarGridSpec(
+            num_scalar_prefetch=1,
+            grid=(rows // block,),
+            in_specs=[half, half],
+            out_specs=pl.BlockSpec((2, block, columns), lambda i, core: (0, i, 0)),
+        ),
+        out_shape=jax.ShapeDtypeStruct((2, rows, columns), F32),
+        compiler_params=pltpu.CompilerParams(
+            dimension_semantics=("arbitrary",), vmem_limit_bytes=32 * 2**20
+        ),
+        cost_estimate=pl.CostEstimate(
+            flops=0, bytes_accessed=12 * rows * columns, transcendentals=0
+        ),
+        name="place",
+    )(core[None].astype(jnp.int32), own, other)
 
 
 def norm_scale(values):
@@ -455,7 +493,7 @@
             expert_place = jnp.stack([core, 0 * core]).astype(jnp.int32)
         else:
             expert_at, hidden = ep_at, ff_width // 2
-            expert_place = jnp.stack([0 * core, core * (hidden // 256)]).astype(jnp.int32)
+            expert_place = jnp.stack([0 * core, core]).astype(jnp.int32)
         hot = (jnp.arange(128, dtype=jnp.int32) == expert_at).astype(F32)[None]
         padded_router = jnp.pad(full_router, ((0, 0), (0, 128 - expert_count)))
 
@@ -491,7 +529,7 @@
             [jnp.sum(query_raw * query_raw, axis=1), jnp.sum(key_raw * key_raw, axis=1)]
         )
         squares = sum_ep(squares, y_count, micro_count)
-        cot_all = [gather(after(cotangent, low_rows))]
+        cot_all = [gather(after(cotangent, sent_qkv))]
         scales = lax.rsqrt(squares / width + NORM_EPSILON)
         query_scale, key_scale = scales[0][:, None], scales[1][:, None]
         query = rope(query_raw * query_scale * gain_query).astype(BF16)
@@ -560,10 +598,6 @@
                 total = term if total is None else total + term
             return total
 
-        def halves(part):
-            middle = part.shape[0] // 2
-            return [part[:middle], part[middle:]]
-
         def over_x(low, start=None):
             sent = low if start is None else after(low, start)
             return [low] + [
@@ -579,15 +613,12 @@
                 total = total + item.astype(F32)
             return total.astype(BF16)
 
-        def both_cores(sums, axis):
-            first, second = [], []
-            for own_part in sums:
-                other = lax.ppermute(own_part, "core", SWAP)
-                first.append(jnp.where(core == 0, own_part, other))
-                second.append(jnp.where(core == 0, other, own_part))
-            first, second = jnp.concatenate(first), jnp.concatenate(second)
+        def both_cores(own_part, axis):
+            other = lax.ppermute(own_part, "core", SWAP)
             if local_experts == 2:
-                return jnp.stack([first, second]).astype(F32)
+                return place_experts(core, own_part, other)
+            first = jnp.where(core == 0, own_part, other)
+            second = jnp.where(core == 0, other, own_part)
             return jnp.concatenate([first, second], axis=axis)[None].astype(F32)
 
         down_low = over_pairs(2, 1).astype(BF16)
@@ -595,9 +626,7 @@
         gate_low = over_pairs(0, 3).astype(BF16)
         up_low = over_pairs(0, 4).astype(BF16)
         router_grad = over_pairs(0, 5)[:, :expert_count]
-        down_parts = [over_x(p) for p in halves(down_low)]
-        gate_parts = [over_x(p) for p in halves(gate_low)]
-        up_first, up_second = halves(up_low)
+        down_parts, gate_parts = over_x(down_low), over_x(gate_low)
 
         grad_out = cotangent.reshape(-1, width).astype(F32)
         moe_gain_grad = jnp.sum(grad_moe_in * resid_mid * moe_scale, axis=0)
@@ -608,11 +637,11 @@
             - resid_mid * (moe_scale**3 * jnp.mean(resid_mid * inner, axis=-1, keepdims=True))
         )
         grad_attn = gather(grad_mid.astype(BF16))
-        mixture = scatter(with_other_core([after(p, grad_attn) for p in out_parts]))
+        mixture = scatter(after(with_other_core(out_parts), grad_attn))
         block_out = (resid_mid + mixture).astype(BF16)
         grad_attended = mm_cols(grad_attn, out_here).astype(BF16)
-        down_sums = [summed(down_parts[0], grad_moe_in), summed(down_parts[1], grad_attn)]
-        up_parts = [over_x(up_first)]
+        down_sum = summed(down_parts, grad_attn)
+        up_parts = over_x(up_low, grad_attn)
         grad_query, grad_key, grad_value = [], [], []
         for m in range(micro_count):
             query_here, key_here, value_here = [], [], []
@@ -644,8 +673,9 @@
         key_back = (
             key_scale * inner_key - key_raw * (key_scale**3 * means[1][:, None])
         ).astype(BF16)
-        raw_grad = jnp.concatenate([query_back, key_back, grad_value], axis=1)
-        d_down = both_cores(down_sums, 0)
+        raw_grad = jnp.concatenate([after(query_back, block_out), key_back, grad_value], axis=1)
+        d_down = both_cores(down_sum, 0)
+        gate_sum = summed(gate_parts, raw_grad)
         normed_part = mm_cols(after(raw_grad, d_down), qkv)
         attn_gain_grad = jnp.sum(normed_part * rows * row_scale, axis=0)
         grad_normed = scatter(normed_part.astype(BF16))
@@ -659,13 +689,11 @@
 
         qkv_grad = mm_rows(normed, raw_grad)
         qkv_kept = keep_core(qkv_grad.reshape(grp_size, -1, 3 * local_width), x_count)
-        up_parts.append(over_x(up_second, qkv_kept))
-        qkv_grad = keep_x(qkv_kept, x_count)
-        gate_sums = [summed(gate_parts[0], raw_grad), summed(gate_parts[1], grad_normed)]
-        d_gate = both_cores(gate_sums, 1)
+        qkv_grad = keep_x(qkv_kept, x_count, (grad_normed,))
+        d_gate = both_cores(gate_sum, 1)
         qkv_grad = after(qkv_grad, d_gate, block_out)
-        up_sums = [summed(up_parts[0], grad_normed), summed(up_parts[1], d_gate)]
-        d_up = both_cores(up_sums, 1)
+        up_sum = summed(up_parts, grad_normed)
+        d_up = both_cores(up_sum, 1)
         qkv_grad = qkv_grad.astype(BF16).reshape(group_size, weight_rows, 3 * local_width)
         qkv_grad = lax.all_to_all(
             qkv_grad, ("z", "y"), split_axis=0, concat_axis=0, tiled=True
@@ -701,7 +729,7 @@
             axis=1,
         )
         small_grads = lax.all_to_all(
-            after(small_grads, grad_normed, gate_sums), ALL, split_axis=0, concat_axis=0, tiled=True
+            after(small_grads, grad_normed, gate_sum), ALL, split_axis=0, concat_axis=0, tiled=True
         )
         small_grads = jnp.sum(small_grads, axis=0)
         gain_grads = small_grads[: 4 * weight_rows].reshape(4, weight_rows)

time: 849 us -> 803 us (0.946)
  other arithmetic: 150 us -> 77.4 us
  Pallas kernels: 79.3 us -> 118 us
  local copies, waits for them, and re-layouts: 110 us -> 90.8 us
  waiting for transfers between devices: 297 us -> 306 us
    pallas_call x0 -> x3, Pallas kernels: none -> 30.8 us  [place_experts(): pl.pallas_call(place_kernel, grid_spec=pltpu.PrefetchScalarGridSpec(num_s...]
    convert_element_type x3 -> x1, other arithmetic: 31 us -> 1.18 us  [per_device(): block_out = (resid_mid + mixture).astype(BF16)]
    ppermute x4, waiting for transfers between devices: 36.6 us -> 53.5 us  [scatter_ep(): near = lax.ppermute(sums[1].astype(BF16), 'z', flip(4, 1)).astype(F32)]
    ppermute x16, waiting for transfers between devices: 62.4 us -> 78.3 us  [along_y(): arrived = lax.ppermute(piece(a, j).astype(BF16), 'y', flip(y_count, j))]
    select_n x6 -> x0, other arithmetic: 15 us -> none  [both_cores(): first.append(jnp.where(core == 0, own_part, other))]
    ppermute x6 -> x3, waiting for transfers between devices: 14.5 us -> 0.01 us  [over_x(): lax.ppermute(sent, 'x', turn(x_count, i))]
    ppermute x4, waiting for transfers between devices: 55.5 us -> 41.7 us  [gather_ep(): by_z[2] = lax.ppermute(block, 'z', flip(4, 2))]
    another operation x6 -> x0, other arithmetic: 13.1 us -> none  [both_cores(): return jnp.stack([first, second]).astype(F32)]
  transfers between devices with their start and end apart: 98 -> 92, of which waited for: 37 -> 41; matrix products, arithmetic and copies ran while one was open for 37% -> 29% of each run, Pallas kernels for 5% -> 7%
where the time goes in v3:
time: 803 us; the launch traced here: 793 us
  waiting for transfers between devices  306 us (38%)
  Pallas kernels  118 us (15%)
  starting transfers between devices  116 us (14%)
  local copies, waits for them, and re-layouts  90.8 us (11%)
  matrix products  80.3 us (10%)
  other arithmetic  77.4 us (10%)
    pallas_call x2, Pallas kernels, run_experts(): pl.pallas_call(lambda at, *refs: experts_kernel(count, experts, *refs), g...  87.6 us
    ppermute x16, waiting for transfers between devices, along_y(): arrived = lax.ppermute(piece(a, j).astype(BF16), 'y', flip(y_count, j))  78.3 us
    unnamed x271, local copies, waits for them, and re-layouts  58.3 us
    ppermute x4, waiting for transfers between devices, scatter_ep(): near = lax.ppermute(sums[1].astype(BF16), 'z', flip(4, 1)).astype(F32)  53.5 us
    dot_general x18, matrix products, mm_rows(): lax.dot_general(left, right, (((0,), (0,)), ((), ())), preferred_element_...  49.8 us
    ppermute x16, waiting for transfers between devices, along_y(): blocks[a, j] = lax.ppermute(by_z[a], 'y', flip(y_count, j))  45 us
    ppermute x4, waiting for transfers between devices, gather_ep(): by_z[2] = lax.ppermute(block, 'z', flip(4, 2))  41.7 us
    ppermute x4, waiting for transfers between devices, gather_ep(): by_z[3] = lax.ppermute(by_z[2], 'z', flip(4, 1))  32.3 us
  transfers between devices with their start and end apart: 92, of which 41 were waited for; matrix products, arithmetic and copies ran while one was open for 29% of the time, Pallas kernels for 7%

profile of v3, /device:TPU:0, one launch (start us, length us, event | category | flops | bytes accessed | tf_op | source)
XLA Modules:
  0.0 792.8 jit_solution(3115523100498843208)
XLA Ops:
  42.3 11.4 %collective-permute-done.5 = bf16[128,2048]{1,0:T(8,128)(2,1)} collective-permute-done((bf16[128,2048]{1,0:T(8,128)(2,1)S(1)}, bf16[128,2048]{1,0:T(8,128)(2,1)}, u32[]{:S(2)}, u32[]{:S(2)}) %collective-permute-start.5) | collective-permute-done | bytes 524320 | tf_op jit(solution)/shard_map/ppermute | solution.py:72
  67.4 7.2 all-to-all-start.1
  101.1 10.9 %collective-permute-done.36 = bf16[128,2048]{1,0:T(8,128)(2,1)S(1)} collective-permute-done((bf16[128,2048]{1,0:T(8,128)(2,1)S(1)}, bf16[128,2048]{1,0:T(8,128)(2,1)S(1)}, u32[]{:S(2)}, u32[]{:S(2)}) %collective-permute-start.36) | collective-permute-done | bytes 524320 | tf_op jit(solution)/shard_map/ppermute | solution.py:62
  117.5 8.7 %collective-permute-done.38 = bf16[128,2048]{1,0:T(8,128)(2,1)} collective-permute-done((bf16[128,2048]{1,0:T(8,128)(2,1)S(1)}, bf16[128,2048]{1,0:T(8,128)(2,1)}, u32[]{:S(2)}, u32[]{:S(2)}) %collective-permute-start.38) | collective-permute-done | bytes 524320 | tf_op jit(solution)/shard_map/ppermute | solution.py:72
  127.0 11.1 %collective-permute-done.35 = bf16[128,2048]{1,0:T(8,128)(2,1)S(1)} collective-permute-done((bf16[128,2048]{1,0:T(8,128)(2,1)}, bf16[128,2048]{1,0:T(8,128)(2,1)S(1)}, u32[]{:S(2)}, u32[]{:S(2)}) %collective-permute-start.35) | collective-permute-done | bytes 524320 | tf_op jit(solution)/shard_map/ppermute | solution.py:69
  144.2 8.2 %fusion.125 = (bf16[1024,768]{0,1:T(8,128)(2,1)}, f32[1024,768]{0,1:T(8,128)S(1)}) fusion(bf16[2048,768]{1,0:T(8,128)(2,1)S(1)} %bitcast.192, bf16[1024,2048]{1,0:T(8,128)(2,1)} %slice_dynamic-update-slice_fusion.46, f32[2048]{0:T(1024)S(1)} %get-tuple-element.191, f32[1024]{0:T(1024)S(1)} %add_rsqrt_fusion.1), kind=kOutput, calls=%fused_computation.384 | convolution fusion | flops 3230400512 | bytes 12070912 | tf_op jit(solution)/shard_map/dot_general | solution.py:36
  184.8 11.1 %collective-permute-done.22 = bf16[128,2048]{1,0:T(8,128)(2,1)S(1)} collective-permute-done((bf16[128,2048]{1,0:T(8,128)(2,1)S(1)}, bf16[128,2048]{1,0:T(8,128)(2,1)S(1)}, u32[]{:S(2)}, u32[]{:S(2)}) %collective-permute-start.22) | collective-permute-done | bytes 524320 | tf_op jit(solution)/shard_map/ppermute | solution.py:99
  198.4 19.7 %collective-permute-done.19 = bf16[128,2048]{1,0:T(8,128)(2,1)S(1)} collective-permute-done((bf16[128,2048]{1,0:T(8,128)(2,1)S(1)}, bf16[128,2048]{1,0:T(8,128)(2,1)S(1)}, u32[]{:S(2)}, u32[]{:S(2)}) %collective-permute-start.19) | collective-permute-done | bytes 524320 | tf_op jit(solution)/shard_map/ppermute | solution.py:99
  223.8 17.2 %collective-permute-done.20 = bf16[128,2048]{1,0:T(8,128)(2,1)S(1)} collective-permute-done((bf16[128,2048]{1,0:T(8,128)(2,1)S(1)}, bf16[128,2048]{1,0:T(8,128)(2,1)S(1)}, u32[]{:S(2)}, u32[]{:S(2)}) %collective-permute-start.20) | collective-permute-done | bytes 524320 | tf_op jit(solution)/shard_map/ppermute | solution.py:108
  247.9 13.2 %collective-permute-done.28 = bf16[128,2048]{1,0:T(8,128)(2,1)S(1)} collective-permute-done((bf16[128,2048]{1,0:T(8,128)(2,1)S(1)}, bf16[128,2048]{1,0:T(8,128)(2,1)S(1)}, u32[]{:S(2)}, u32[]{:S(2)}) %collective-permute-start.28) | collective-permute-done | bytes 524320 | tf_op jit(solution)/shard_map/ppermute | solution.py:62
  274.3 7.3 collective-permute-done.27
  301.2 48.9 %experts.3 = (bf16[512,2048]{1,0:T(8,128)(2,1)}, bf16[512,2048]{1,0:T(8,128)(2,1)}, bf16[512,2048]{1,0:T(8,128)(2,1)}, bf16[512,2048]{1,0:T(8,128)(2,1)}, bf16[5...) custom-call(s32[2]{0:T(128)} %pad_add_fusion.at, ...), custom_call_target="tpu_custom_call" | custom-call | flops 19327352832 | bytes 38797312 | tf_op jit(solution)/shard_map/experts/pallas_call | solution.py:275
  350.7 38.7 %experts.2 = (bf16[512,2048]{1,0:T(8,128)(2,1)}, bf16[512,2048]{1,0:T(8,128)(2,1)}, bf16[512,2048]{1,0:T(8,128)(2,1)}, bf16[512,2048]{1,0:T(8,128)(2,1)}, bf16[5...) custom-call(s32[2]{0:T(128)} %pad_add_fusion.at, ...), custom_call_target="tpu_custom_call" | custom-call | flops 19327352832 | bytes 38797312 | tf_op jit(solution)/shard_map/experts/pallas_call | solution.py:275
  417.0 7.6 add_convert_fusion.3
  437.3 7.4 collective-permute-done.46
  454.7 14.6 %collective-permute-done.47 = bf16[128,2048]{1,0:T(8,128)(2,1)S(1)} collective-permute-done((bf16[128,2048]{1,0:T(8,128)(2,1)S(1)}, bf16[128,2048]{1,0:T(8,128)(2,1)S(1)}, u32[]{:S(2)}, u32[]{:S(2)}) %collective-permute-start.47) | collective-permute-done | bytes 524320 | tf_op jit(solution)/shard_map/ppermute | solution.py:108
  484.7 14.0 %collective-permute-done.55 = bf16[128,2048]{1,0:T(8,128)(2,1)S(1)} collective-permute-done((bf16[128,2048]{1,0:T(8,128)(2,1)S(1)}, bf16[128,2048]{1,0:T(8,128)(2,1)S(1)}, u32[]{:S(2)}, u32[]{:S(2)}) %collective-permute-start.55) | collective-permute-done | bytes 524320 | tf_op jit(solution)/shard_map/ppermute | solution.py:62
  500.9 8.1 %collective-permute-done.57 = bf16[128,2048]{1,0:T(8,128)(2,1)S(1)} collective-permute-done((bf16[128,2048]{1,0:T(8,128)(2,1)S(1)}, bf16[128,2048]{1,0:T(8,128)(2,1)S(1)}, u32[]{:S(2)}, u32[]{:S(2)}) %collective-permute-start.57) | collective-permute-done | bytes 524320 | tf_op jit(solution)/shard_map/ppermute | solution.py:72
  509.9 12.2 %collective-permute-done.54 = bf16[128,2048]{1,0:T(8,128)(2,1)S(1)} collective-permute-done((bf16[128,2048]{1,0:T(8,128)(2,1)S(1)}, bf16[128,2048]{1,0:T(8,128)(2,1)S(1)}, u32[]{:S(2)}, u32[]{:S(2)}) %collective-permute-start.54) | collective-permute-done | bytes 524320 | tf_op jit(solution)/shard_map/ppermute | solution.py:69
  558.1 8.5 %add_convert_fusion.4.own_ref = bf16[1024,2048]{1,0:T(8,128)(2,1)} fusion(bf16[1024,2048]{1,0:T(8,128)(2,1)} %collective-permute-done.70, bf16[1024,2048]{1,0:T(8,128)(2,1)} %add_convert_fusion.5), kind=kLoop, calls=%fused_computation.14 | loop fusion | flops 8388608 | bytes 12582912 | tf_op jit(solution)/shard_map/convert_element_type | solution.py:614
  585.9 9.0 %collective-permute-done.60 = bf16[128,2048]{1,0:T(8,128)(2,1)} collective-permute-done((bf16[128,2048]{1,0:T(8,128)(2,1)}, bf16[128,2048]{1,0:T(8,128)(2,1)}, u32[]{:S(2)}, u32[]{:S(2)}) %collective-permute-start.60) | collective-permute-done | bytes 524320 | tf_op jit(solution)/shard_map/ppermute | solution.py:99
  605.9 11.1 %collective-permute-done.61 = bf16[128,2048]{1,0:T(8,128)(2,1)S(1)} collective-permute-done((bf16[128,2048]{1,0:T(8,128)(2,1)S(1)}, bf16[128,2048]{1,0:T(8,128)(2,1)S(1)}, u32[]{:S(2)}, u32[]{:S(2)}) %collective-permute-start.61) | collective-permute-done | bytes 524320 | tf_op jit(solution)/shard_map/ppermute | solution.py:108
  623.1 10.4 %place.3 = f32[2,1024,2048]{2,1,0:T(8,128)} custom-call(s32[1]{0:T(128)} %bitcast.32.core_ref, bf16[1024,2048]{1,0:T(8,128)(2,1)} %add_convert_fusion.4.own_ref, bf16[1024,2048]{1,0:T(8,128)(2,1)} %collective-permute-done.71.other_ref), custom_call_target="tpu_custom_call" | custom-call | bytes 25165824 | tf_op jit(solution)/shard_map/place/pallas_call | solution.py:324
  633.5 6.6 fusion.4
  641.9 7.6 add_convert_fusion.2.own_ref
  652.0 23.2 %collective-permute-done.73 = bf16[128,2048]{1,0:T(8,128)(2,1)S(1)} collective-permute-done((bf16[128,2048]{1,0:T(8,128)(2,1)S(1)}, bf16[128,2048]{1,0:T(8,128)(2,1)S(1)}, u32[]{:S(2)}, u32[]{:S(2)}) %collective-permute-start.73) | collective-permute-done | bytes 524320 | tf_op jit(solution)/shard_map/ppermute | solution.py:99
  678.7 6.1 fusion.8
  688.7 10.6 %collective-permute-done.74 = bf16[128,2048]{1,0:T(8,128)(2,1)S(1)} collective-permute-done((bf16[128,2048]{1,0:T(8,128)(2,1)S(1)}, bf16[128,2048]{1,0:T(8,128)(2,1)S(1)}, u32[]{:S(2)}, u32[]{:S(2)}) %collective-permute-start.74) | collective-permute-done | bytes 524320 | tf_op jit(solution)/shard_map/ppermute | solution.py:108
  728.5 12.5 %collective-permute-done.81 = bf16[512,768]{1,0:T(8,128)(2,1)} collective-permute-done((bf16[512,768]{1,0:T(8,128)(2,1)S(1)}, bf16[512,768]{1,0:T(8,128)(2,1)}, u32[]{:S(2)}, u32[]{:S(2)}) %collective-permute-start.81) | collective-permute-done | bytes 786464 | tf_op jit(solution)/shard_map/ppermute | solution.py:155
  741.0 10.2 %place.4 = f32[2,2048,1024]{2,1,0:T(8,128)} custom-call(s32[1]{0:T(128)} %bitcast.32.core_ref, bf16[2048,1024]{1,0:T(8,128)(2,1)} %add_convert_fusion.2.own_ref, bf16[2048,1024]{1,0:T(8,128)(2,1)} %collective-permute-done.82.other_ref), custom_call_target="tpu_custom_call" | custom-call | bytes 25165824 | tf_op jit(solution)/shard_map/place/pallas_call | solution.py:324
  762.7 14.3 %all-to-all-done.3 = bf16[8,64,768]{2,1,0:T(8,128)(2,1)S(1)} async-done(((bf16[8,64,768]{2,1,0:T(8,128)(2,1)}), bf16[8,64,768]{2,1,0:T(8,128)(2,1)S(1)}, u32[]{:S(2)}, u32[]{:S(2)}) %all-to-all-start.3) | async-done | bytes 786464 | tf_op jit(solution)/shard_map/all_to_all | solution.py:698
  782.1 10.2 %place.5 = f32[2,2048,1024]{2,1,0:T(8,128)} custom-call(s32[1]{0:T(128)} %bitcast.32.core_ref, bf16[2048,1024]{1,0:T(8,128)(2,1)} %add_convert_fusion.own_ref, bf16[2048,1024]{1,0:T(8,128)(2,1)} %collective-permute-done.87.other_ref), custom_call_target="tpu_custom_call" | custom-call | bytes 25165824 | tf_op jit(solution)/shard_map/place/pallas_call | solution.py:324
  (683 shorter events, 371.4 us)
Async XLA Ops:
  0.7 36.9 %collective-permute-start = (bf16[128,2048]{1,0:T(8,128)(2,1)}, bf16[128,2048]{1,0:T(8,128)(2,1)S(1)}, u32[]{:S(2)}, u32[]{:S(2)}) collective-permute-start(bf16[128,2048]{1,0:T(8,128)(2,1)} %bitcast.175), channel_id=1, source_target_pairs={{0,1},{1,0},{2,3},{3,2},{4,5},{5,4},{6,7},{7,6},{8,9},{9,8},{10,11... | collective-permute-start | bytes 1572872 | tf_op jit(solution)/shard_map/ppermute | solution.py:69
  3.8 33.8 %collective-permute-start.1 = (bf16[128,2048]{1,0:T(8,128)(2,1)}, bf16[128,2048]{1,0:T(8,128)(2,1)}, u32[]{:S(2)}, u32[]{:S(2)}) collective-permute-start(bf16[128,2048]{1,0:T(8,128)(2,1)} %bitcast.176), channel_id=1, source_target_pairs={{0,2},{2,0},{4,6},{6,4},{1,3},{3,1},{5,7},{7,5},{8,10},{10,8},{12,... | collective-permute-start | bytes 1572872 | tf_op jit(solution)/shard_map/ppermute | solution.py:63
  17.0 46.8 %all-to-all-start = ((bf16[8,64,768]{2,1,0:T(8,128)(2,1)}), bf16[8,64,768]{2,1,0:T(8,128)(2,1)S(1)}, u32[]{:S(2)}, u32[]{:S(2)}) async-start(bf16[8,64,768]{2,1,0:T(8,128)(2,1)} %pad_maximum_fusion.4), calls=%async_computation | async-start | bytes 1572864 | tf_op jit(solution)/shard_map/all_to_all | solution.py:404
  29.7 31.5 %collective-permute-start.4 = (bf16[128,2048]{1,0:T(8,128)(2,1)S(1)}, bf16[128,2048]{1,0:T(8,128)(2,1)S(1)}, u32[]{:S(2)}, u32[]{:S(2)}) collective-permute-start(bf16[128,2048]{1,0:T(8,128)(2,1)S(1)} %collective-permute-done.3), channel_id=1, source_target_pairs={{0,1},{1,0},{2,3},{3,2},{4,5},{5,4},{6,7},{7,6},{8,9},{9,8},{10,11... | collective-permute-start | bytes 1572872 | tf_op jit(solution)/shard_map/ppermute | solution.py:69
  53.7 32.1 %collective-permute-start.6 = (bf16[128,2048]{1,0:T(8,128)(2,1)}, bf16[128,2048]{1,0:T(8,128)(2,1)}, u32[]{:S(2)}, u32[]{:S(2)}) collective-permute-start(bf16[128,2048]{1,0:T(8,128)(2,1)} %collective-permute-done.5), channel_id=1, source_target_pairs={{0,1},{1,0},{2,3},{3,2},{4,5},{5,4},{6,7},{7,6},{8,9},{9,8},{10,11... | collective-permute-start | bytes 1572872 | tf_op jit(solution)/shard_map/ppermute | solution.py:69
  63.8 53.7 %collective-permute-start.7 = (bf16[512,768]{1,0:T(8,128)(2,1)S(1)}, bf16[512,768]{1,0:T(8,128)(2,1)S(1)}, u32[]{:S(2)}, u32[]{:S(2)}) collective-permute-start(bf16[512,768]{1,0:T(8,128)(2,1)S(1)} %bitcast.194), channel_id=1, source_target_pairs={{0,16},{16,0},{1,17},{17,1},{2,18},{18,2},{3,19},{19,3},{4,20},{20... | collective-permute-start | bytes 2359304 | tf_op jit(solution)/shard_map/ppermute | solution.py:133
  65.4 76.7 %collective-permute-start.9 = (bf16[512,768]{1,0:T(8,128)(2,1)S(1)}, bf16[512,768]{1,0:T(8,128)(2,1)}, u32[]{:S(2)}, u32[]{:S(2)}) collective-permute-start(bf16[512,768]{1,0:T(8,128)(2,1)S(1)} %bitcast.195), channel_id=1, source_target_pairs={{0,8},{8,0},{1,9},{9,1},{2,10},{10,2},{3,11},{11,3},{4,12},{12,4},... | collective-permute-start | bytes 2359304 | tf_op jit(solution)/shard_map/ppermute | solution.py:134
  75.3 38.0 %collective-permute-start.33 = (bf16[128,2048]{1,0:T(8,128)(2,1)S(1)}, bf16[128,2048]{1,0:T(8,128)(2,1)}, u32[]{:S(2)}, u32[]{:S(2)}) collective-permute-start(bf16[128,2048]{1,0:T(8,128)(2,1)S(1)} %bitcast.184), channel_id=1, source_target_pairs={{0,1},{1,0},{2,3},{3,2},{4,5},{5,4},{6,7},{7,6},{8,9},{9,8},{10,11... | collective-permute-start | bytes 1572872 | tf_op jit(solution)/shard_map/ppermute | solution.py:69
  77.0 36.2 %collective-permute-start.34 = (bf16[128,2048]{1,0:T(8,128)(2,1)S(1)}, bf16[128,2048]{1,0:T(8,128)(2,1)}, u32[]{:S(2)}, u32[]{:S(2)}) collective-permute-start(bf16[128,2048]{1,0:T(8,128)(2,1)S(1)} %bitcast.185), channel_id=1, source_target_pairs={{0,2},{2,0},{4,6},{6,4},{1,3},{3,1},{5,7},{7,5},{8,10},{10,8},{12,... | collective-permute-start | bytes 1572872 | tf_op jit(solution)/shard_map/ppermute | solution.py:63
  85.8 26.2 %collective-permute-start.36 = (bf16[128,2048]{1,0:T(8,128)(2,1)S(1)}, bf16[128,2048]{1,0:T(8,128)(2,1)S(1)}, u32[]{:S(2)}, u32[]{:S(2)}) collective-permute-start(bf16[128,2048]{1,0:T(8,128)(2,1)S(1)} %bitcast.186), channel_id=1, source_target_pairs={{0,4},{2,6},{4,0},{6,2},{1,5},{3,7},{5,1},{7,3},{8,12},{10,14},{12... | collective-permute-start | bytes 1572872 | tf_op jit(solution)/shard_map/ppermute | solution.py:62
  112.0 27.6 %collective-permute-start.37 = (bf16[128,2048]{1,0:T(8,128)(2,1)S(1)}, bf16[128,2048]{1,0:T(8,128)(2,1)S(1)}, u32[]{:S(2)}, u32[]{:S(2)}) collective-permute-start(bf16[128,2048]{1,0:T(8,128)(2,1)S(1)} %collective-permute-done.36), channel_id=1, source_target_pairs={{0,1},{1,0},{2,3},{3,2},{4,5},{5,4},{6,7},{7,6},{8,9},{9,8},{10,11... | collective-permute-start | bytes 1572872 | tf_op jit(solution)/shard_map/ppermute | solution.py:69
  126.2 27.8 %collective-permute-start.39 = (bf16[128,2048]{1,0:T(8,128)(2,1)}, bf16[128,2048]{1,0:T(8,128)(2,1)}, u32[]{:S(2)}, u32[]{:S(2)}) collective-permute-start(bf16[128,2048]{1,0:T(8,128)(2,1)} %collective-permute-done.38), channel_id=1, source_target_pairs={{0,1},{1,0},{2,3},{3,2},{4,5},{5,4},{6,7},{7,6},{8,9},{9,8},{10,11... | collective-permute-start | bytes 1572872 | tf_op jit(solution)/shard_map/ppermute | solution.py:69
  182.6 36.7 %collective-permute-start.21 = (bf16[128,2048]{1,0:T(8,128)(2,1)S(1)}, bf16[128,2048]{1,0:T(8,128)(2,1)S(1)}, u32[]{:S(2)}, u32[]{:S(2)}) collective-permute-start(bf16[128,2048]{1,0:T(8,128)(2,1)S(1)} %pad_maximum_fusion.7), channel_id=1, source_target_pairs={{0,1},{1,0},{2,3},{3,2},{4,5},{5,4},{6,7},{7,6},{8,9},{9,8},{10,11... | collective-permute-start | bytes 1572872 | tf_op jit(solution)/shard_map/ppermute | solution.py:99
  183.9 34.2 %collective-permute-start.19 = (bf16[128,2048]{1,0:T(8,128)(2,1)S(1)}, bf16[128,2048]{1,0:T(8,128)(2,1)S(1)}, u32[]{:S(2)}, u32[]{:S(2)}) collective-permute-start(bf16[128,2048]{1,0:T(8,128)(2,1)S(1)} %pad_maximum_fusion.6), channel_id=1, source_target_pairs={{0,1},{1,0},{2,3},{3,2},{4,5},{5,4},{6,7},{7,6},{8,9},{9,8},{10,11... | collective-permute-start | bytes 1572872 | tf_op jit(solution)/shard_map/ppermute | solution.py:99
  197.5 26.2 %collective-permute-start.18 = (bf16[128,2048]{1,0:T(8,128)(2,1)S(1)}, bf16[128,2048]{1,0:T(8,128)(2,1)S(1)}, u32[]{:S(2)}, u32[]{:S(2)}) collective-permute-start(bf16[128,2048]{1,0:T(8,128)(2,1)S(1)} %pad_maximum_fusion.5), channel_id=1, source_target_pairs={{0,1},{1,0},{2,3},{3,2},{4,5},{5,4},{6,7},{7,6},{8,9},{9,8},{10,11... | collective-permute-start | bytes 1572872 | tf_op jit(solution)/shard_map/ppermute | solution.py:99
  247.2 53.7 %collective-permute-start.40 = (bf16[1024,2048]{1,0:T(8,128)(2,1)}, bf16[1024,2048]{1,0:T(8,128)(2,1)}, u32[]{:S(2)}, u32[]{:S(2)}) collective-permute-start(bf16[1024,2048]{1,0:T(8,128)(2,1)} %slice_dynamic-update-slice_fusion.16.refs_8_), channel_id=1, source_target_pairs={{0,8},{8,0},{1,9},{9,1},{2,10},{10,2},{3,11},{11,3},{4,12},{12,4},... | collective-permute-start | bytes 12582920 | tf_op jit(solution)/shard_map/ppermute | solution.py:565
  350.1 79.8 %collective-permute-start.42 = (bf16[512,2048]{1,0:T(8,128)(2,1)}, bf16[512,2048]{1,0:T(8,128)(2,1)}, u32[]{:S(2)}, u32[]{:S(2)}) collective-permute-start(bf16[512,2048]{1,0:T(8,128)(2,1)} %get-tuple-element.59), channel_id=1, source_target_pairs={{0,8},{8,0},{1,9},{9,1},{2,10},{10,2},{3,11},{11,3},{4,12},{12,4},... | collective-permute-start | bytes 6291464 | tf_op jit(solution)/shard_map/ppermute | solution.py:553
  350.3 51.4 %collective-permute-start.44 = (bf16[512,2048]{1,0:T(8,128)(2,1)}, bf16[512,2048]{1,0:T(8,128)(2,1)}, u32[]{:S(2)}, u32[]{:S(2)}) collective-permute-start(bf16[512,2048]{1,0:T(8,128)(2,1)} %get-tuple-element.63), channel_id=1, source_target_pairs={{0,8},{8,0},{1,9},{9,1},{2,10},{10,2},{3,11},{11,3},{4,12},{12,4},... | collective-permute-start | bytes 6291464 | tf_op jit(solution)/shard_map/ppermute | solution.py:553
  389.4 45.4 %collective-permute-start.41 = (bf16[512,2048]{1,0:T(8,128)(2,1)}, bf16[512,2048]{1,0:T(8,128)(2,1)S(1)}, u32[]{:S(2)}, u32[]{:S(2)}) collective-permute-start(bf16[512,2048]{1,0:T(8,128)(2,1)} %get-tuple-element.57), channel_id=1, source_target_pairs={{0,8},{8,0},{1,9},{9,1},{2,10},{10,2},{3,11},{11,3},{4,12},{12,4},... | collective-permute-start | bytes 6291464 | tf_op jit(solution)/shard_map/ppermute | solution.py:553
  400.9 157.2 %collective-permute-start.70 = (bf16[1024,2048]{1,0:T(8,128)(2,1)}, bf16[1024,2048]{1,0:T(8,128)(2,1)}, u32[]{:S(2)}, u32[]{:S(2)}) collective-permute-start(bf16[1024,2048]{1,0:T(8,128)(2,1)} %add_convert_fusion.5), channel_id=1, source_target_pairs={{0,16},{16,0},{1,17},{17,1},{2,18},{18,2},{3,19},{19,3},{4,20},{20... | collective-permute-start | bytes 12582920 | tf_op jit(solution)/shard_map/ppermute | solution.py:604
  405.4 28.9 %collective-permute-start.49 = (bf16[128,2048]{1,0:T(8,128)(2,1)S(1)}, bf16[128,2048]{1,0:T(8,128)(2,1)S(1)}, u32[]{:S(2)}, u32[]{:S(2)}) collective-permute-start(bf16[128,2048]{1,0:T(8,128)(2,1)S(1)} %pad_maximum_fusion.12), channel_id=1, source_target_pairs={{0,1},{1,0},{2,3},{3,2},{4,5},{5,4},{6,7},{7,6},{8,9},{9,8},{10,11... | collective-permute-start | bytes 1572872 | tf_op jit(solution)/shard_map/ppermute | solution.py:99
  407.6 39.2 %collective-permute-start.48 = (bf16[128,2048]{1,0:T(8,128)(2,1)S(1)}, bf16[128,2048]{1,0:T(8,128)(2,1)S(1)}, u32[]{:S(2)}, u32[]{:S(2)}) collective-permute-start(bf16[128,2048]{1,0:T(8,128)(2,1)S(1)} %pad_maximum_fusion.11), channel_id=1, source_target_pairs={{0,1},{1,0},{2,3},{3,2},{4,5},{5,4},{6,7},{7,6},{8,9},{9,8},{10,11... | collective-permute-start | bytes 1572872 | tf_op jit(solution)/shard_map/ppermute | solution.py:99
  480.4 142.6 %collective-permute-start.79 = (bf16[2048,1024]{1,0:T(8,128)(2,1)}, bf16[2048,1024]{1,0:T(8,128)(2,1)}, u32[]{:S(2)}, u32[]{:S(2)}) collective-permute-start(bf16[2048,1024]{1,0:T(8,128)(2,1)} %add_convert_fusion.3), channel_id=1, source_target_pairs={{0,16},{16,0},{1,17},{17,1},{2,18},{18,2},{3,19},{19,3},{4,20},{20... | collective-permute-start | bytes 12582920 | tf_op jit(solution)/shard_map/ppermute | solution.py:604
  538.0 45.7 %collective-permute-start.63 = (bf16[128,2048]{1,0:T(8,128)(2,1)}, bf16[128,2048]{1,0:T(8,128)(2,1)}, u32[]{:S(2)}, u32[]{:S(2)}) collective-permute-start(bf16[128,2048]{1,0:T(8,128)(2,1)} %pad_maximum_fusion.16), channel_id=1, source_target_pairs={{0,1},{1,0},{2,3},{3,2},{4,5},{5,4},{6,7},{7,6},{8,9},{9,8},{10,11... | collective-permute-start | bytes 1572872 | tf_op jit(solution)/shard_map/ppermute | solution.py:99
  540.2 56.8 %collective-permute-start.62 = (bf16[128,2048]{1,0:T(8,128)(2,1)}, bf16[128,2048]{1,0:T(8,128)(2,1)}, u32[]{:S(2)}, u32[]{:S(2)}) collective-permute-start(bf16[128,2048]{1,0:T(8,128)(2,1)} %pad_maximum_fusion.15), channel_id=1, source_target_pairs={{0,1},{1,0},{2,3},{3,2},{4,5},{5,4},{6,7},{7,6},{8,9},{9,8},{10,11... | collective-permute-start | bytes 1572872 | tf_op jit(solution)/shard_map/ppermute | solution.py:99
  566.6 56.4 %collective-permute-start.71 = (bf16[1024,2048]{1,0:T(8,128)(2,1)}, bf16[1024,2048]{1,0:T(8,128)(2,1)}, u32[]{:S(2)}, u32[]{:S(2)}) collective-permute-start(bf16[1024,2048]{1,0:T(8,128)(2,1)} %add_convert_fusion.4.own_ref), channel_id=1, source_target_pairs={{0,8},{8,0},{1,9},{9,1},{2,10},{10,2},{3,11},{11,3},{4,12},{12,4},... | collective-permute-start | bytes 12582920 | tf_op jit(solution)/shard_map/ppermute | solution.py:617
  605.9 97.4 %collective-permute-start.86 = (bf16[2048,1024]{1,0:T(8,128)(2,1)S(1)}, bf16[2048,1024]{1,0:T(8,128)(2,1)S(1)}, u32[]{:S(2)}, u32[]{:S(2)}) collective-permute-start(bf16[2048,1024]{1,0:T(8,128)(2,1)S(1)} %copy-done.19), channel_id=1, source_target_pairs={{0,16},{16,0},{1,17},{17,1},{2,18},{18,2},{3,19},{19,3},{4,20},{20... | collective-permute-start | bytes 12582920 | tf_op jit(solution)/shard_map/ppermute | solution.py:604
  649.5 91.5 %collective-permute-start.82 = (bf16[2048,1024]{1,0:T(8,128)(2,1)}, bf16[2048,1024]{1,0:T(8,128)(2,1)}, u32[]{:S(2)}, u32[]{:S(2)}) collective-permute-start(bf16[2048,1024]{1,0:T(8,128)(2,1)} %add_convert_fusion.2.own_ref), channel_id=1, source_target_pairs={{0,8},{8,0},{1,9},{9,1},{2,10},{10,2},{3,11},{11,3},{4,12},{12,4},... | collective-permute-start | bytes 12582920 | tf_op jit(solution)/shard_map/ppermute | solution.py:617
  649.6 26.5 %collective-permute-start.75 = (bf16[128,2048]{1,0:T(8,128)(2,1)S(1)}, bf16[128,2048]{1,0:T(8,128)(2,1)S(1)}, u32[]{:S(2)}, u32[]{:S(2)}) collective-permute-start(bf16[128,2048]{1,0:T(8,128)(2,1)S(1)} %pad_maximum_fusion.19), channel_id=1, source_target_pairs={{0,1},{1,0},{2,3},{3,2},{4,5},{5,4},{6,7},{7,6},{8,9},{9,8},{10,11... | collective-permute-start | bytes 1572872 | tf_op jit(solution)/shard_map/ppermute | solution.py:99
  707.6 74.5 %collective-permute-start.87 = (bf16[2048,1024]{1,0:T(8,128)(2,1)}, bf16[2048,1024]{1,0:T(8,128)(2,1)}, u32[]{:S(2)}, u32[]{:S(2)}) collective-permute-start(bf16[2048,1024]{1,0:T(8,128)(2,1)} %add_convert_fusion.own_ref), channel_id=1, source_target_pairs={{0,8},{8,0},{1,9},{9,1},{2,10},{10,2},{3,11},{11,3},{4,12},{12,4},... | collective-permute-start | bytes 12582920 | tf_op jit(solution)/shard_map/ppermute | solution.py:617
  721.6 31.9 %all-to-all-start.2 = ((f32[32,1,1280]{2,1,0:T(1,128)}), f32[32,1,1280]{2,1,0:T(1,128)S(1)}, u32[]{:S(2)}, u32[]{:S(2)}) async-start(f32[32,1,1280]{2,1,0:T(1,128)} %copy.109), calls=%async_computation.2 | async-start | bytes 327680 | tf_op jit(solution)/shard_map/all_to_all | solution.py:731
  726.6 30.8 %collective-permute-start.85 = (bf16[64,2048]{1,0:T(8,128)(2,1)}, bf16[64,2048]{1,0:T(8,128)(2,1)S(1)}, u32[]{:S(2)}, u32[]{:S(2)}) collective-permute-start(bf16[64,2048]{1,0:T(8,128)(2,1)} %fusion.32), channel_id=1, source_target_pairs={{0,0},{8,1},{16,8},{24,9},{1,16},{9,17},{17,24},{25,25},{2,2},{10,... | collective-permute-start | bytes 786440 | tf_op jit(solution)/shard_map/ppermute | solution.py:711
  (162 other events, 2232.8 us)

commit v4 on v3

--- a/solution.py
+++ b/solution.py
@@ -73,15 +73,17 @@
     for a in (1, 2, 3):
         along_y(a)
     rows = block.shape[0] // micro_count
-    return jnp.concatenate(
-        [
-            blocks[a, j][m * rows : (m + 1) * rows]
-            for m in range(micro_count)
-            for a in range(4)
-            for j in range(y_count)
-        ],
-        axis=0,
-    )
+    return [
+        jnp.concatenate(
+            [
+                blocks[a, j][m * rows : (m + 1) * rows]
+                for a in range(4)
+                for j in range(y_count)
+            ],
+            axis=0,
+        )
+        for m in range(micro_count)
+    ]
 
 
 def scatter_ep(part, y_count, micro_count):
@@ -226,7 +228,7 @@
 
 
 def run_experts(
-    sets, at, hot, router, select, select_t, micro, moe, cot, w_gate, w_up, w_down, experts, hidden
+    sets, at, hot, router, select, select_t, moe, cot, w_gate, w_up, w_down, experts, hidden
 ):
     count, (slots, seq_len), width = len(sets), select.shape[1:], router.shape[0]
     block = min(hidden, 512)
@@ -243,9 +245,6 @@
     wide = pl.BlockSpec((1, width, block), lambda f, at: (at[0], 0, at[1] + f))
     tall = pl.BlockSpec((1, block, width), lambda f, at: (at[0], at[1] + f, 0))
     hidden_rows = pl.BlockSpec((rows, block), lambda f, at: (0, f))
-    one_micro = pl.BlockSpec(
-        (seq_len, width), lambda f, at: (micro, 0), pipeline_mode=pl.Buffered(1)
-    )
     tables = [array for array in (select, select_t) for _ in sets]
     table_specs = [
         pl.BlockSpec(
@@ -279,7 +278,7 @@
             grid=(steps,),
             in_specs=[whole(hot), whole(router)]
             + table_specs
-            + [one_micro] * (2 * count)
+            + [whole(a) for a in (*moe, *cot)]
             + [wide, wide, tall],
             out_specs=[kept((seq_len, width))] * (2 * count)
             + [kept((rows, width))] * 2
@@ -390,8 +389,11 @@
         local_experts = w_gate.shape[0]
         ff_width = w_gate.shape[2]
 
+        def gather_micros(block):
+            return gather_ep(block.reshape(-1, width), y_count, micro_count)
+
         def gather(block):
-            return gather_ep(block.reshape(-1, width), y_count, micro_count)
+            return jnp.concatenate(gather_micros(block), axis=0)
 
         def scatter(part):
             return scatter_ep(part, y_count, micro_count)
@@ -529,7 +531,7 @@
             [jnp.sum(query_raw * query_raw, axis=1), jnp.sum(key_raw * key_raw, axis=1)]
         )
         squares = sum_ep(squares, y_count, micro_count)
-        cot_all = [gather(after(cotangent, sent_qkv))]
+        cot_own = gather_micros(after(cotangent, sent_qkv))
         scales = lax.rsqrt(squares / width + NORM_EPSILON)
         query_scale, key_scale = scales[0][:, None], scales[1][:, None]
         query = rope(query_raw * query_scale * gain_query).astype(BF16)
@@ -547,6 +549,7 @@
                 here.append(mm(prob.astype(BF16), value[at]).astype(BF16))
             attended.append(jnp.concatenate(here, axis=1))
         attended = jnp.concatenate(attended, axis=0)
+        attended = after(attended, select, select_t, padded_router)
         resid_mid = own + scatter(mm(attended, out_here).astype(BF16))
 
         def with_other_core(parts):
@@ -560,9 +563,9 @@
             )
 
         moe_scale = norm_scale(resid_mid)
-        moe_all = [gather((resid_mid * moe_scale * gain_moe).astype(BF16))]
-        moe_all.append(lax.ppermute(moe_all[0], "core", SWAP))
-        cot_all.append(lax.ppermute(cot_all[0], "core", SWAP))
+        moe_own = gather_micros((resid_mid * moe_scale * gain_moe).astype(BF16))
+        moe_other = [lax.ppermute(rows_here, "core", SWAP) for rows_here in moe_own]
+        cot_other = [lax.ppermute(rows_here, "core", SWAP) for rows_here in cot_own]
         saved, out_parts, grad_parts = [], [], []
         for m in micros:
             sets = [slice(0, 2)] if slots <= 288 else [slice(0, 1), slice(1, 2)]
@@ -575,9 +578,8 @@
                     padded_router,
                     select,
                     select_t,
-                    m,
-                    moe_all[here],
-                    cot_all[here],
+                    [moe_own[m], moe_other[m]][here],
+                    [cot_own[m], cot_other[m]][here],
                     w_gate,
                     w_up,
                     w_down,

time: 803 us -> 775 us (0.965)
  waiting for transfers between devices: 306 us -> 290 us
  starting transfers between devices: 116 us -> 129 us
  local copies, waits for them, and re-layouts: 90.8 us -> 79.9 us
  Pallas kernels: 118 us -> 109 us
    unnamed x271 -> x233, local copies, waits for them, and re-layouts: 58.3 us -> 48.1 us
    pallas_call x2, Pallas kernels: 87.6 us -> 77.8 us  [run_experts(): pl.pallas_call(lambda at, *refs: experts_kernel(count, experts, *refs), g...]
    ppermute x4, waiting for transfers between devices: 32.3 us -> 22.6 us  [gather_ep(): by_z[3] = lax.ppermute(by_z[2], 'z', flip(4, 1))]
    ppermute x4, starting transfers between devices: 8.18 us -> 16.9 us  [gather_ep(): by_z[3] = lax.ppermute(by_z[2], 'z', flip(4, 1))]
  transfers between devices with their start and end apart: 92 -> 94, of which waited for: 41 -> 41; matrix products, arithmetic and copies ran while one was open for 29% -> 29% of each run, Pallas kernels for 7% -> 13%
where the time goes in v4:
time: 775 us; the launch traced here: 768 us
  waiting for transfers between devices  290 us (37%)
  starting transfers between devices  129 us (17%)
  Pallas kernels  109 us (14%)
  matrix products  80.1 us (10%)
  local copies, waits for them, and re-layouts  79.9 us (10%)
  other arithmetic  77.4 us (10%)
    pallas_call x2, Pallas kernels, run_experts(): pl.pallas_call(lambda at, *refs: experts_kernel(count, experts, *refs), g...  77.8 us
    ppermute x16, waiting for transfers between devices, along_y(): arrived = lax.ppermute(piece(a, j).astype(BF16), 'y', flip(y_count, j))  75.4 us
    dot_general x18, matrix products, mm_rows(): lax.dot_general(left, right, (((0,), (0,)), ((), ())), preferred_element_...  49.6 us
    unnamed x233, local copies, waits for them, and re-layouts  48.1 us
    ppermute x4, waiting for transfers between devices, scatter_ep(): near = lax.ppermute(sums[1].astype(BF16), 'z', flip(4, 1)).astype(F32)  46.1 us
    ppermute x4, waiting for transfers between devices, gather_ep(): by_z[2] = lax.ppermute(block, 'z', flip(4, 2))  42.7 us
    ppermute x16, waiting for transfers between devices, along_y(): blocks[a, j] = lax.ppermute(by_z[a], 'y', flip(y_count, j))  37.7 us
    pallas_call x3, Pallas kernels, place_experts(): pl.pallas_call(place_kernel, grid_spec=pltpu.PrefetchScalarGridSpec(num_s...  30.8 us
  transfers between devices with their start and end apart: 94, of which 41 were waited for; matrix products, arithmetic and copies ran while one was open for 29% of the time, Pallas kernels for 13%

profile of v4, /device:TPU:0, one launch (start us, length us, event | category | flops | bytes accessed | tf_op | source)
XLA Modules:
  0.0 768.4 jit_solution(13639171962527287963)
XLA Ops:
  42.9 9.6 %collective-permute-done.5 = bf16[128,2048]{1,0:T(8,128)(2,1)} collective-permute-done((bf16[128,2048]{1,0:T(8,128)(2,1)S(1)}, bf16[128,2048]{1,0:T(8,128)(2,1)}, u32[]{:S(2)}, u32[]{:S(2)}) %collective-permute-start.5) | collective-permute-done | bytes 524320 | tf_op jit(solution)/shard_map/ppermute | solution.py:72
  52.9 8.3 %collective-permute-done.2 = bf16[128,2048]{1,0:T(8,128)(2,1)S(1)} collective-permute-done((bf16[128,2048]{1,0:T(8,128)(2,1)}, bf16[128,2048]{1,0:T(8,128)(2,1)S(1)}, u32[]{:S(2)}, u32[]{:S(2)}) %collective-permute-start.2) | collective-permute-done | bytes 524320 | tf_op jit(solution)/shard_map/ppermute | solution.py:69
  68.7 6.9 all-to-all-start.1
  108.4 10.0 %collective-permute-done.36 = bf16[128,2048]{1,0:T(8,128)(2,1)} collective-permute-done((bf16[128,2048]{1,0:T(8,128)(2,1)S(1)}, bf16[128,2048]{1,0:T(8,128)(2,1)}, u32[]{:S(2)}, u32[]{:S(2)}) %collective-permute-start.36) | collective-permute-done | bytes 524320 | tf_op jit(solution)/shard_map/ppermute | solution.py:62
  124.5 8.2 %fusion.122 = (bf16[1024,768]{0,1:T(8,128)(2,1)}, f32[1024,768]{0,1:T(8,128)S(1)}) fusion(bf16[2048,768]{1,0:T(8,128)(2,1)S(1)} %bitcast.195, bf16[1024,2048]{1,0:T(8,128)(2,1)} %slice_dynamic-update-slice_fusion.46, f32[2048]{0:T(1024)S(1)} %get-tuple-element.193, f32[1024]{0:T(1024)S(1)} %add_rsqrt_fusion.1), kind=kOutput, calls=%fused_computation.381 | convolution fusion | flops 3230400512 | bytes 12070912 | tf_op jit(solution)/shard_map/dot_general | solution.py:36
  136.9 8.1 %collective-permute-done.10 = f32[4,4,2,64]{3,2,1,0:T(2,128)S(1)} collective-permute-done((f32[4,4,2,64]{3,2,1,0:T(2,128)S(1)}, f32[4,4,2,64]{3,2,1,0:T(2,128)S(1)}, u32[]{:S(2)}, u32[]{:S(2)}) %collective-permute-start.10) | collective-permute-done | bytes 8224 | tf_op jit(solution)/shard_map/ppermute | solution.py:120
  171.2 9.6 %collective-permute-done.22 = bf16[128,2048]{1,0:T(8,128)(2,1)S(1)} collective-permute-done((bf16[128,2048]{1,0:T(8,128)(2,1)S(1)}, bf16[128,2048]{1,0:T(8,128)(2,1)S(1)}, u32[]{:S(2)}, u32[]{:S(2)}) %collective-permute-start.22) | collective-permute-done | bytes 524320 | tf_op jit(solution)/shard_map/ppermute | solution.py:101
  182.6 18.0 %collective-permute-done.19 = bf16[128,2048]{1,0:T(8,128)(2,1)S(1)} collective-permute-done((bf16[128,2048]{1,0:T(8,128)(2,1)S(1)}, bf16[128,2048]{1,0:T(8,128)(2,1)S(1)}, u32[]{:S(2)}, u32[]{:S(2)}) %collective-permute-start.19) | collective-permute-done | bytes 524320 | tf_op jit(solution)/shard_map/ppermute | solution.py:101
  210.8 9.7 %collective-permute-done.20 = bf16[128,2048]{1,0:T(8,128)(2,1)S(1)} collective-permute-done((bf16[128,2048]{1,0:T(8,128)(2,1)S(1)}, bf16[128,2048]{1,0:T(8,128)(2,1)S(1)}, u32[]{:S(2)}, u32[]{:S(2)}) %collective-permute-start.20) | collective-permute-done | bytes 524320 | tf_op jit(solution)/shard_map/ppermute | solution.py:110
  230.6 13.3 %collective-permute-done.28 = bf16[128,2048]{1,0:T(8,128)(2,1)S(1)} collective-permute-done((bf16[128,2048]{1,0:T(8,128)(2,1)S(1)}, bf16[128,2048]{1,0:T(8,128)(2,1)S(1)}, u32[]{:S(2)}, u32[]{:S(2)}) %collective-permute-start.28) | collective-permute-done | bytes 524320 | tf_op jit(solution)/shard_map/ppermute | solution.py:62
  244.8 7.1 collective-permute-start.30
  259.5 9.2 %collective-permute-done.27 = bf16[128,2048]{1,0:T(8,128)(2,1)S(1)} collective-permute-done((bf16[128,2048]{1,0:T(8,128)(2,1)S(1)}, bf16[128,2048]{1,0:T(8,128)(2,1)S(1)}, u32[]{:S(2)}, u32[]{:S(2)}) %collective-permute-start.27) | collective-permute-done | bytes 524320 | tf_op jit(solution)/shard_map/ppermute | solution.py:69
  282.2 38.9 %experts.3 = (bf16[512,2048]{1,0:T(8,128)(2,1)}, bf16[512,2048]{1,0:T(8,128)(2,1)}, bf16[512,2048]{1,0:T(8,128)(2,1)}, bf16[512,2048]{1,0:T(8,128)(2,1)}, bf16[5...) custom-call(s32[2]{0:T(128)} %pad_add_fusion.at, ...), custom_call_target="tpu_custom_call" | custom-call | flops 19327352832 | bytes 38797312 | tf_op jit(solution)/shard_map/experts/pallas_call | solution.py:274
  321.6 39.0 %experts.2 = (bf16[512,2048]{1,0:T(8,128)(2,1)}, bf16[512,2048]{1,0:T(8,128)(2,1)}, bf16[512,2048]{1,0:T(8,128)(2,1)}, bf16[512,2048]{1,0:T(8,128)(2,1)}, bf16[5...) custom-call(s32[2]{0:T(128)} %pad_add_fusion.at, ...), custom_call_target="tpu_custom_call" | custom-call | flops 19327352832 | bytes 38797312 | tf_op jit(solution)/shard_map/experts/pallas_call | solution.py:274
  389.6 7.5 add_convert_fusion.3
  426.8 13.9 %collective-permute-done.49 = bf16[128,2048]{1,0:T(8,128)(2,1)S(1)} collective-permute-done((bf16[128,2048]{1,0:T(8,128)(2,1)S(1)}, bf16[128,2048]{1,0:T(8,128)(2,1)S(1)}, u32[]{:S(2)}, u32[]{:S(2)}) %collective-permute-start.49) | collective-permute-done | bytes 524320 | tf_op jit(solution)/shard_map/ppermute | solution.py:110
  451.0 15.1 %collective-permute-done.57 = bf16[128,2048]{1,0:T(8,128)(2,1)S(1)} collective-permute-done((bf16[128,2048]{1,0:T(8,128)(2,1)S(1)}, bf16[128,2048]{1,0:T(8,128)(2,1)S(1)}, u32[]{:S(2)}, u32[]{:S(2)}) %collective-permute-start.57) | collective-permute-done | bytes 524320 | tf_op jit(solution)/shard_map/ppermute | solution.py:62
  472.9 7.8 %collective-permute-done.59 = bf16[128,2048]{1,0:T(8,128)(2,1)S(1)} collective-permute-done((bf16[128,2048]{1,0:T(8,128)(2,1)S(1)}, bf16[128,2048]{1,0:T(8,128)(2,1)S(1)}, u32[]{:S(2)}, u32[]{:S(2)}) %collective-permute-start.59) | collective-permute-done | bytes 524320 | tf_op jit(solution)/shard_map/ppermute | solution.py:72
  481.4 9.4 %collective-permute-done.56 = bf16[128,2048]{1,0:T(8,128)(2,1)S(1)} collective-permute-done((bf16[128,2048]{1,0:T(8,128)(2,1)S(1)}, bf16[128,2048]{1,0:T(8,128)(2,1)S(1)}, u32[]{:S(2)}, u32[]{:S(2)}) %collective-permute-start.56) | collective-permute-done | bytes 524320 | tf_op jit(solution)/shard_map/ppermute | solution.py:69
  491.0 6.8 collective-permute-done.60
  529.1 8.5 %add_convert_fusion.4.own_ref = bf16[1024,2048]{1,0:T(8,128)(2,1)} fusion(bf16[1024,2048]{1,0:T(8,128)(2,1)} %collective-permute-done.72, bf16[1024,2048]{1,0:T(8,128)(2,1)} %add_convert_fusion.5), kind=kLoop, calls=%fused_computation.14 | loop fusion | flops 8388608 | bytes 12582912 | tf_op jit(solution)/shard_map/convert_element_type | solution.py:616
  544.6 8.6 %collective-permute-start.71 = (f32[4,4,2,64]{3,2,1,0:T(2,128)S(1)}, f32[4,4,2,64]{3,2,1,0:T(2,128)S(1)}, u32[]{:S(2)}, u32[]{:S(2)}) collective-permute-start(f32[4,4,2,64]{3,2,1,0:T(2,128)S(1)} %get-tuple-element.333), channel_id=1, source_target_pairs={{0,6},{2,4},{4,2},{6,0},{1,7},{3,5},{5,3},{7,1},{8,14},{10,12},{12... | collective-permute-start | bytes 24584 | tf_op jit(solution)/shard_map/ppermute | solution.py:120
  560.7 10.1 %collective-permute-done.62 = bf16[128,2048]{1,0:T(8,128)(2,1)} collective-permute-done((bf16[128,2048]{1,0:T(8,128)(2,1)}, bf16[128,2048]{1,0:T(8,128)(2,1)}, u32[]{:S(2)}, u32[]{:S(2)}) %collective-permute-start.62) | collective-permute-done | bytes 524320 | tf_op jit(solution)/shard_map/ppermute | solution.py:101
  581.6 11.6 %collective-permute-done.63 = bf16[128,2048]{1,0:T(8,128)(2,1)S(1)} collective-permute-done((bf16[128,2048]{1,0:T(8,128)(2,1)S(1)}, bf16[128,2048]{1,0:T(8,128)(2,1)S(1)}, u32[]{:S(2)}, u32[]{:S(2)}) %collective-permute-start.63) | collective-permute-done | bytes 524320 | tf_op jit(solution)/shard_map/ppermute | solution.py:110
  598.0 10.4 %place.3 = f32[2,1024,2048]{2,1,0:T(8,128)} custom-call(s32[1]{0:T(128)} %bitcast.37.core_ref, bf16[1024,2048]{1,0:T(8,128)(2,1)} %add_convert_fusion.4.own_ref, bf16[1024,2048]{1,0:T(8,128)(2,1)} %collective-permute-done.73.other_ref), custom_call_target="tpu_custom_call" | custom-call | bytes 25165824 | tf_op jit(solution)/shard_map/place/pallas_call | solution.py:323
  617.2 7.6 add_convert_fusion.2.own_ref
  627.4 23.2 %collective-permute-done.75 = bf16[128,2048]{1,0:T(8,128)(2,1)S(1)} collective-permute-done((bf16[128,2048]{1,0:T(8,128)(2,1)S(1)}, bf16[128,2048]{1,0:T(8,128)(2,1)S(1)}, u32[]{:S(2)}, u32[]{:S(2)}) %collective-permute-start.75) | collective-permute-done | bytes 524320 | tf_op jit(solution)/shard_map/ppermute | solution.py:101
  664.1 10.8 %collective-permute-done.76 = bf16[128,2048]{1,0:T(8,128)(2,1)S(1)} collective-permute-done((bf16[128,2048]{1,0:T(8,128)(2,1)S(1)}, bf16[128,2048]{1,0:T(8,128)(2,1)S(1)}, u32[]{:S(2)}, u32[]{:S(2)}) %collective-permute-start.76) | collective-permute-done | bytes 524320 | tf_op jit(solution)/shard_map/ppermute | solution.py:110
  704.3 12.5 %collective-permute-done.83 = bf16[512,768]{1,0:T(8,128)(2,1)} collective-permute-done((bf16[512,768]{1,0:T(8,128)(2,1)S(1)}, bf16[512,768]{1,0:T(8,128)(2,1)}, u32[]{:S(2)}, u32[]{:S(2)}) %collective-permute-start.83) | collective-permute-done | bytes 786464 | tf_op jit(solution)/shard_map/ppermute | solution.py:157
  716.8 10.2 %place.4 = f32[2,2048,1024]{2,1,0:T(8,128)} custom-call(s32[1]{0:T(128)} %bitcast.37.core_ref, bf16[2048,1024]{1,0:T(8,128)(2,1)} %add_convert_fusion.2.own_ref, bf16[2048,1024]{1,0:T(8,128)(2,1)} %collective-permute-done.84.other_ref), custom_call_target="tpu_custom_call" | custom-call | bytes 25165824 | tf_op jit(solution)/shard_map/place/pallas_call | solution.py:323
  738.6 14.3 %all-to-all-done.3 = bf16[8,64,768]{2,1,0:T(8,128)(2,1)S(1)} async-done(((bf16[8,64,768]{2,1,0:T(8,128)(2,1)}), bf16[8,64,768]{2,1,0:T(8,128)(2,1)S(1)}, u32[]{:S(2)}, u32[]{:S(2)}) %all-to-all-start.3) | async-done | bytes 786464 | tf_op jit(solution)/shard_map/all_to_all | solution.py:700
  758.0 10.2 %place.5 = f32[2,2048,1024]{2,1,0:T(8,128)} custom-call(s32[1]{0:T(128)} %bitcast.37.core_ref, bf16[2048,1024]{1,0:T(8,128)(2,1)} %add_convert_fusion.own_ref, bf16[2048,1024]{1,0:T(8,128)(2,1)} %collective-permute-done.89.other_ref), custom_call_target="tpu_custom_call" | custom-call | bytes 25165824 | tf_op jit(solution)/shard_map/place/pallas_call | solution.py:323
  (650 shorter events, 370.6 us)
Async XLA Ops:
  0.7 32.9 %collective-permute-start = (bf16[128,2048]{1,0:T(8,128)(2,1)}, bf16[128,2048]{1,0:T(8,128)(2,1)S(1)}, u32[]{:S(2)}, u32[]{:S(2)}) collective-permute-start(bf16[128,2048]{1,0:T(8,128)(2,1)} %bitcast.177), channel_id=1, source_target_pairs={{0,1},{1,0},{2,3},{3,2},{4,5},{5,4},{6,7},{7,6},{8,9},{9,8},{10,11... | collective-permute-start | bytes 1572872 | tf_op jit(solution)/shard_map/ppermute | solution.py:69
  3.7 34.4 %collective-permute-start.1 = (bf16[128,2048]{1,0:T(8,128)(2,1)}, bf16[128,2048]{1,0:T(8,128)(2,1)}, u32[]{:S(2)}, u32[]{:S(2)}) collective-permute-start(bf16[128,2048]{1,0:T(8,128)(2,1)} %bitcast.178), channel_id=1, source_target_pairs={{0,2},{2,0},{4,6},{6,4},{1,3},{3,1},{5,7},{7,5},{8,10},{10,8},{12,... | collective-permute-start | bytes 1572872 | tf_op jit(solution)/shard_map/ppermute | solution.py:63
  12.5 52.7 %all-to-all-start = ((bf16[8,64,768]{2,1,0:T(8,128)(2,1)}), bf16[8,64,768]{2,1,0:T(8,128)(2,1)S(1)}, u32[]{:S(2)}, u32[]{:S(2)}) async-start(bf16[8,64,768]{2,1,0:T(8,128)(2,1)} %pad_maximum_fusion.4), calls=%async_computation | async-start | bytes 1572864 | tf_op jit(solution)/shard_map/all_to_all | solution.py:406
  32.7 29.9 %collective-permute-start.4 = (bf16[128,2048]{1,0:T(8,128)(2,1)S(1)}, bf16[128,2048]{1,0:T(8,128)(2,1)S(1)}, u32[]{:S(2)}, u32[]{:S(2)}) collective-permute-start(bf16[128,2048]{1,0:T(8,128)(2,1)S(1)} %collective-permute-done.3), channel_id=1, source_target_pairs={{0,1},{1,0},{2,3},{3,2},{4,5},{5,4},{6,7},{7,6},{8,9},{9,8},{10,11... | collective-permute-start | bytes 1572872 | tf_op jit(solution)/shard_map/ppermute | solution.py:69
  52.5 39.8 %collective-permute-start.6 = (bf16[128,2048]{1,0:T(8,128)(2,1)}, bf16[128,2048]{1,0:T(8,128)(2,1)}, u32[]{:S(2)}, u32[]{:S(2)}) collective-permute-start(bf16[128,2048]{1,0:T(8,128)(2,1)} %collective-permute-done.5), channel_id=1, source_target_pairs={{0,1},{1,0},{2,3},{3,2},{4,5},{5,4},{6,7},{7,6},{8,9},{9,8},{10,11... | collective-permute-start | bytes 1572872 | tf_op jit(solution)/shard_map/ppermute | solution.py:69
  65.2 40.1 %collective-permute-start.7 = (bf16[512,768]{1,0:T(8,128)(2,1)S(1)}, bf16[512,768]{1,0:T(8,128)(2,1)S(1)}, u32[]{:S(2)}, u32[]{:S(2)}) collective-permute-start(bf16[512,768]{1,0:T(8,128)(2,1)S(1)} %bitcast.197), channel_id=1, source_target_pairs={{0,16},{16,0},{1,17},{17,1},{2,18},{18,2},{3,19},{19,3},{4,20},{20... | collective-permute-start | bytes 2359304 | tf_op jit(solution)/shard_map/ppermute | solution.py:135
  66.7 55.7 %collective-permute-start.9 = (bf16[512,768]{1,0:T(8,128)(2,1)S(1)}, bf16[512,768]{1,0:T(8,128)(2,1)}, u32[]{:S(2)}, u32[]{:S(2)}) collective-permute-start(bf16[512,768]{1,0:T(8,128)(2,1)S(1)} %bitcast.198), channel_id=1, source_target_pairs={{0,8},{8,0},{1,9},{9,1},{2,10},{10,2},{3,11},{11,3},{4,12},{12,4},... | collective-permute-start | bytes 2359304 | tf_op jit(solution)/shard_map/ppermute | solution.py:136
  76.5 43.0 %collective-permute-start.33 = (bf16[128,2048]{1,0:T(8,128)(2,1)S(1)}, bf16[128,2048]{1,0:T(8,128)(2,1)}, u32[]{:S(2)}, u32[]{:S(2)}) collective-permute-start(bf16[128,2048]{1,0:T(8,128)(2,1)S(1)} %bitcast.186), channel_id=1, source_target_pairs={{0,1},{1,0},{2,3},{3,2},{4,5},{5,4},{6,7},{7,6},{8,9},{9,8},{10,11... | collective-permute-start | bytes 1572872 | tf_op jit(solution)/shard_map/ppermute | solution.py:69
  78.4 41.2 %collective-permute-start.34 = (bf16[128,2048]{1,0:T(8,128)(2,1)S(1)}, bf16[128,2048]{1,0:T(8,128)(2,1)}, u32[]{:S(2)}, u32[]{:S(2)}) collective-permute-start(bf16[128,2048]{1,0:T(8,128)(2,1)S(1)} %bitcast.187), channel_id=1, source_target_pairs={{0,2},{2,0},{4,6},{6,4},{1,3},{3,1},{5,7},{7,5},{8,10},{10,8},{12,... | collective-permute-start | bytes 1572872 | tf_op jit(solution)/shard_map/ppermute | solution.py:63
  118.4 86.1 %collective-permute-start.37 = (bf16[128,2048]{1,0:T(8,128)(2,1)}, bf16[128,2048]{1,0:T(8,128)(2,1)}, u32[]{:S(2)}, u32[]{:S(2)}) collective-permute-start(bf16[128,2048]{1,0:T(8,128)(2,1)} %collective-permute-done.36), channel_id=1, source_target_pairs={{0,1},{1,0},{2,3},{3,2},{4,5},{5,4},{6,7},{7,6},{8,9},{9,8},{10,11... | collective-permute-start | bytes 1572872 | tf_op jit(solution)/shard_map/ppermute | solution.py:69
  136.0 92.0 %collective-permute-start.39 = (bf16[128,2048]{1,0:T(8,128)(2,1)}, bf16[128,2048]{1,0:T(8,128)(2,1)}, u32[]{:S(2)}, u32[]{:S(2)}) collective-permute-start(bf16[128,2048]{1,0:T(8,128)(2,1)} %collective-permute-done.38), channel_id=1, source_target_pairs={{0,1},{1,0},{2,3},{3,2},{4,5},{5,4},{6,7},{7,6},{8,9},{9,8},{10,11... | collective-permute-start | bytes 1572872 | tf_op jit(solution)/shard_map/ppermute | solution.py:69
  169.0 32.8 %collective-permute-start.21 = (bf16[128,2048]{1,0:T(8,128)(2,1)S(1)}, bf16[128,2048]{1,0:T(8,128)(2,1)S(1)}, u32[]{:S(2)}, u32[]{:S(2)}) collective-permute-start(bf16[128,2048]{1,0:T(8,128)(2,1)S(1)} %pad_maximum_fusion.7), channel_id=1, source_target_pairs={{0,1},{1,0},{2,3},{3,2},{4,5},{5,4},{6,7},{7,6},{8,9},{9,8},{10,11... | collective-permute-start | bytes 1572872 | tf_op jit(solution)/shard_map/ppermute | solution.py:101
  170.0 30.5 %collective-permute-start.19 = (bf16[128,2048]{1,0:T(8,128)(2,1)S(1)}, bf16[128,2048]{1,0:T(8,128)(2,1)S(1)}, u32[]{:S(2)}, u32[]{:S(2)}) collective-permute-start(bf16[128,2048]{1,0:T(8,128)(2,1)S(1)} %pad_maximum_fusion.6), channel_id=1, source_target_pairs={{0,1},{1,0},{2,3},{3,2},{4,5},{5,4},{6,7},{7,6},{8,9},{9,8},{10,11... | collective-permute-start | bytes 1572872 | tf_op jit(solution)/shard_map/ppermute | solution.py:101
  224.7 27.6 %collective-permute-start.25 = (bf16[128,2048]{1,0:T(8,128)(2,1)S(1)}, bf16[128,2048]{1,0:T(8,128)(2,1)S(1)}, u32[]{:S(2)}, u32[]{:S(2)}) collective-permute-start(bf16[128,2048]{1,0:T(8,128)(2,1)S(1)} %multiply_convert_fusion.4), channel_id=1, source_target_pairs={{0,1},{1,0},{2,3},{3,2},{4,5},{5,4},{6,7},{7,6},{8,9},{9,8},{10,11... | collective-permute-start | bytes 1572872 | tf_op jit(solution)/shard_map/ppermute | solution.py:69
  229.8 50.0 %collective-permute-start.43 = (bf16[512,2048]{1,0:T(8,128)(2,1)}, bf16[512,2048]{1,0:T(8,128)(2,1)}, u32[]{:S(2)}, u32[]{:S(2)}) collective-permute-start(bf16[512,2048]{1,0:T(8,128)(2,1)} %get-tuple-element.301.refs_8_), channel_id=1, source_target_pairs={{0,8},{8,0},{1,9},{9,1},{2,10},{10,2},{3,11},{11,3},{4,12},{12,4},... | collective-permute-start | bytes 6291464 | tf_op jit(solution)/shard_map/ppermute | solution.py:568
  278.2 43.4 %collective-permute-start.40 = (bf16[512,2048]{1,0:T(8,128)(2,1)}, bf16[512,2048]{1,0:T(8,128)(2,1)}, u32[]{:S(2)}, u32[]{:S(2)}) collective-permute-start(bf16[512,2048]{1,0:T(8,128)(2,1)} %get-tuple-element.300.refs_8_), channel_id=1, source_target_pairs={{0,8},{8,0},{1,9},{9,1},{2,10},{10,2},{3,11},{11,3},{4,12},{12,4},... | collective-permute-start | bytes 6291464 | tf_op jit(solution)/shard_map/ppermute | solution.py:568
  278.7 42.9 %collective-permute-start.32 = (bf16[512,2048]{1,0:T(8,128)(2,1)}, bf16[512,2048]{1,0:T(8,128)(2,1)}, u32[]{:S(2)}, u32[]{:S(2)}) collective-permute-start(bf16[512,2048]{1,0:T(8,128)(2,1)} %copy-done.68), channel_id=1, source_target_pairs={{0,8},{8,0},{1,9},{9,1},{2,10},{10,2},{3,11},{11,3},{4,12},{12,4},... | collective-permute-start | bytes 6291464 | tf_op jit(solution)/shard_map/ppermute | solution.py:567
  321.1 81.3 %collective-permute-start.44 = (bf16[512,2048]{1,0:T(8,128)(2,1)}, bf16[512,2048]{1,0:T(8,128)(2,1)}, u32[]{:S(2)}, u32[]{:S(2)}) collective-permute-start(bf16[512,2048]{1,0:T(8,128)(2,1)} %get-tuple-element.61), channel_id=1, source_target_pairs={{0,8},{8,0},{1,9},{9,1},{2,10},{10,2},{3,11},{11,3},{4,12},{12,4},... | collective-permute-start | bytes 6291464 | tf_op jit(solution)/shard_map/ppermute | solution.py:556
  321.3 51.8 %collective-permute-start.46 = (bf16[512,2048]{1,0:T(8,128)(2,1)}, bf16[512,2048]{1,0:T(8,128)(2,1)}, u32[]{:S(2)}, u32[]{:S(2)}) collective-permute-start(bf16[512,2048]{1,0:T(8,128)(2,1)} %get-tuple-element.65), channel_id=1, source_target_pairs={{0,8},{8,0},{1,9},{9,1},{2,10},{10,2},{3,11},{11,3},{4,12},{12,4},... | collective-permute-start | bytes 6291464 | tf_op jit(solution)/shard_map/ppermute | solution.py:556
  360.6 46.6 %collective-permute-start.41 = (bf16[512,2048]{1,0:T(8,128)(2,1)}, bf16[512,2048]{1,0:T(8,128)(2,1)S(1)}, u32[]{:S(2)}, u32[]{:S(2)}) collective-permute-start(bf16[512,2048]{1,0:T(8,128)(2,1)} %get-tuple-element.59), channel_id=1, source_target_pairs={{0,8},{8,0},{1,9},{9,1},{2,10},{10,2},{3,11},{11,3},{4,12},{12,4},... | collective-permute-start | bytes 6291464 | tf_op jit(solution)/shard_map/ppermute | solution.py:556
  372.2 156.9 %collective-permute-start.72 = (bf16[1024,2048]{1,0:T(8,128)(2,1)}, bf16[1024,2048]{1,0:T(8,128)(2,1)}, u32[]{:S(2)}, u32[]{:S(2)}) collective-permute-start(bf16[1024,2048]{1,0:T(8,128)(2,1)} %add_convert_fusion.5), channel_id=1, source_target_pairs={{0,16},{16,0},{1,17},{17,1},{2,18},{18,2},{3,19},{19,3},{4,20},{20... | collective-permute-start | bytes 12582920 | tf_op jit(solution)/shard_map/ppermute | solution.py:606
  378.1 27.8 %collective-permute-start.51 = (bf16[128,2048]{1,0:T(8,128)(2,1)S(1)}, bf16[128,2048]{1,0:T(8,128)(2,1)S(1)}, u32[]{:S(2)}, u32[]{:S(2)}) collective-permute-start(bf16[128,2048]{1,0:T(8,128)(2,1)S(1)} %pad_maximum_fusion.12), channel_id=1, source_target_pairs={{0,1},{1,0},{2,3},{3,2},{4,5},{5,4},{6,7},{7,6},{8,9},{9,8},{10,11... | collective-permute-start | bytes 1572872 | tf_op jit(solution)/shard_map/ppermute | solution.py:101
  379.1 41.3 %collective-permute-start.50 = (bf16[128,2048]{1,0:T(8,128)(2,1)S(1)}, bf16[128,2048]{1,0:T(8,128)(2,1)S(1)}, u32[]{:S(2)}, u32[]{:S(2)}) collective-permute-start(bf16[128,2048]{1,0:T(8,128)(2,1)S(1)} %pad_maximum_fusion.11), channel_id=1, source_target_pairs={{0,1},{1,0},{2,3},{3,2},{4,5},{5,4},{6,7},{7,6},{8,9},{9,8},{10,11... | collective-permute-start | bytes 1572872 | tf_op jit(solution)/shard_map/ppermute | solution.py:101
  449.8 148.2 %collective-permute-start.81 = (bf16[2048,1024]{1,0:T(8,128)(2,1)}, bf16[2048,1024]{1,0:T(8,128)(2,1)}, u32[]{:S(2)}, u32[]{:S(2)}) collective-permute-start(bf16[2048,1024]{1,0:T(8,128)(2,1)} %add_convert_fusion.3), channel_id=1, source_target_pairs={{0,16},{16,0},{1,17},{17,1},{2,18},{18,2},{3,19},{19,3},{4,20},{20... | collective-permute-start | bytes 12582920 | tf_op jit(solution)/shard_map/ppermute | solution.py:606
  508.1 51.0 %collective-permute-start.65 = (bf16[128,2048]{1,0:T(8,128)(2,1)}, bf16[128,2048]{1,0:T(8,128)(2,1)}, u32[]{:S(2)}, u32[]{:S(2)}) collective-permute-start(bf16[128,2048]{1,0:T(8,128)(2,1)} %pad_maximum_fusion.16), channel_id=1, source_target_pairs={{0,1},{1,0},{2,3},{3,2},{4,5},{5,4},{6,7},{7,6},{8,9},{9,8},{10,11... | collective-permute-start | bytes 1572872 | tf_op jit(solution)/shard_map/ppermute | solution.py:101
  509.7 62.5 %collective-permute-start.64 = (bf16[128,2048]{1,0:T(8,128)(2,1)}, bf16[128,2048]{1,0:T(8,128)(2,1)}, u32[]{:S(2)}, u32[]{:S(2)}) collective-permute-start(bf16[128,2048]{1,0:T(8,128)(2,1)} %pad_maximum_fusion.15), channel_id=1, source_target_pairs={{0,1},{1,0},{2,3},{3,2},{4,5},{5,4},{6,7},{7,6},{8,9},{9,8},{10,11... | collective-permute-start | bytes 1572872 | tf_op jit(solution)/shard_map/ppermute | solution.py:101
  537.6 60.4 %collective-permute-start.73 = (bf16[1024,2048]{1,0:T(8,128)(2,1)}, bf16[1024,2048]{1,0:T(8,128)(2,1)}, u32[]{:S(2)}, u32[]{:S(2)}) collective-permute-start(bf16[1024,2048]{1,0:T(8,128)(2,1)} %add_convert_fusion.4.own_ref), channel_id=1, source_target_pairs={{0,8},{8,0},{1,9},{9,1},{2,10},{10,2},{3,11},{11,3},{4,12},{12,4},... | collective-permute-start | bytes 12582920 | tf_op jit(solution)/shard_map/ppermute | solution.py:619
  581.2 97.0 %collective-permute-start.88 = (bf16[2048,1024]{1,0:T(8,128)(2,1)S(1)}, bf16[2048,1024]{1,0:T(8,128)(2,1)S(1)}, u32[]{:S(2)}, u32[]{:S(2)}) collective-permute-start(bf16[2048,1024]{1,0:T(8,128)(2,1)S(1)} %copy-done.17), channel_id=1, source_target_pairs={{0,16},{16,0},{1,17},{17,1},{2,18},{18,2},{3,19},{19,3},{4,20},{20... | collective-permute-start | bytes 12582920 | tf_op jit(solution)/shard_map/ppermute | solution.py:606
  624.8 92.0 %collective-permute-start.84 = (bf16[2048,1024]{1,0:T(8,128)(2,1)}, bf16[2048,1024]{1,0:T(8,128)(2,1)}, u32[]{:S(2)}, u32[]{:S(2)}) collective-permute-start(bf16[2048,1024]{1,0:T(8,128)(2,1)} %add_convert_fusion.2.own_ref), channel_id=1, source_target_pairs={{0,8},{8,0},{1,9},{9,1},{2,10},{10,2},{3,11},{11,3},{4,12},{12,4},... | collective-permute-start | bytes 12582920 | tf_op jit(solution)/shard_map/ppermute | solution.py:619
  682.5 75.5 %collective-permute-start.89 = (bf16[2048,1024]{1,0:T(8,128)(2,1)}, bf16[2048,1024]{1,0:T(8,128)(2,1)}, u32[]{:S(2)}, u32[]{:S(2)}) collective-permute-start(bf16[2048,1024]{1,0:T(8,128)(2,1)} %add_convert_fusion.own_ref), channel_id=1, source_target_pairs={{0,8},{8,0},{1,9},{9,1},{2,10},{10,2},{3,11},{11,3},{4,12},{12,4},... | collective-permute-start | bytes 12582920 | tf_op jit(solution)/shard_map/ppermute | solution.py:619
  697.0 32.2 %all-to-all-start.2 = ((f32[32,1,1280]{2,1,0:T(1,128)}), f32[32,1,1280]{2,1,0:T(1,128)S(1)}, u32[]{:S(2)}, u32[]{:S(2)}) async-start(f32[32,1,1280]{2,1,0:T(1,128)} %copy.109), calls=%async_computation.2 | async-start | bytes 327680 | tf_op jit(solution)/shard_map/all_to_all | solution.py:733
  702.4 30.8 %collective-permute-start.87 = (bf16[64,2048]{1,0:T(8,128)(2,1)}, bf16[64,2048]{1,0:T(8,128)(2,1)S(1)}, u32[]{:S(2)}, u32[]{:S(2)}) collective-permute-start(bf16[64,2048]{1,0:T(8,128)(2,1)} %fusion.32), channel_id=1, source_target_pairs={{0,0},{8,1},{16,8},{24,9},{1,16},{9,17},{17,24},{25,25},{2,2},{10,... | collective-permute-start | bytes 786440 | tf_op jit(solution)/shard_map/ppermute | solution.py:713
  (153 other events, 1892.9 us)

commit v5 on v4

--- a/solution.py
+++ b/solution.py
@@ -86,7 +86,7 @@
     ]
 
 
-def scatter_ep(part, y_count, micro_count):
+def scatter_ep(part, y_count, micro_count, marks=None):
     rows = part.shape[0] // (4 * y_count * micro_count)
 
     def piece(a, j):
@@ -107,6 +107,8 @@
     sums[2] = sums[2] + lax.ppermute(sums[3].astype(BF16), "z", flip(4, 1)).astype(F32)
     across = lax.ppermute(sums[2].astype(BF16), "z", flip(4, 2)).astype(F32)
     along_y(1)
+    if marks is not None:
+        marks.append(sums[1])
     near = lax.ppermute(sums[1].astype(BF16), "z", flip(4, 1)).astype(F32)
     along_y(0)
     return sums[0] + near + across
@@ -395,8 +397,8 @@
         def gather(block):
             return jnp.concatenate(gather_micros(block), axis=0)
 
-        def scatter(part):
-            return scatter_ep(part, y_count, micro_count)
+        def scatter(part, marks=None):
+            return scatter_ep(part, y_count, micro_count, marks)
 
         def by_owner(weight):
             shaped = weight.reshape(weight_rows, pieces, heads_here, head_sets, head_dim)
@@ -680,7 +682,8 @@
         gate_sum = summed(gate_parts, raw_grad)
         normed_part = mm_cols(after(raw_grad, d_down), qkv)
         attn_gain_grad = jnp.sum(normed_part * rows * row_scale, axis=0)
-        grad_normed = scatter(normed_part.astype(BF16))
+        marks = []
+        grad_normed = scatter(normed_part.astype(BF16), marks)
         in_scale = norm_scale(own)
         inner = grad_normed * gain_attn
         d_tokens = (
@@ -691,7 +694,7 @@
 
         qkv_grad = mm_rows(normed, raw_grad)
         qkv_kept = keep_core(qkv_grad.reshape(grp_size, -1, 3 * local_width), x_count)
-        qkv_grad = keep_x(qkv_kept, x_count, (grad_normed,))
+        qkv_grad = keep_x(qkv_kept, x_count, marks)
         d_gate = both_cores(gate_sum, 1)
         qkv_grad = after(qkv_grad, d_gate, block_out)
         up_sum = summed(up_parts, grad_normed)

time: 775 us -> 776 us (level)
    unnamed x233 -> x231, local copies, waits for them, and re-layouts: 48.1 us -> 48 us
  transfers between devices with their start and end apart: 94 -> 94, of which waited for: 41 -> 41; matrix products, arithmetic and copies ran while one was open for 29% -> 30% of each run, Pallas kernels for 13% -> 13%
where the time goes in v5:
time: 776 us; the launch traced here: 769 us
  waiting for transfers between devices  290 us (37%)
  starting transfers between devices  129 us (17%)
  Pallas kernels  109 us (14%)
  matrix products  80.1 us (10%)
  local copies, waits for them, and re-layouts  79.8 us (10%)
  other arithmetic  78 us (10%)
    pallas_call x2, Pallas kernels, run_experts(): pl.pallas_call(lambda at, *refs: experts_kernel(count, experts, *refs), g...  77.8 us
    ppermute x16, waiting for transfers between devices, along_y(): arrived = lax.ppermute(piece(a, j).astype(BF16), 'y', flip(y_count, j))  75.5 us
    dot_general x18, matrix products, mm_rows(): lax.dot_general(left, right, (((0,), (0,)), ((), ())), preferred_element_...  49.6 us
    unnamed x231, local copies, waits for them, and re-layouts  48 us
    ppermute x4, waiting for transfers between devices, scatter_ep(): near = lax.ppermute(sums[1].astype(BF16), 'z', flip(4, 1)).astype(F32)  46.1 us
    ppermute x4, waiting for transfers between devices, gather_ep(): by_z[2] = lax.ppermute(block, 'z', flip(4, 2))  42.7 us
    ppermute x16, waiting for transfers between devices, along_y(): blocks[a, j] = lax.ppermute(by_z[a], 'y', flip(y_count, j))  37.5 us
    pallas_call x3, Pallas kernels, place_experts(): pl.pallas_call(place_kernel, grid_spec=pltpu.PrefetchScalarGridSpec(num_s...  30.8 us
  transfers between devices with their start and end apart: 94, of which 41 were waited for; matrix products, arithmetic and copies ran while one was open for 30% of the time, Pallas kernels for 13%

profile of v5, /device:TPU:0, one launch (start us, length us, event | category | flops | bytes accessed | tf_op | source)
XLA Modules:
  0.0 769.0 jit_solution(9799999094173703659)
XLA Ops:
  42.9 9.6 %collective-permute-done.5 = bf16[128,2048]{1,0:T(8,128)(2,1)} collective-permute-done((bf16[128,2048]{1,0:T(8,128)(2,1)S(1)}, bf16[128,2048]{1,0:T(8,128)(2,1)}, u32[]{:S(2)}, u32[]{:S(2)}) %collective-permute-start.5) | collective-permute-done | bytes 524320 | tf_op jit(solution)/shard_map/ppermute | solution.py:72
  52.9 8.3 %collective-permute-done.2 = bf16[128,2048]{1,0:T(8,128)(2,1)S(1)} collective-permute-done((bf16[128,2048]{1,0:T(8,128)(2,1)}, bf16[128,2048]{1,0:T(8,128)(2,1)S(1)}, u32[]{:S(2)}, u32[]{:S(2)}) %collective-permute-start.2) | collective-permute-done | bytes 524320 | tf_op jit(solution)/shard_map/ppermute | solution.py:69
  68.7 6.9 all-to-all-start.1
  108.4 10.0 %collective-permute-done.36 = bf16[128,2048]{1,0:T(8,128)(2,1)} collective-permute-done((bf16[128,2048]{1,0:T(8,128)(2,1)S(1)}, bf16[128,2048]{1,0:T(8,128)(2,1)}, u32[]{:S(2)}, u32[]{:S(2)}) %collective-permute-start.36) | collective-permute-done | bytes 524320 | tf_op jit(solution)/shard_map/ppermute | solution.py:62
  124.5 8.2 %fusion.123 = (bf16[1024,768]{0,1:T(8,128)(2,1)}, f32[1024,768]{0,1:T(8,128)S(1)}) fusion(bf16[2048,768]{1,0:T(8,128)(2,1)S(1)} %bitcast.195, bf16[1024,2048]{1,0:T(8,128)(2,1)} %slice_dynamic-update-slice_fusion.46, f32[2048]{0:T(1024)S(1)} %get-tuple-element.193, f32[1024]{0:T(1024)S(1)} %add_rsqrt_fusion.1), kind=kOutput, calls=%fused_computation.382 | convolution fusion | flops 3230400512 | bytes 12070912 | tf_op jit(solution)/shard_map/dot_general | solution.py:36
  136.9 8.1 %collective-permute-done.10 = f32[4,4,2,64]{3,2,1,0:T(2,128)S(1)} collective-permute-done((f32[4,4,2,64]{3,2,1,0:T(2,128)S(1)}, f32[4,4,2,64]{3,2,1,0:T(2,128)S(1)}, u32[]{:S(2)}, u32[]{:S(2)}) %collective-permute-start.10) | collective-permute-done | bytes 8224 | tf_op jit(solution)/shard_map/ppermute | solution.py:122
  171.2 9.7 %collective-permute-done.22 = bf16[128,2048]{1,0:T(8,128)(2,1)S(1)} collective-permute-done((bf16[128,2048]{1,0:T(8,128)(2,1)S(1)}, bf16[128,2048]{1,0:T(8,128)(2,1)S(1)}, u32[]{:S(2)}, u32[]{:S(2)}) %collective-permute-start.22) | collective-permute-done | bytes 524320 | tf_op jit(solution)/shard_map/ppermute | solution.py:101
  182.5 18.0 %collective-permute-done.19 = bf16[128,2048]{1,0:T(8,128)(2,1)S(1)} collective-permute-done((bf16[128,2048]{1,0:T(8,128)(2,1)S(1)}, bf16[128,2048]{1,0:T(8,128)(2,1)S(1)}, u32[]{:S(2)}, u32[]{:S(2)}) %collective-permute-start.19) | collective-permute-done | bytes 524320 | tf_op jit(solution)/shard_map/ppermute | solution.py:101
  210.7 9.8 %collective-permute-done.20 = bf16[128,2048]{1,0:T(8,128)(2,1)S(1)} collective-permute-done((bf16[128,2048]{1,0:T(8,128)(2,1)S(1)}, bf16[128,2048]{1,0:T(8,128)(2,1)S(1)}, u32[]{:S(2)}, u32[]{:S(2)}) %collective-permute-start.20) | collective-permute-done | bytes 524320 | tf_op jit(solution)/shard_map/ppermute | solution.py:112
  230.6 13.2 %collective-permute-done.28 = bf16[128,2048]{1,0:T(8,128)(2,1)S(1)} collective-permute-done((bf16[128,2048]{1,0:T(8,128)(2,1)S(1)}, bf16[128,2048]{1,0:T(8,128)(2,1)S(1)}, u32[]{:S(2)}, u32[]{:S(2)}) %collective-permute-start.28) | collective-permute-done | bytes 524320 | tf_op jit(solution)/shard_map/ppermute | solution.py:62
  245.0 6.8 collective-permute-start.30
  259.6 8.7 %collective-permute-done.27 = bf16[128,2048]{1,0:T(8,128)(2,1)S(1)} collective-permute-done((bf16[128,2048]{1,0:T(8,128)(2,1)S(1)}, bf16[128,2048]{1,0:T(8,128)(2,1)S(1)}, u32[]{:S(2)}, u32[]{:S(2)}) %collective-permute-start.27) | collective-permute-done | bytes 524320 | tf_op jit(solution)/shard_map/ppermute | solution.py:69
  282.1 38.9 %experts.3 = (bf16[512,2048]{1,0:T(8,128)(2,1)}, bf16[512,2048]{1,0:T(8,128)(2,1)}, bf16[512,2048]{1,0:T(8,128)(2,1)}, bf16[512,2048]{1,0:T(8,128)(2,1)}, bf16[5...) custom-call(s32[2]{0:T(128)} %pad_add_fusion.at, ...), custom_call_target="tpu_custom_call" | custom-call | flops 19327352832 | bytes 38797312 | tf_op jit(solution)/shard_map/experts/pallas_call | solution.py:276
  321.5 39.0 %experts.2 = (bf16[512,2048]{1,0:T(8,128)(2,1)}, bf16[512,2048]{1,0:T(8,128)(2,1)}, bf16[512,2048]{1,0:T(8,128)(2,1)}, bf16[512,2048]{1,0:T(8,128)(2,1)}, bf16[5...) custom-call(s32[2]{0:T(128)} %pad_add_fusion.at, ...), custom_call_target="tpu_custom_call" | custom-call | flops 19327352832 | bytes 38797312 | tf_op jit(solution)/shard_map/experts/pallas_call | solution.py:276
  389.6 7.5 add_convert_fusion.3
  426.8 13.8 %collective-permute-done.49 = bf16[128,2048]{1,0:T(8,128)(2,1)S(1)} collective-permute-done((bf16[128,2048]{1,0:T(8,128)(2,1)S(1)}, bf16[128,2048]{1,0:T(8,128)(2,1)S(1)}, u32[]{:S(2)}, u32[]{:S(2)}) %collective-permute-start.49) | collective-permute-done | bytes 524320 | tf_op jit(solution)/shard_map/ppermute | solution.py:112
  451.0 15.2 %collective-permute-done.57 = bf16[128,2048]{1,0:T(8,128)(2,1)S(1)} collective-permute-done((bf16[128,2048]{1,0:T(8,128)(2,1)S(1)}, bf16[128,2048]{1,0:T(8,128)(2,1)S(1)}, u32[]{:S(2)}, u32[]{:S(2)}) %collective-permute-start.57) | collective-permute-done | bytes 524320 | tf_op jit(solution)/shard_map/ppermute | solution.py:62
  473.0 7.8 %collective-permute-done.59 = bf16[128,2048]{1,0:T(8,128)(2,1)S(1)} collective-permute-done((bf16[128,2048]{1,0:T(8,128)(2,1)S(1)}, bf16[128,2048]{1,0:T(8,128)(2,1)S(1)}, u32[]{:S(2)}, u32[]{:S(2)}) %collective-permute-start.59) | collective-permute-done | bytes 524320 | tf_op jit(solution)/shard_map/ppermute | solution.py:72
  481.5 9.4 %collective-permute-done.56 = bf16[128,2048]{1,0:T(8,128)(2,1)S(1)} collective-permute-done((bf16[128,2048]{1,0:T(8,128)(2,1)S(1)}, bf16[128,2048]{1,0:T(8,128)(2,1)S(1)}, u32[]{:S(2)}, u32[]{:S(2)}) %collective-permute-start.56) | collective-permute-done | bytes 524320 | tf_op jit(solution)/shard_map/ppermute | solution.py:69
  491.0 6.8 collective-permute-done.60
  529.2 8.5 %add_convert_fusion.4.own_ref = bf16[1024,2048]{1,0:T(8,128)(2,1)} fusion(bf16[1024,2048]{1,0:T(8,128)(2,1)} %collective-permute-done.72, bf16[1024,2048]{1,0:T(8,128)(2,1)} %add_convert_fusion.5), kind=kLoop, calls=%fused_computation.14 | loop fusion | flops 8388608 | bytes 12582912 | tf_op jit(solution)/shard_map/convert_element_type | solution.py:618
  544.6 8.6 %collective-permute-start.71 = (f32[4,4,2,64]{3,2,1,0:T(2,128)S(1)}, f32[4,4,2,64]{3,2,1,0:T(2,128)S(1)}, u32[]{:S(2)}, u32[]{:S(2)}) collective-permute-start(f32[4,4,2,64]{3,2,1,0:T(2,128)S(1)} %get-tuple-element.333), channel_id=1, source_target_pairs={{0,6},{2,4},{4,2},{6,0},{1,7},{3,5},{5,3},{7,1},{8,14},{10,12},{12... | collective-permute-start | bytes 24584 | tf_op jit(solution)/shard_map/ppermute | solution.py:122
  560.7 10.1 %collective-permute-done.62 = bf16[128,2048]{1,0:T(8,128)(2,1)} collective-permute-done((bf16[128,2048]{1,0:T(8,128)(2,1)}, bf16[128,2048]{1,0:T(8,128)(2,1)}, u32[]{:S(2)}, u32[]{:S(2)}) %collective-permute-start.62) | collective-permute-done | bytes 524320 | tf_op jit(solution)/shard_map/ppermute | solution.py:101
  581.5 11.8 %collective-permute-done.63 = bf16[128,2048]{1,0:T(8,128)(2,1)S(1)} collective-permute-done((bf16[128,2048]{1,0:T(8,128)(2,1)S(1)}, bf16[128,2048]{1,0:T(8,128)(2,1)S(1)}, u32[]{:S(2)}, u32[]{:S(2)}) %collective-permute-start.63) | collective-permute-done | bytes 524320 | tf_op jit(solution)/shard_map/ppermute | solution.py:112
  598.1 10.4 %place.3 = f32[2,1024,2048]{2,1,0:T(8,128)} custom-call(s32[1]{0:T(128)} %bitcast.37.core_ref, bf16[1024,2048]{1,0:T(8,128)(2,1)} %add_convert_fusion.4.own_ref, bf16[1024,2048]{1,0:T(8,128)(2,1)} %collective-permute-done.73.other_ref), custom_call_target="tpu_custom_call" | custom-call | bytes 25165824 | tf_op jit(solution)/shard_map/place/pallas_call | solution.py:325
  617.2 7.6 add_convert_fusion.2.own_ref
  627.4 23.2 %collective-permute-done.75 = bf16[128,2048]{1,0:T(8,128)(2,1)S(1)} collective-permute-done((bf16[128,2048]{1,0:T(8,128)(2,1)S(1)}, bf16[128,2048]{1,0:T(8,128)(2,1)S(1)}, u32[]{:S(2)}, u32[]{:S(2)}) %collective-permute-start.75) | collective-permute-done | bytes 524320 | tf_op jit(solution)/shard_map/ppermute | solution.py:101
  664.1 10.8 %collective-permute-done.76 = bf16[128,2048]{1,0:T(8,128)(2,1)S(1)} collective-permute-done((bf16[128,2048]{1,0:T(8,128)(2,1)S(1)}, bf16[128,2048]{1,0:T(8,128)(2,1)S(1)}, u32[]{:S(2)}, u32[]{:S(2)}) %collective-permute-start.76) | collective-permute-done | bytes 524320 | tf_op jit(solution)/shard_map/ppermute | solution.py:112
  704.1 12.7 %collective-permute-done.83 = bf16[512,768]{1,0:T(8,128)(2,1)} collective-permute-done((bf16[512,768]{1,0:T(8,128)(2,1)S(1)}, bf16[512,768]{1,0:T(8,128)(2,1)}, u32[]{:S(2)}, u32[]{:S(2)}) %collective-permute-start.83) | collective-permute-done | bytes 786464 | tf_op jit(solution)/shard_map/ppermute | solution.py:159
  719.5 10.2 %place.4 = f32[2,2048,1024]{2,1,0:T(8,128)} custom-call(s32[1]{0:T(128)} %bitcast.37.core_ref, bf16[2048,1024]{1,0:T(8,128)(2,1)} %add_convert_fusion.2.own_ref, bf16[2048,1024]{1,0:T(8,128)(2,1)} %collective-permute-done.84.other_ref), custom_call_target="tpu_custom_call" | custom-call | bytes 25165824 | tf_op jit(solution)/shard_map/place/pallas_call | solution.py:325
  739.1 14.3 %all-to-all-done.3 = bf16[8,64,768]{2,1,0:T(8,128)(2,1)S(1)} async-done(((bf16[8,64,768]{2,1,0:T(8,128)(2,1)}), bf16[8,64,768]{2,1,0:T(8,128)(2,1)S(1)}, u32[]{:S(2)}, u32[]{:S(2)}) %all-to-all-start.3) | async-done | bytes 786464 | tf_op jit(solution)/shard_map/all_to_all | solution.py:703
  758.5 10.2 %place.5 = f32[2,2048,1024]{2,1,0:T(8,128)} custom-call(s32[1]{0:T(128)} %bitcast.37.core_ref, bf16[2048,1024]{1,0:T(8,128)(2,1)} %add_convert_fusion.own_ref, bf16[2048,1024]{1,0:T(8,128)(2,1)} %collective-permute-done.89.other_ref), custom_call_target="tpu_custom_call" | custom-call | bytes 25165824 | tf_op jit(solution)/shard_map/place/pallas_call | solution.py:325
  (648 shorter events, 371.6 us)
Async XLA Ops:
  0.7 32.9 %collective-permute-start = (bf16[128,2048]{1,0:T(8,128)(2,1)}, bf16[128,2048]{1,0:T(8,128)(2,1)S(1)}, u32[]{:S(2)}, u32[]{:S(2)}) collective-permute-start(bf16[128,2048]{1,0:T(8,128)(2,1)} %bitcast.177), channel_id=1, source_target_pairs={{0,1},{1,0},{2,3},{3,2},{4,5},{5,4},{6,7},{7,6},{8,9},{9,8},{10,11... | collective-permute-start | bytes 1572872 | tf_op jit(solution)/shard_map/ppermute | solution.py:69
  3.7 34.4 %collective-permute-start.1 = (bf16[128,2048]{1,0:T(8,128)(2,1)}, bf16[128,2048]{1,0:T(8,128)(2,1)}, u32[]{:S(2)}, u32[]{:S(2)}) collective-permute-start(bf16[128,2048]{1,0:T(8,128)(2,1)} %bitcast.178), channel_id=1, source_target_pairs={{0,2},{2,0},{4,6},{6,4},{1,3},{3,1},{5,7},{7,5},{8,10},{10,8},{12,... | collective-permute-start | bytes 1572872 | tf_op jit(solution)/shard_map/ppermute | solution.py:63
  12.5 52.7 %all-to-all-start = ((bf16[8,64,768]{2,1,0:T(8,128)(2,1)}), bf16[8,64,768]{2,1,0:T(8,128)(2,1)S(1)}, u32[]{:S(2)}, u32[]{:S(2)}) async-start(bf16[8,64,768]{2,1,0:T(8,128)(2,1)} %pad_maximum_fusion.4), calls=%async_computation | async-start | bytes 1572864 | tf_op jit(solution)/shard_map/all_to_all | solution.py:408
  32.7 29.9 %collective-permute-start.4 = (bf16[128,2048]{1,0:T(8,128)(2,1)S(1)}, bf16[128,2048]{1,0:T(8,128)(2,1)S(1)}, u32[]{:S(2)}, u32[]{:S(2)}) collective-permute-start(bf16[128,2048]{1,0:T(8,128)(2,1)S(1)} %collective-permute-done.3), channel_id=1, source_target_pairs={{0,1},{1,0},{2,3},{3,2},{4,5},{5,4},{6,7},{7,6},{8,9},{9,8},{10,11... | collective-permute-start | bytes 1572872 | tf_op jit(solution)/shard_map/ppermute | solution.py:69
  52.5 39.8 %collective-permute-start.6 = (bf16[128,2048]{1,0:T(8,128)(2,1)}, bf16[128,2048]{1,0:T(8,128)(2,1)}, u32[]{:S(2)}, u32[]{:S(2)}) collective-permute-start(bf16[128,2048]{1,0:T(8,128)(2,1)} %collective-permute-done.5), channel_id=1, source_target_pairs={{0,1},{1,0},{2,3},{3,2},{4,5},{5,4},{6,7},{7,6},{8,9},{9,8},{10,11... | collective-permute-start | bytes 1572872 | tf_op jit(solution)/shard_map/ppermute | solution.py:69
  65.2 40.0 %collective-permute-start.7 = (bf16[512,768]{1,0:T(8,128)(2,1)S(1)}, bf16[512,768]{1,0:T(8,128)(2,1)S(1)}, u32[]{:S(2)}, u32[]{:S(2)}) collective-permute-start(bf16[512,768]{1,0:T(8,128)(2,1)S(1)} %bitcast.197), channel_id=1, source_target_pairs={{0,16},{16,0},{1,17},{17,1},{2,18},{18,2},{3,19},{19,3},{4,20},{20... | collective-permute-start | bytes 2359304 | tf_op jit(solution)/shard_map/ppermute | solution.py:137
  66.7 55.7 %collective-permute-start.9 = (bf16[512,768]{1,0:T(8,128)(2,1)S(1)}, bf16[512,768]{1,0:T(8,128)(2,1)}, u32[]{:S(2)}, u32[]{:S(2)}) collective-permute-start(bf16[512,768]{1,0:T(8,128)(2,1)S(1)} %bitcast.198), channel_id=1, source_target_pairs={{0,8},{8,0},{1,9},{9,1},{2,10},{10,2},{3,11},{11,3},{4,12},{12,4},... | collective-permute-start | bytes 2359304 | tf_op jit(solution)/shard_map/ppermute | solution.py:138
  76.5 43.0 %collective-permute-start.33 = (bf16[128,2048]{1,0:T(8,128)(2,1)S(1)}, bf16[128,2048]{1,0:T(8,128)(2,1)}, u32[]{:S(2)}, u32[]{:S(2)}) collective-permute-start(bf16[128,2048]{1,0:T(8,128)(2,1)S(1)} %bitcast.186), channel_id=1, source_target_pairs={{0,1},{1,0},{2,3},{3,2},{4,5},{5,4},{6,7},{7,6},{8,9},{9,8},{10,11... | collective-permute-start | bytes 1572872 | tf_op jit(solution)/shard_map/ppermute | solution.py:69
  78.4 41.2 %collective-permute-start.34 = (bf16[128,2048]{1,0:T(8,128)(2,1)S(1)}, bf16[128,2048]{1,0:T(8,128)(2,1)}, u32[]{:S(2)}, u32[]{:S(2)}) collective-permute-start(bf16[128,2048]{1,0:T(8,128)(2,1)S(1)} %bitcast.187), channel_id=1, source_target_pairs={{0,2},{2,0},{4,6},{6,4},{1,3},{3,1},{5,7},{7,5},{8,10},{10,8},{12,... | collective-permute-start | bytes 1572872 | tf_op jit(solution)/shard_map/ppermute | solution.py:63
  118.4 86.1 %collective-permute-start.37 = (bf16[128,2048]{1,0:T(8,128)(2,1)}, bf16[128,2048]{1,0:T(8,128)(2,1)}, u32[]{:S(2)}, u32[]{:S(2)}) collective-permute-start(bf16[128,2048]{1,0:T(8,128)(2,1)} %collective-permute-done.36), channel_id=1, source_target_pairs={{0,1},{1,0},{2,3},{3,2},{4,5},{5,4},{6,7},{7,6},{8,9},{9,8},{10,11... | collective-permute-start | bytes 1572872 | tf_op jit(solution)/shard_map/ppermute | solution.py:69
  136.0 91.9 %collective-permute-start.39 = (bf16[128,2048]{1,0:T(8,128)(2,1)}, bf16[128,2048]{1,0:T(8,128)(2,1)}, u32[]{:S(2)}, u32[]{:S(2)}) collective-permute-start(bf16[128,2048]{1,0:T(8,128)(2,1)} %collective-permute-done.38), channel_id=1, source_target_pairs={{0,1},{1,0},{2,3},{3,2},{4,5},{5,4},{6,7},{7,6},{8,9},{9,8},{10,11... | collective-permute-start | bytes 1572872 | tf_op jit(solution)/shard_map/ppermute | solution.py:69
  169.0 32.8 %collective-permute-start.21 = (bf16[128,2048]{1,0:T(8,128)(2,1)S(1)}, bf16[128,2048]{1,0:T(8,128)(2,1)S(1)}, u32[]{:S(2)}, u32[]{:S(2)}) collective-permute-start(bf16[128,2048]{1,0:T(8,128)(2,1)S(1)} %pad_maximum_fusion.7), channel_id=1, source_target_pairs={{0,1},{1,0},{2,3},{3,2},{4,5},{5,4},{6,7},{7,6},{8,9},{9,8},{10,11... | collective-permute-start | bytes 1572872 | tf_op jit(solution)/shard_map/ppermute | solution.py:101
  170.0 30.5 %collective-permute-start.19 = (bf16[128,2048]{1,0:T(8,128)(2,1)S(1)}, bf16[128,2048]{1,0:T(8,128)(2,1)S(1)}, u32[]{:S(2)}, u32[]{:S(2)}) collective-permute-start(bf16[128,2048]{1,0:T(8,128)(2,1)S(1)} %pad_maximum_fusion.6), channel_id=1, source_target_pairs={{0,1},{1,0},{2,3},{3,2},{4,5},{5,4},{6,7},{7,6},{8,9},{9,8},{10,11... | collective-permute-start | bytes 1572872 | tf_op jit(solution)/shard_map/ppermute | solution.py:101
  224.8 27.6 %collective-permute-start.25 = (bf16[128,2048]{1,0:T(8,128)(2,1)S(1)}, bf16[128,2048]{1,0:T(8,128)(2,1)S(1)}, u32[]{:S(2)}, u32[]{:S(2)}) collective-permute-start(bf16[128,2048]{1,0:T(8,128)(2,1)S(1)} %multiply_convert_fusion.4), channel_id=1, source_target_pairs={{0,1},{1,0},{2,3},{3,2},{4,5},{5,4},{6,7},{7,6},{8,9},{9,8},{10,11... | collective-permute-start | bytes 1572872 | tf_op jit(solution)/shard_map/ppermute | solution.py:69
  229.8 49.9 %collective-permute-start.43 = (bf16[512,2048]{1,0:T(8,128)(2,1)}, bf16[512,2048]{1,0:T(8,128)(2,1)}, u32[]{:S(2)}, u32[]{:S(2)}) collective-permute-start(bf16[512,2048]{1,0:T(8,128)(2,1)} %get-tuple-element.301.refs_8_), channel_id=1, source_target_pairs={{0,8},{8,0},{1,9},{9,1},{2,10},{10,2},{3,11},{11,3},{4,12},{12,4},... | collective-permute-start | bytes 6291464 | tf_op jit(solution)/shard_map/ppermute | solution.py:570
  278.1 43.4 %collective-permute-start.40 = (bf16[512,2048]{1,0:T(8,128)(2,1)}, bf16[512,2048]{1,0:T(8,128)(2,1)}, u32[]{:S(2)}, u32[]{:S(2)}) collective-permute-start(bf16[512,2048]{1,0:T(8,128)(2,1)} %get-tuple-element.300.refs_8_), channel_id=1, source_target_pairs={{0,8},{8,0},{1,9},{9,1},{2,10},{10,2},{3,11},{11,3},{4,12},{12,4},... | collective-permute-start | bytes 6291464 | tf_op jit(solution)/shard_map/ppermute | solution.py:570
  278.6 42.9 %collective-permute-start.32 = (bf16[512,2048]{1,0:T(8,128)(2,1)}, bf16[512,2048]{1,0:T(8,128)(2,1)}, u32[]{:S(2)}, u32[]{:S(2)}) collective-permute-start(bf16[512,2048]{1,0:T(8,128)(2,1)} %copy-done.67), channel_id=1, source_target_pairs={{0,8},{8,0},{1,9},{9,1},{2,10},{10,2},{3,11},{11,3},{4,12},{12,4},... | collective-permute-start | bytes 6291464 | tf_op jit(solution)/shard_map/ppermute | solution.py:569
  320.9 81.4 %collective-permute-start.44 = (bf16[512,2048]{1,0:T(8,128)(2,1)}, bf16[512,2048]{1,0:T(8,128)(2,1)}, u32[]{:S(2)}, u32[]{:S(2)}) collective-permute-start(bf16[512,2048]{1,0:T(8,128)(2,1)} %get-tuple-element.61), channel_id=1, source_target_pairs={{0,8},{8,0},{1,9},{9,1},{2,10},{10,2},{3,11},{11,3},{4,12},{12,4},... | collective-permute-start | bytes 6291464 | tf_op jit(solution)/shard_map/ppermute | solution.py:558
  321.2 51.9 %collective-permute-start.46 = (bf16[512,2048]{1,0:T(8,128)(2,1)}, bf16[512,2048]{1,0:T(8,128)(2,1)}, u32[]{:S(2)}, u32[]{:S(2)}) collective-permute-start(bf16[512,2048]{1,0:T(8,128)(2,1)} %get-tuple-element.65), channel_id=1, source_target_pairs={{0,8},{8,0},{1,9},{9,1},{2,10},{10,2},{3,11},{11,3},{4,12},{12,4},... | collective-permute-start | bytes 6291464 | tf_op jit(solution)/shard_map/ppermute | solution.py:558
  360.5 46.7 %collective-permute-start.41 = (bf16[512,2048]{1,0:T(8,128)(2,1)}, bf16[512,2048]{1,0:T(8,128)(2,1)S(1)}, u32[]{:S(2)}, u32[]{:S(2)}) collective-permute-start(bf16[512,2048]{1,0:T(8,128)(2,1)} %get-tuple-element.59), channel_id=1, source_target_pairs={{0,8},{8,0},{1,9},{9,1},{2,10},{10,2},{3,11},{11,3},{4,12},{12,4},... | collective-permute-start | bytes 6291464 | tf_op jit(solution)/shard_map/ppermute | solution.py:558
  372.1 157.1 %collective-permute-start.72 = (bf16[1024,2048]{1,0:T(8,128)(2,1)}, bf16[1024,2048]{1,0:T(8,128)(2,1)}, u32[]{:S(2)}, u32[]{:S(2)}) collective-permute-start(bf16[1024,2048]{1,0:T(8,128)(2,1)} %add_convert_fusion.5), channel_id=1, source_target_pairs={{0,16},{16,0},{1,17},{17,1},{2,18},{18,2},{3,19},{19,3},{4,20},{20... | collective-permute-start | bytes 12582920 | tf_op jit(solution)/shard_map/ppermute | solution.py:608
  378.1 27.8 %collective-permute-start.51 = (bf16[128,2048]{1,0:T(8,128)(2,1)S(1)}, bf16[128,2048]{1,0:T(8,128)(2,1)S(1)}, u32[]{:S(2)}, u32[]{:S(2)}) collective-permute-start(bf16[128,2048]{1,0:T(8,128)(2,1)S(1)} %pad_maximum_fusion.12), channel_id=1, source_target_pairs={{0,1},{1,0},{2,3},{3,2},{4,5},{5,4},{6,7},{7,6},{8,9},{9,8},{10,11... | collective-permute-start | bytes 1572872 | tf_op jit(solution)/shard_map/ppermute | solution.py:101
  379.1 41.3 %collective-permute-start.50 = (bf16[128,2048]{1,0:T(8,128)(2,1)S(1)}, bf16[128,2048]{1,0:T(8,128)(2,1)S(1)}, u32[]{:S(2)}, u32[]{:S(2)}) collective-permute-start(bf16[128,2048]{1,0:T(8,128)(2,1)S(1)} %pad_maximum_fusion.11), channel_id=1, source_target_pairs={{0,1},{1,0},{2,3},{3,2},{4,5},{5,4},{6,7},{7,6},{8,9},{9,8},{10,11... | collective-permute-start | bytes 1572872 | tf_op jit(solution)/shard_map/ppermute | solution.py:101
  449.8 148.2 %collective-permute-start.81 = (bf16[2048,1024]{1,0:T(8,128)(2,1)}, bf16[2048,1024]{1,0:T(8,128)(2,1)}, u32[]{:S(2)}, u32[]{:S(2)}) collective-permute-start(bf16[2048,1024]{1,0:T(8,128)(2,1)} %add_convert_fusion.3), channel_id=1, source_target_pairs={{0,16},{16,0},{1,17},{17,1},{2,18},{18,2},{3,19},{19,3},{4,20},{20... | collective-permute-start | bytes 12582920 | tf_op jit(solution)/shard_map/ppermute | solution.py:608
  508.1 51.0 %collective-permute-start.65 = (bf16[128,2048]{1,0:T(8,128)(2,1)}, bf16[128,2048]{1,0:T(8,128)(2,1)}, u32[]{:S(2)}, u32[]{:S(2)}) collective-permute-start(bf16[128,2048]{1,0:T(8,128)(2,1)} %pad_maximum_fusion.16), channel_id=1, source_target_pairs={{0,1},{1,0},{2,3},{3,2},{4,5},{5,4},{6,7},{7,6},{8,9},{9,8},{10,11... | collective-permute-start | bytes 1572872 | tf_op jit(solution)/shard_map/ppermute | solution.py:101
  509.8 62.5 %collective-permute-start.64 = (bf16[128,2048]{1,0:T(8,128)(2,1)}, bf16[128,2048]{1,0:T(8,128)(2,1)}, u32[]{:S(2)}, u32[]{:S(2)}) collective-permute-start(bf16[128,2048]{1,0:T(8,128)(2,1)} %pad_maximum_fusion.15), channel_id=1, source_target_pairs={{0,1},{1,0},{2,3},{3,2},{4,5},{5,4},{6,7},{7,6},{8,9},{9,8},{10,11... | collective-permute-start | bytes 1572872 | tf_op jit(solution)/shard_map/ppermute | solution.py:101
  537.7 60.4 %collective-permute-start.73 = (bf16[1024,2048]{1,0:T(8,128)(2,1)}, bf16[1024,2048]{1,0:T(8,128)(2,1)}, u32[]{:S(2)}, u32[]{:S(2)}) collective-permute-start(bf16[1024,2048]{1,0:T(8,128)(2,1)} %add_convert_fusion.4.own_ref), channel_id=1, source_target_pairs={{0,8},{8,0},{1,9},{9,1},{2,10},{10,2},{3,11},{11,3},{4,12},{12,4},... | collective-permute-start | bytes 12582920 | tf_op jit(solution)/shard_map/ppermute | solution.py:621
  581.3 97.0 %collective-permute-start.88 = (bf16[2048,1024]{1,0:T(8,128)(2,1)S(1)}, bf16[2048,1024]{1,0:T(8,128)(2,1)S(1)}, u32[]{:S(2)}, u32[]{:S(2)}) collective-permute-start(bf16[2048,1024]{1,0:T(8,128)(2,1)S(1)} %copy-done.16), channel_id=1, source_target_pairs={{0,16},{16,0},{1,17},{17,1},{2,18},{18,2},{3,19},{19,3},{4,20},{20... | collective-permute-start | bytes 12582920 | tf_op jit(solution)/shard_map/ppermute | solution.py:608
  624.9 94.7 %collective-permute-start.84 = (bf16[2048,1024]{1,0:T(8,128)(2,1)}, bf16[2048,1024]{1,0:T(8,128)(2,1)}, u32[]{:S(2)}, u32[]{:S(2)}) collective-permute-start(bf16[2048,1024]{1,0:T(8,128)(2,1)} %add_convert_fusion.2.own_ref), channel_id=1, source_target_pairs={{0,8},{8,0},{1,9},{9,1},{2,10},{10,2},{3,11},{11,3},{4,12},{12,4},... | collective-permute-start | bytes 12582920 | tf_op jit(solution)/shard_map/ppermute | solution.py:621
  682.5 76.0 %collective-permute-start.89 = (bf16[2048,1024]{1,0:T(8,128)(2,1)}, bf16[2048,1024]{1,0:T(8,128)(2,1)}, u32[]{:S(2)}, u32[]{:S(2)}) collective-permute-start(bf16[2048,1024]{1,0:T(8,128)(2,1)} %add_convert_fusion.own_ref), channel_id=1, source_target_pairs={{0,8},{8,0},{1,9},{9,1},{2,10},{10,2},{3,11},{11,3},{4,12},{12,4},... | collective-permute-start | bytes 12582920 | tf_op jit(solution)/shard_map/ppermute | solution.py:621
  697.0 32.7 %all-to-all-start.2 = ((f32[32,1,1280]{2,1,0:T(1,128)}), f32[32,1,1280]{2,1,0:T(1,128)S(1)}, u32[]{:S(2)}, u32[]{:S(2)}) async-start(f32[32,1,1280]{2,1,0:T(1,128)} %copy.109), calls=%async_computation.2 | async-start | bytes 327680 | tf_op jit(solution)/shard_map/all_to_all | solution.py:736
  702.5 31.3 %collective-permute-start.87 = (bf16[64,2048]{1,0:T(8,128)(2,1)}, bf16[64,2048]{1,0:T(8,128)(2,1)S(1)}, u32[]{:S(2)}, u32[]{:S(2)}) collective-permute-start(bf16[64,2048]{1,0:T(8,128)(2,1)} %fusion.32), channel_id=1, source_target_pairs={{0,0},{8,1},{16,8},{24,9},{1,16},{9,17},{17,24},{25,25},{2,2},{10,... | collective-permute-start | bytes 786440 | tf_op jit(solution)/shard_map/ppermute | solution.py:716
  (152 other events, 1875.5 us)
